TPU v7x, 32 devices: a whole 2x2x4 slice. The times are simulated.
32 devices in a mesh: section: 2 (over x), seq: 4 (over y, core), dp: 4 (over z).
Axes of the slice: x: 2, y: 2, z: 4, core: 2. Of those that a mesh axis runs over, the one named last changes fastest.
Arguments:
- inputs: bfloat16 [16, 512, 768], P('dp', 'seq'), may hold values from -6 to 6
- cotangent: bfloat16 [16, 512, 768], P('dp', 'seq'), may hold values from -6 to 6
- lengths: int32 [16], P('dp'), may hold values from 60 to 512, as said below
- w_qkv: bfloat16 [2, 768, 2304], P('section'), may hold values from -0.21875 to 0.21875
- attn_bias: bfloat16 [2, 1536], P('section'), may hold values from -3 to 3
- w_out: bfloat16 [2, 768, 768], P('section'), may hold values from -0.875 to 0.875
- out_bias: bfloat16 [2, 1536], P('section'), may hold values from -2 to 2
- w_up: bfloat16 [2, 768, 3072], P('section'), may hold values from -0.21875 to 0.21875
- bias_up: bfloat16 [2, 3072], P('section'), may hold values from -3 to 3
- w_down: bfloat16 [2, 3072, 768], P('section'), may hold values from -0.109375 to 0.109375
- norm_gain: bfloat16 [2, 1536], P('section'), may hold values from 0.5 to 1.5
- norm_bias: bfloat16 [2, 1536], P('section'), may hold values from -2 to 2
Outputs:
- section_out: bfloat16 [2, 16, 512, 768], P('section', 'dp', 'seq')
- section_grad: float32 [2, 16, 512, 768], P('section', 'dp', 'seq')
- grad_w_qkv: float32 [2, 768, 2304], P('section', ('seq', 'dp'))
- grad_attn_bias: float32 [2, 1536], P('section', ('seq', 'dp'))
- grad_w_out: float32 [2, 768, 768], P('section', ('seq', 'dp'))
- grad_out_bias: float32 [2, 1536], P('section', ('seq', 'dp'))
- grad_w_up: float32 [2, 768, 3072], P('section', ('seq', 'dp'))
- grad_bias_up: float32 [2, 3072], P('section', ('seq', 'dp'))
- grad_w_down: float32 [2, 3072, 768], P('section', ('seq', 'dp'))
- grad_norm_gain: float32 [2, 1536], P('section', ('seq', 'dp'))
- grad_norm_bias: float32 [2, 1536], P('section', ('seq', 'dp'))
Inputs may be any that keep to these rules, and one draw needn't show every extreme that they name: `lengths`: in each aligned group of 4 tables, one table drawn from the seed has length 512.
All inputs are finite; a program needn't handle non-finite values.
Results may differ from a plain program's by a relative error of at most 0.019.
Values may be sent and summed in bfloat16 or wider, within the bound.
A program may use at most 192 MiB of HBM per device.

v0:
```python
import jax
import jax.numpy as jnp
from jax import lax
from jax.sharding import PartitionSpec as P

H = 12
MICRO = 2


EPS = 1e-12


def from_behind(value, axis, by):
    count = lax.axis_size(axis)
    pairs = [(i, i + by) for i in range(count) if 0 <= i + by < count]
    return lax.ppermute(value, axis, pairs)


def layer_norm(resid, gain, shift):
    average = jnp.mean(resid, axis=-1, keepdims=True)
    centred = resid - average
    spread = jnp.mean(centred * centred, axis=-1, keepdims=True)
    return centred * lax.rsqrt(spread + EPS) * gain + shift


def gelu_exact(argument):
    return jax.nn.gelu(argument, approximate=False)


def product(first_arg, second_arg):
    return jnp.dot(first_arg, second_arg, preferred_element_type=jnp.float32)


def weight_product(first_arg, second_arg):
    return lax.dot_general(
        first_arg, second_arg, (((0,), (0,)), ((), ())), preferred_element_type=jnp.float32
    )


def back_product(first_arg, second_arg):
    return lax.dot_general(
        first_arg, second_arg, (((1,), (1,)), ((), ())), preferred_element_type=jnp.float32
    )


def project_qkv(flat_in, weights):
    width = flat_in.shape[1]
    projected = product(flat_in, weights[0])
    queries = (projected[:, :width] + weights[1][:width]).astype(jnp.bfloat16)
    key_rows = projected[:, width : 2 * width].astype(jnp.bfloat16)
    value_rows = (projected[:, 2 * width :] + weights[1][width:]).astype(jnp.bfloat16)
    return (queries, key_rows, value_rows)


def attention_parts(queries, keys_all, values_all, key_valid, batch):
    width = queries.shape[1]
    head_dim = width // H
    query_heads = queries.reshape(batch, -1, H, head_dim)
    key_heads = keys_all.reshape(batch, -1, H, head_dim)
    value_heads = values_all.reshape(batch, -1, H, head_dim)
    scores = jnp.einsum(
        "bqhe,bkhe->bhqk", query_heads, key_heads, preferred_element_type=jnp.float32
    ) * head_dim ** (-0.5)
    scores = jnp.where(key_valid[:, None, None, :], scores, -1e30)
    row_top = jnp.max(scores, axis=-1, keepdims=True)
    exp_scores = jnp.exp(scores - row_top)
    row_total = jnp.sum(exp_scores, axis=-1, keepdims=True)
    probs = exp_scores / row_total
    probs_low = probs.astype(jnp.bfloat16)
    attended = jnp.einsum(
        "bhqk,bkhe->bqhe", probs_low, value_heads, preferred_element_type=jnp.float32
    )
    return (probs, probs_low, attended.reshape(-1, width).astype(jnp.bfloat16), row_top, row_total)


def forward_local(flat_in, weights, queries, keys_all, values_all, key_valid, batch):
    width = flat_in.shape[1]
    probs, probs_low, attended, row_top, row_total = attention_parts(
        queries, keys_all, values_all, key_valid, batch
    )
    resid_one = flat_in.astype(jnp.float32) + product(attended, weights[2]) + weights[3][:width]
    normed_one = layer_norm(resid_one, weights[7][:width], weights[8][:width])
    normed_low = normed_one.astype(jnp.bfloat16)
    pre_act = product(normed_low, weights[4]) + weights[5]
    hidden_low = gelu_exact(pre_act).astype(jnp.bfloat16)
    resid_two = normed_one + product(hidden_low, weights[6]) + weights[3][width:]
    result = layer_norm(resid_two, weights[7][width:], weights[8][width:])
    return (
        result,
        (
            probs,
            probs_low,
            attended,
            resid_one,
            normed_low,
            pre_act,
            hidden_low,
            resid_two,
            row_top,
            row_total,
        ),
    )


def backward_local(flat_in, weights, queries, keys_all, values_all, saved, grad_out, batch):
    width = flat_in.shape[1]
    head_dim = width // H
    scale = head_dim ** (-0.5)
    (
        probs,
        probs_low,
        attended,
        resid_one,
        normed_low,
        pre_act,
        hidden_low,
        resid_two,
        row_top,
        row_total,
    ) = saved
    gain, shift = (weights[7], weights[8])
    unused_two, norm_two_back = jax.vjp(layer_norm, resid_two, gain[width:], shift[width:])
    grad_r2, grad_g2, grad_c2 = norm_two_back(grad_out)
    grad_branch = grad_r2.astype(jnp.bfloat16)
    grad_bdown = jnp.sum(grad_branch.astype(jnp.float32), axis=0)
    grad_wdown = weight_product(hidden_low, grad_branch)
    grad_hidden = back_product(grad_branch, weights[6])
    unused_act, gelu_back = jax.vjp(gelu_exact, pre_act)
    grad_pre = gelu_back(grad_hidden)[0].astype(jnp.bfloat16)
    grad_bup = jnp.sum(grad_pre.astype(jnp.float32), axis=0)
    grad_wup = weight_product(normed_low, grad_pre)
    grad_n1 = grad_r2 + back_product(grad_pre, weights[4])
    unused_one, norm_one_back = jax.vjp(layer_norm, resid_one, gain[:width], shift[:width])
    grad_r1, grad_g1, grad_c1 = norm_one_back(grad_n1)
    grad_attn = grad_r1.astype(jnp.bfloat16)
    grad_bout = jnp.sum(grad_attn.astype(jnp.float32), axis=0)
    grad_wout = weight_product(attended, grad_attn)
    grad_att_flat = back_product(grad_attn, weights[2]).astype(jnp.bfloat16)
    grad_att = grad_att_flat.reshape(batch, -1, H, head_dim)
    query_heads = queries.reshape(batch, -1, H, head_dim)
    key_heads = keys_all.reshape(batch, -1, H, head_dim)
    value_heads = values_all.reshape(batch, -1, H, head_dim)
    grad_probs = jnp.einsum(
        "bqhe,bkhe->bhqk", grad_att, value_heads, preferred_element_type=jnp.float32
    )
    inner = jnp.sum(probs * grad_probs, axis=-1, keepdims=True)
    grad_scores = (probs * (grad_probs - inner)).astype(jnp.bfloat16)
    grad_query = (
        jnp.einsum("bhqk,bkhe->bqhe", grad_scores, key_heads, preferred_element_type=jnp.float32)
        * scale
    )
    grad_values = jnp.einsum(
        "bhqk,bqhe->bkhe", probs_low, grad_att, preferred_element_type=jnp.float32
    )
    grad_keys = (
        jnp.einsum("bhqk,bqhe->bkhe", grad_scores, query_heads, preferred_element_type=jnp.float32)
        * scale
    )
    key_share, value_share = (
        lax.psum_scatter(
            grad_keys.reshape(batch, -1, width).astype(jnp.bfloat16),
            "seq",
            scatter_dimension=1,
            tiled=True,
        ).astype(jnp.float32),
        lax.psum_scatter(
            grad_values.reshape(batch, -1, width).astype(jnp.bfloat16),
            "seq",
            scatter_dimension=1,
            tiled=True,
        ).astype(jnp.float32),
    )
    query_low = grad_query.reshape(-1, width).astype(jnp.bfloat16)
    key_low = key_share.reshape(-1, width).astype(jnp.bfloat16)
    value_low = value_share.reshape(-1, width).astype(jnp.bfloat16)
    grad_qkv = jnp.concatenate([query_low, key_low, value_low], axis=1)
    grad_abias = jnp.concatenate(
        [
            jnp.sum(query_low.astype(jnp.float32), axis=0),
            jnp.sum(value_low.astype(jnp.float32), axis=0),
        ]
    )
    grad_wqkv = weight_product(flat_in, grad_qkv)
    grad_in = grad_r1 + back_product(grad_qkv, weights[0])
    grads = (
        grad_wqkv,
        grad_abias,
        grad_wout,
        jnp.concatenate([grad_bout, grad_bdown]),
        grad_wup,
        grad_bup,
        grad_wdown,
        jnp.concatenate([grad_g1, grad_g2]),
        jnp.concatenate([grad_c1, grad_c2]),
    )
    return (grad_in, grads)


def local(
    inputs,
    cotangent,
    lengths,
    w_qkv,
    attn_bias,
    w_out,
    out_bias,
    w_up,
    bias_up,
    w_down,
    norm_gain,
    norm_bias,
):
    weights = tuple(
        (
            entry[0]
            for entry in (
                w_qkv,
                attn_bias,
                w_out,
                out_bias,
                w_up,
                bias_up,
                w_down,
                norm_gain,
                norm_bias,
            )
        )
    )
    seq_dev, span, width = inputs.shape
    per_batch = seq_dev // MICRO
    section_index = lax.axis_index("section")
    is_first = section_index == 0
    positions = jnp.arange(span * lax.axis_size("seq"), dtype=jnp.int32)
    local_pos = lax.axis_index("seq") * span + jnp.arange(span, dtype=jnp.int32)
    received = jnp.zeros((per_batch, span, width), jnp.bfloat16)
    kept = jnp.zeros_like(inputs)
    outputs = jnp.zeros_like(inputs)
    for tick in range(MICRO + 1):
        micro_index = tick - section_index
        is_live = (micro_index >= 0) & (micro_index < MICRO)
        slot = jnp.clip(micro_index, 0, MICRO - 1)
        row_start = slot * per_batch
        own_rows = lax.dynamic_slice_in_dim(inputs, row_start, per_batch, 0)
        section_in = jnp.where(is_first, own_rows, received)
        lengths_mb = lax.dynamic_slice_in_dim(lengths, row_start, per_batch, 0)
        key_valid = positions[None, :] < lengths_mb[:, None]
        flat_in = section_in.reshape(-1, width)
        queries, key_rows, value_rows = project_qkv(flat_in, weights)
        keys_all, values_all = (
            lax.all_gather(key_rows.reshape(per_batch, span, width), "seq", axis=1, tiled=True),
            lax.all_gather(value_rows.reshape(per_batch, span, width), "seq", axis=1, tiled=True),
        )
        result, saved = forward_local(
            flat_in, weights, queries, keys_all, values_all, key_valid, per_batch
        )
        result_low = result.astype(jnp.bfloat16).reshape(per_batch, span, width)
        kept = jnp.where(
            is_live, lax.dynamic_update_slice_in_dim(kept, section_in, row_start, 0), kept
        )
        outputs = jnp.where(
            is_live, lax.dynamic_update_slice_in_dim(outputs, result_low, row_start, 0), outputs
        )
        if tick < MICRO:
            received = from_behind(result_low, "section", 1)
    totals = tuple((jnp.zeros(entry.shape, jnp.float32) for entry in weights))
    grad_recv = jnp.zeros((per_batch, span, width), jnp.bfloat16)
    in_grads = jnp.zeros(inputs.shape, jnp.float32)
    for tick in range(MICRO + 1):
        micro_index = MICRO - tick - section_index
        is_live = (micro_index >= 0) & (micro_index < MICRO)
        slot = jnp.clip(micro_index, 0, MICRO - 1)
        row_start = slot * per_batch
        section_in = lax.dynamic_slice_in_dim(kept, row_start, per_batch, 0)
        lengths_mb = lax.dynamic_slice_in_dim(lengths, row_start, per_batch, 0)
        key_valid = positions[None, :] < lengths_mb[:, None]
        row_valid = (local_pos[None, :] < lengths_mb[:, None]).astype(jnp.float32)
        cot_rows = (
            lax.dynamic_slice_in_dim(cotangent, row_start, per_batch, 0).astype(jnp.float32)
            * row_valid[..., None]
        )
        grad_out = jnp.where(is_first, grad_recv.astype(jnp.float32), cot_rows).reshape(-1, width)
        flat_in = section_in.reshape(-1, width)
        queries, key_rows, value_rows = project_qkv(flat_in, weights)
        keys_all, values_all = (
            lax.all_gather(key_rows.reshape(per_batch, span, width), "seq", axis=1, tiled=True),
            lax.all_gather(value_rows.reshape(per_batch, span, width), "seq", axis=1, tiled=True),
        )
        unused_result, saved = forward_local(
            flat_in, weights, queries, keys_all, values_all, key_valid, per_batch
        )
        grad_in, grads = backward_local(
            flat_in, weights, queries, keys_all, values_all, saved, grad_out, per_batch
        )
        grad_in_low = grad_in.astype(jnp.bfloat16)
        stored = jnp.where(is_first, grad_in, grad_in_low.astype(jnp.float32)).reshape(
            per_batch, span, width
        )
        in_grads = jnp.where(
            is_live, lax.dynamic_update_slice_in_dim(in_grads, stored, row_start, 0), in_grads
        )
        masked = tuple((jnp.where(is_live, entry, 0.0) for entry in grads))
        totals = tuple((total + entry for total, entry in zip(totals, masked)))
        if tick < MICRO:
            grad_recv = from_behind(grad_in_low.reshape(per_batch, span, width), "section", -1)
    summed = (
        lax.psum_scatter(totals[0], ("seq", "dp"), scatter_dimension=0, tiled=True),
        lax.psum_scatter(totals[1], ("seq", "dp"), scatter_dimension=0, tiled=True),
        lax.psum_scatter(totals[2], ("seq", "dp"), scatter_dimension=0, tiled=True),
        lax.psum_scatter(totals[3], ("seq", "dp"), scatter_dimension=0, tiled=True),
        lax.psum_scatter(totals[4], ("seq", "dp"), scatter_dimension=0, tiled=True),
        lax.psum_scatter(totals[5], ("seq", "dp"), scatter_dimension=0, tiled=True),
        lax.psum_scatter(totals[6], ("seq", "dp"), scatter_dimension=0, tiled=True),
        lax.psum_scatter(totals[7], ("seq", "dp"), scatter_dimension=0, tiled=True),
        lax.psum_scatter(totals[8], ("seq", "dp"), scatter_dimension=0, tiled=True),
    )
    return (
        outputs[None],
        in_grads[None],
        summed[0][None],
        summed[1][None],
        summed[2][None],
        summed[3][None],
        summed[4][None],
        summed[5][None],
        summed[6][None],
        summed[7][None],
        summed[8][None],
    )


def solution(mesh):
    return jax.shard_map(
        local,
        mesh=mesh,
        in_specs=(
            P("dp", "seq", None),
            P("dp", "seq", None),
            P("dp"),
            P("section", None, None),
            P("section", None),
            P("section", None, None),
            P("section", None),
            P("section", None, None),
            P("section", None),
            P("section", None, None),
            P("section", None),
            P("section", None),
        ),
        out_specs=(
            P("section", "dp", "seq", None),
            P("section", "dp", "seq", None),
            P("section", ("seq", "dp"), None),
            P("section", ("seq", "dp")),
            P("section", ("seq", "dp"), None),
            P("section", ("seq", "dp")),
            P("section", ("seq", "dp"), None),
            P("section", ("seq", "dp")),
            P("section", ("seq", "dp"), None),
            P("section", ("seq", "dp")),
            P("section", ("seq", "dp")),
        ),
        check_vma=False,
    )
```

profile of v0, /device:TPU:0, one launch (start us, length us, event | category | flops | bytes accessed | tf_op | source)
XLA Modules:
  0.0 1033.3 jit_solution(90179812669588209)
XLA Ops:
  27.3 8.9 all-gather.15.cloned.1.call-done
  38.8 6.9 fusion.684
  45.7 12.4 %all-gather.13.cloned.1.call-done = bf16[2,512,768]{2,1,0:T(8,128)(2,1)} async-done(((bf16[2,128,768]{2,1,0:T(8,128)(2,1)}), bf16[2,512,768]{2,1,0:T(8,128)(2,1)}) %all-gather.13.cloned.1.call-update) | async-done | bytes 1572880 | tf_op jit(solution)/shard_map/all_gather | solution.py:251
  58.1 2.7 copy.107
  60.8 4.6 fusion.382
  68.2 14.7 %fusion.690 = (f32[256]{0:T(256)}, f32[256,768]{1,0:T(8,128)}) fusion(f32[768]{0:T(1024)} %get-tuple-element.30, bf16[1,3072,768]{2,1,0:T(8,128)(2,1)} %param.21, bf16[1,768,3072]{2,1,0:T(8,128)(2,1)} %param.19, f32[3072]{0:T(1024)} %bitcast.593, f32[256,768]{1,0:T(8,128)} %copy-done.84, f32[768]{0:T(1024)S(1)} %get-tuple-element.29, ...), kind=kOutput, calls=%fused_computation.798 | convolution fusion | flops 2470182656 | bytes 11034624 | tf_op jit(solution)/shard_map/dot_general | solution.py:31
  87.0 4.5 collective-permute-start
  91.5 7.9 collective-permute-done
  112.4 13.4 %all-gather.19.cloned.1.call-done = bf16[2,512,768]{2,1,0:T(8,128)(2,1)} async-done(((bf16[2,128,768]{2,1,0:T(8,128)(2,1)}), bf16[2,512,768]{2,1,0:T(8,128)(2,1)}) %all-gather.19.cloned.1.call-update) | async-done | bytes 1572880 | tf_op jit(solution)/shard_map/all_gather | solution.py:250
  128.3 6.9 fusion.695
  135.2 12.2 %all-gather.17.cloned.1.call-done = bf16[2,512,768]{2,1,0:T(8,128)(2,1)} async-done(((bf16[2,128,768]{2,1,0:T(8,128)(2,1)}), bf16[2,512,768]{2,1,0:T(8,128)(2,1)}) %all-gather.17.cloned.1.call-update) | async-done | bytes 1572880 | tf_op jit(solution)/shard_map/all_gather | solution.py:251
  150.0 4.6 fusion.383
  157.4 14.7 %fusion.701 = (f32[256]{0:T(256)}, f32[256,768]{1,0:T(8,128)}) fusion(f32[768]{0:T(1024)} %get-tuple-element.30, bf16[1,3072,768]{2,1,0:T(8,128)(2,1)} %param.21, bf16[1,768,3072]{2,1,0:T(8,128)(2,1)} %param.19, f32[3072]{0:T(1024)} %bitcast.594, f32[256,768]{1,0:T(8,128)} %copy-done.85, f32[256]{0:T(256)} %add_rsqrt_fusion.3, f32[256]{0:T(256)} %copy-done.128, ...), kind=kOutput, calls=%fused_computation.801 | convolution fusion | flops 2470182656 | bytes 11034624 | tf_op jit(solution)/shard_map/dot_general | solution.py:31
  176.2 4.3 collective-permute-start.1
  180.5 8.2 collective-permute-done.1
  214.3 2.7 fusion.545
  234.7 6.9 fusion.712
  241.7 2.8 copy.122
  244.5 5.1 fusion.379
  251.2 8.1 multiply_convert_fusion.8
  263.5 2.7 convert_reduce_fusion.2
  276.3 4.9 convolution_convert_fusion.2
  281.2 3.8 multiply_reduce_fusion.2
  292.9 6.8 fusion.706
  299.7 2.7 copy.152
  302.5 6.9 fusion.720
  311.9 4.7 fusion.376
  329.6 5.2 fusion.373
  340.7 11.7 %multiply_convert_fusion.6 = (bf16[256,3072]{1,0:T(8,128)(2,1)S(1)}, f32[256,3072]{1,0:T(8,128)}, f32[256,3072]{1,0:T(8,128)}) fusion(f32[3072]{0:T(1024)} %bitcast.595, bf16[1,768,3072]{2,1,0:T(8,128)(2,1)} %param.19, f32[256,768]{1,0:T(8,128)} %copy-done.24, f32[256]{0:T(256)} %fusion.552, f32[256]{0:T(256)S(1)} %broadcast_multiply_fusion.3, ...), kind=kOutput, calls=%fused_computation.135 | convolution fusion | flops 1260847104 | bytes 13389824 | tf_op jit(solution)/shard_map/dot_general | solution.py:31
  352.3 5.5 fusion.719
  360.8 2.8 copy.119
  363.6 6.8 fusion.727
  373.1 11.7 %multiply_convert_fusion.4 = (bf16[256,3072]{1,0:T(8,128)(2,1)S(1)}, f32[256,3072]{1,0:T(8,128)}, f32[256,3072]{1,0:T(8,128)}) fusion(f32[3072]{0:T(1024)} %bitcast.596, bf16[1,768,3072]{2,1,0:T(8,128)(2,1)} %param.19, f32[256,768]{1,0:T(8,128)} %get-tuple-element.148, f32[256]{0:T(256)} %fusion.554, f32[256]{0:T(256)} %broadcast_multiply_fusion.1, ...), kind=kOutput, calls=%fused_computation.119 | convolution fusion | flops 1260847104 | bytes 13389824 | tf_op jit(solution)/shard_map/dot_general | solution.py:31
  384.8 5.8 fusion.726
  392.8 3.6 reduce-scatter.13.cloned.1.call-done
  398.3 28.8 %reduce-scatter.11.cloned.1.call-done = bf16[2,128,768]{2,1,0:T(8,128)(2,1)} async-done(((bf16[2,512,768]{2,1,0:T(8,128)(2,1)}), bf16[2,128,768]{2,1,0:T(8,128)(2,1)}) %reduce-scatter.11.cloned.1.call-update) | async-done | bytes 393232 | tf_op jit(solution)/shard_map/reduce_scatter | solution.py:160
  429.1 3.6 select_select_fusion
  435.0 10.5 %collective-permute-done.2 = bf16[2,128,768]{2,1,0:T(8,128)(2,1)S(1)} collective-permute-done((bf16[2,128,768]{2,1,0:T(8,128)(2,1)S(1)}, bf16[2,128,768]{2,1,0:T(8,128)(2,1)S(1)}, u32[]{:S(2)}, u32[]{:S(2)}) %collective-permute-start.2) | collective-permute-done | bytes 393248 | tf_op jit(solution)/shard_map/ppermute | solution.py:16
  448.4 5.5 convert_reduce_fusion.1
  463.9 4.8 convolution_convert_fusion.1
  474.9 3.0 fusion.732
  478.4 4.2 multiply_reduce_fusion.1
  492.3 14.7 %fusion.733 = (f32[256]{0:T(256)}, f32[256,768]{1,0:T(8,128)}) fusion(f32[768]{0:T(1024)} %get-tuple-element.30, bf16[1,3072,768]{2,1,0:T(8,128)(2,1)} %param.21, bf16[1,768,3072]{2,1,0:T(8,128)(2,1)} %param.19, f32[3072]{0:T(1024)} %bitcast.597, f32[256,768]{1,0:T(8,128)} %get-tuple-element.155, f32[256]{0:T(256)} %add_rsqrt_fusion.1, ...), kind=kOutput, calls=%fused_computation.813 | convolution fusion | flops 2470182656 | bytes 11034624 | tf_op jit(solution)/shard_map/dot_general | solution.py:31
  506.9 4.6 convert_reduce_fusion.12
  514.6 14.8 %reduce-scatter.15.cloned.1.call-done = bf16[2,128,768]{2,1,0:T(8,128)(2,1)} async-done(((bf16[2,512,768]{2,1,0:T(8,128)(2,1)}), bf16[2,128,768]{2,1,0:T(8,128)(2,1)}) %reduce-scatter.15.cloned.1.call-update) | async-done | bytes 393232 | tf_op jit(solution)/shard_map/reduce_scatter | solution.py:160
  531.4 3.6 convert_select_fusion.1
  537.0 11.0 %collective-permute-done.3 = bf16[2,128,768]{2,1,0:T(8,128)(2,1)S(1)} collective-permute-done((bf16[2,128,768]{2,1,0:T(8,128)(2,1)S(1)}, bf16[2,128,768]{2,1,0:T(8,128)(2,1)S(1)}, u32[]{:S(2)}, u32[]{:S(2)}) %collective-permute-start.3) | collective-permute-done | bytes 393248 | tf_op jit(solution)/shard_map/ppermute | solution.py:16
  551.7 5.5 convert_reduce_fusion
  567.3 4.7 convolution_convert_fusion
  574.6 5.0 multiply_reduce_fusion
  579.6 3.9 multiply_convert_fusion
  594.6 5.5 fusion.436
  600.1 4.1 fusion.435
  609.2 23.5 %reduce-scatter.19.cloned.1.call-done = bf16[2,128,768]{2,1,0:T(8,128)(2,1)} async-done(((bf16[2,512,768]{2,1,0:T(8,128)(2,1)}), bf16[2,128,768]{2,1,0:T(8,128)(2,1)}) %reduce-scatter.19.cloned.1.call-update) | async-done | bytes 393232 | tf_op jit(solution)/shard_map/reduce_scatter | solution.py:160
  634.6 8.1 select_add_fusion.2
  643.3 3.5 fusion.669
  648.5 6.6 select_add_fusion.1
  655.4 3.1 fusion.738
  660.0 4.7 select_add_fusion
  680.2 2.7 copy.331
  691.8 62.9 %all-reduce.5 = (f32[1536]{0:T(1024)}, f32[1536]{0:T(1024)}, f32[3072]{0:T(1024)}, f32[1536]{0:T(1024)}, f32[1536]{0:T(1024)}) all-reduce(f32[1536]{0:T(1024)} %fusion.547, f32[1536]{0:T(1024)} %fusion.549, f32[3072]{0:T(1024)S(1)} %select_add_fusion.4, ...), channel_id=9, replica_groups=mesh['section'=2,'seq'=4,'dp'=4] {'seq','dp'}, use_global_device_ids=true, to_apply=%region_64.65.clone | all-reduce | flops 9216 | bytes 73728
  765.9 28.3 %reduce-scatter.23.cloned.1.call-done = f32[48,2304]{1,0:T(8,128)} async-done(((f32[768,2304]{1,0:T(8,128)}), f32[48,2304]{1,0:T(8,128)}) %reduce-scatter.23.cloned.1.call-update) | async-done | bytes 442384 | tf_op jit(solution)/shard_map/reduce_scatter | solution.py:306
  794.2 115.7 %reduce-scatter.27.cloned.1.call-done = f32[48,3072]{1,0:T(8,128)} async-done(((f32[768,3072]{1,0:T(8,128)}), f32[48,3072]{1,0:T(8,128)}) %reduce-scatter.27.cloned.1.call-update) | async-done | bytes 589840 | tf_op jit(solution)/shard_map/reduce_scatter | solution.py:310
  909.9 116.4 %reduce-scatter.29.cloned.1.call-done = f32[192,768]{1,0:T(8,128)} async-done(((f32[3072,768]{1,0:T(8,128)}), f32[192,768]{1,0:T(8,128)}) %reduce-scatter.29.cloned.1.call-update) | async-done | bytes 589840 | tf_op jit(solution)/shard_map/reduce_scatter | solution.py:312
  (584 shorter events, 264.6 us)
Async XLA Ops:
  7.2 29.0 %all-gather.15.cloned.1.call-start = ((), (), s32[]{:S(2)}) async-start(), calls=%async_computation.11 | async-start | bytes 1966080 | tf_op jit(solution)/shard_map/all_gather | solution.py:250
  13.7 44.3 %all-gather.13.cloned.1.call-start = ((), (), s32[]{:S(2)}) async-start(), calls=%async_computation.10 | async-start | bytes 1966080 | tf_op jit(solution)/shard_map/all_gather | solution.py:251
  17.5 108.3 %all-gather.19.cloned.1.call-start = ((), (), s32[]{:S(2)}) async-start(), calls=%async_computation.13 | async-start | bytes 1966080 | tf_op jit(solution)/shard_map/all_gather | solution.py:250
  87.0 12.4 %collective-permute-start = (bf16[2,128,768]{2,1,0:T(8,128)(2,1)}, bf16[2,128,768]{2,1,0:T(8,128)(2,1)}, u32[]{:S(2)}, u32[]{:S(2)}) collective-permute-start(bf16[2,128,768]{2,1,0:T(8,128)(2,1)} %bitcast.11), channel_id=1, source_target_pairs={{0,16},{1,17},{2,18},{3,19},{4,20},{5,21},{6,22},{7,23},{8,24},{9,... | collective-permute-start | bytes 1179656 | tf_op jit(solution)/shard_map/ppermute | solution.py:16
  104.8 42.6 %all-gather.17.cloned.1.call-start = ((), (), s32[]{:S(2)}) async-start(), calls=%async_computation.12 | async-start | bytes 1966080 | tf_op jit(solution)/shard_map/all_gather | solution.py:251
  107.3 124.9 %all-gather.27.cloned.1.call-start = ((), (), s32[]{:S(2)}) async-start(), calls=%async_computation.17 | async-start | bytes 1966080 | tf_op jit(solution)/shard_map/all_gather | solution.py:285
  176.2 12.4 %collective-permute-start.1 = (bf16[2,128,768]{2,1,0:T(8,128)(2,1)}, bf16[2,128,768]{2,1,0:T(8,128)(2,1)}, u32[]{:S(2)}, u32[]{:S(2)}) collective-permute-start(bf16[2,128,768]{2,1,0:T(8,128)(2,1)} %bitcast.18), channel_id=1, source_target_pairs={{0,16},{1,17},{2,18},{3,19},{4,20},{5,21},{6,22},{7,23},{8,24},{9,... | collective-permute-start | bytes 1179656 | tf_op jit(solution)/shard_map/ppermute | solution.py:16
  196.4 45.3 %all-gather.25.cloned.1.call-start = ((), (), s32[]{:S(2)}) async-start(), calls=%async_computation.16 | async-start | bytes 1966080 | tf_op jit(solution)/shard_map/all_gather | solution.py:286
  204.7 7.6 copy-start.123
  204.7 85.6 %all-gather.31.cloned.1.call-start = ((), (), s32[]{:S(2)}) async-start(), calls=%async_computation.21 | async-start | bytes 1966080 | tf_op jit(solution)/shard_map/all_gather | solution.py:285
  206.9 92.8 %all-gather.35.cloned.1.call-start = ((), (), s32[]{:S(2)}) async-start(), calls=%async_computation.25 | async-start | bytes 1966080 | tf_op jit(solution)/shard_map/all_gather | solution.py:285
  208.9 100.4 %all-gather.29.cloned.1.call-start = ((), (), s32[]{:S(2)}) async-start(), calls=%async_computation.20 | async-start | bytes 1966080 | tf_op jit(solution)/shard_map/all_gather | solution.py:286
  209.7 117.3 %all-gather.33.cloned.1.call-start = ((), (), s32[]{:S(2)}) async-start(), calls=%async_computation.24 | async-start | bytes 1966080 | tf_op jit(solution)/shard_map/all_gather | solution.py:286
  210.2 150.6 %all-gather.23.cloned.1.call-start = ((), (), s32[]{:S(2)}) async-start(), calls=%async_computation.15 | async-start | bytes 1966080 | tf_op jit(solution)/shard_map/all_gather | solution.py:250
  212.2 158.2 %all-gather.21.cloned.1.call-start = ((), (), s32[]{:S(2)}) async-start(), calls=%async_computation.14 | async-start | bytes 1966080 | tf_op jit(solution)/shard_map/all_gather | solution.py:251
  226.4 8.3 copy-start.139
  232.0 164.4 %reduce-scatter.13.cloned.1.call-start = ((), (), s32[]{:S(2)}) async-start(), calls=%async_computation.19 | async-start | bytes 1966080 | tf_op jit(solution)/shard_map/reduce_scatter | solution.py:166
  244.5 14.8 %slice-start.4 = ((s8[4718592]{0:T(1024)(128)(4,1)}), s8[4194304]{0:T(1024)(128)(4,1)S(1)}, s32[]{:S(2)}) async-start(s8[4718592]{0:T(1024)(128)(4,1)} %bitcast.600), calls=%async_computation.36 | async-start | bytes 8388608
  250.0 9.3 copy-start.73
  250.7 17.9 %copy-start.23 = (f32[256,768]{1,0:T(8,128)}, f32[256,768]{1,0:T(8,128)S(1)}, u32[]{:S(2)}) copy-start(f32[256,768]{1,0:T(8,128)S(1)} %get-tuple-element.133) | copy-start | bytes 2359300
  250.7 17.9 %copy-start.94 = (f32[256]{0:T(256)}, f32[256]{0:T(256)S(1)}, u32[]{:S(2)}) copy-start(f32[256]{0:T(256)S(1)} %broadcast_multiply_fusion.5) | copy-start | bytes 3076
  251.2 17.4 %copy-start.106 = (f32[256]{0:T(256)}, f32[256]{0:T(256)S(1)}, u32[]{:S(2)}) copy-start(f32[256]{0:T(256)S(1)} %fusion.550) | copy-start | bytes 3076
  251.2 8.2 copy-start.129
  251.2 8.2 slice-start.5
  276.3 8.7 slice-start.2
  339.2 88.0 %reduce-scatter.11.cloned.1.call-start = ((), (), s32[]{:S(2)}) async-start(), calls=%async_computation.18 | async-start | bytes 1966080 | tf_op jit(solution)/shard_map/reduce_scatter | solution.py:160
  340.6 17.7 %copy-start.115 = (f32[256]{0:T(256)}, f32[256]{0:T(256)S(1)}, u32[]{:S(2)}) copy-start(f32[256]{0:T(256)S(1)} %multiply_reduce_fusion.9) | copy-start | bytes 3076
  340.6 11.7 %copy-start.25 = (f32[256,768]{1,0:T(8,128)S(1)}, f32[256,768]{1,0:T(8,128)}, u32[]{:S(2)}) copy-start(f32[256,768]{1,0:T(8,128)} %copy-done.24) | copy-start | bytes 2359300
  340.6 11.7 %copy-start.107 = (f32[256]{0:T(256)S(1)}, f32[256]{0:T(256)}, u32[]{:S(2)}) copy-start(f32[256]{0:T(256)} %fusion.552) | copy-start | bytes 3076
  340.6 11.7 %copy-start.130 = (f32[768]{0:T(1024)S(1)}, f32[768]{0:T(1024)}, u32[]{:S(2)}) copy-start(f32[768]{0:T(1024)} %get-tuple-element.30) | copy-start | bytes 9220
  358.9 153.8 %reduce-scatter.17.cloned.1.call-start = ((), (), s32[]{:S(2)}) async-start(), calls=%async_computation.23 | async-start | bytes 1966080 | tf_op jit(solution)/shard_map/reduce_scatter | solution.py:166
  373.0 11.7 %copy-start.28 = (f32[256,768]{1,0:T(8,128)S(1)}, f32[256,768]{1,0:T(8,128)}, u32[]{:S(2)}) copy-start(f32[256,768]{1,0:T(8,128)} %get-tuple-element.148) | copy-start | bytes 2359300
  373.0 11.7 %copy-start.96 = (f32[256]{0:T(256)S(1)}, f32[256]{0:T(256)}, u32[]{:S(2)}) copy-start(f32[256]{0:T(256)} %broadcast_multiply_fusion.1) | copy-start | bytes 3076
  373.0 11.7 %copy-start.112 = (f32[256]{0:T(256)S(1)}, f32[256]{0:T(256)}, u32[]{:S(2)}) copy-start(f32[256]{0:T(256)} %fusion.554) | copy-start | bytes 3076
  373.0 11.7 %copy-start.131 = (f32[768]{0:T(1024)S(1)}, f32[768]{0:T(1024)}, u32[]{:S(2)}) copy-start(f32[768]{0:T(1024)} %get-tuple-element.30) | copy-start | bytes 9220
  429.1 16.4 %copy-start.52 = (bf16[4,128,768]{2,1,0:T(8,128)(2,1)S(1)}, bf16[4,128,768]{2,1,0:T(8,128)(2,1)}, u32[]{:S(2)}) copy-start(bf16[4,128,768]{2,1,0:T(8,128)(2,1)} %param.13) | copy-start | bytes 2359300
  429.1 16.4 %copy-start.126 = (f32[2,128]{1,0:T(2,128)S(1)}, f32[2,128]{1,0:T(2,128)}, u32[]{:S(2)}) copy-start(f32[2,128]{1,0:T(2,128)} %get-tuple-element.108) | copy-start | bytes 3076
  429.1 17.2 %copy-start.19 = (f32[256,768]{1,0:T(8,128)S(1)}, f32[256,768]{1,0:T(8,128)}, u32[]{:S(2)}) copy-start(f32[256,768]{1,0:T(8,128)} %get-tuple-element.141) | copy-start | bytes 2359300
  429.1 17.1 %copy-start.101 = (f32[256]{0:T(256)S(1)}, f32[256]{0:T(256)}, u32[]{:S(2)}) copy-start(f32[256]{0:T(256)} %broadcast_multiply_fusion.2) | copy-start | bytes 3076
  432.7 12.7 %collective-permute-start.2 = (bf16[2,128,768]{2,1,0:T(8,128)(2,1)S(1)}, bf16[2,128,768]{2,1,0:T(8,128)(2,1)S(1)}, u32[]{:S(2)}, u32[]{:S(2)}) collective-permute-start(bf16[2,128,768]{2,1,0:T(8,128)(2,1)S(1)} %bitcast.612), channel_id=1, source_target_pairs={{16,0},{17,1},{18,2},{19,3},{20,4},{21,5},{22,6},{23,7},{24,8},{25... | collective-permute-start | bytes 1179656 | tf_op jit(solution)/shard_map/ppermute | solution.py:16
  446.3 7.6 slice-start.8
  471.3 58.2 %reduce-scatter.15.cloned.1.call-start = ((), (), s32[]{:S(2)}) async-start(), calls=%async_computation.22 | async-start | bytes 1966080 | tf_op jit(solution)/shard_map/reduce_scatter | solution.py:160
  471.3 7.1 copy-start.69
  471.3 7.1 copy-start.86
  471.3 7.1 copy-start.103
  472.8 9.8 copy-start.119
  490.1 117.2 %reduce-scatter.21.cloned.1.call-start = ((), (), s32[]{:S(2)}) async-start(), calls=%async_computation.27 | async-start | bytes 1966080 | tf_op jit(solution)/shard_map/reduce_scatter | solution.py:166
  531.4 16.6 %copy-start.53 = (bf16[4,128,768]{2,1,0:T(8,128)(2,1)S(1)}, bf16[4,128,768]{2,1,0:T(8,128)(2,1)}, u32[]{:S(2)}) copy-start(bf16[4,128,768]{2,1,0:T(8,128)(2,1)} %param.13) | copy-start | bytes 2359300
  531.4 16.6 %copy-start.125 = (f32[2,128]{1,0:T(2,128)S(1)}, f32[2,128]{1,0:T(2,128)}, u32[]{:S(2)}) copy-start(f32[2,128]{1,0:T(2,128)} %get-tuple-element.107) | copy-start | bytes 3076
  531.4 17.3 %copy-start.22 = (f32[256,768]{1,0:T(8,128)S(1)}, f32[256,768]{1,0:T(8,128)}, u32[]{:S(2)}) copy-start(f32[256,768]{1,0:T(8,128)} %get-tuple-element.151) | copy-start | bytes 2359300
  531.4 17.3 %copy-start.105 = (f32[256]{0:T(256)S(1)}, f32[256]{0:T(256)}, u32[]{:S(2)}) copy-start(f32[256]{0:T(256)} %broadcast_multiply_fusion) | copy-start | bytes 3076
  531.4 17.3 %copy-start.122 = (f32[256]{0:T(256)S(1)}, f32[256]{0:T(256)}, u32[]{:S(2)}) copy-start(f32[256]{0:T(256)} %fusion.555) | copy-start | bytes 3076
  535.1 14.5 %copy-start.120 = (f32[256]{0:T(256)S(1)}, f32[256]{0:T(256)}, u32[]{:S(2)}) copy-start(f32[256]{0:T(256)} %copy-done.119) | copy-start | bytes 3076
  535.1 14.5 %copy-start.90 = (f32[768]{0:T(1024)S(1)}, f32[768]{0:T(1024)}, u32[]{:S(2)}) copy-start(f32[768]{0:T(1024)} %get-tuple-element.28) | copy-start | bytes 9220
  535.1 12.9 %collective-permute-start.3 = (bf16[2,128,768]{2,1,0:T(8,128)(2,1)S(1)}, bf16[2,128,768]{2,1,0:T(8,128)(2,1)S(1)}, u32[]{:S(2)}, u32[]{:S(2)}) collective-permute-start(bf16[2,128,768]{2,1,0:T(8,128)(2,1)S(1)} %bitcast.611), channel_id=1, source_target_pairs={{16,0},{17,1},{18,2},{19,3},{20,4},{21,5},{22,6},{23,7},{24,8},{25... | collective-permute-start | bytes 1179656 | tf_op jit(solution)/shard_map/ppermute | solution.py:16
  548.7 8.5 slice-start.10
  559.9 12.0 %copy-start.136 = (f32[256]{0:T(256)}, f32[256]{0:T(256)S(1)}, u32[]{:S(2)}) copy-start(f32[256]{0:T(256)S(1)} %negate_multiply_fusion.6) | copy-start | bytes 3076
  574.5 58.2 %reduce-scatter.19.cloned.1.call-start = ((), (), s32[]{:S(2)}) async-start(), calls=%async_computation.26 | async-start | bytes 1966080 | tf_op jit(solution)/shard_map/reduce_scatter | solution.py:160
  589.7 176.3 %reduce-scatter.25.cloned.1.call-start = ((), (), s32[]{:S(2)}) async-start(), calls=%async_computation.29 | async-start | bytes 2506752 | tf_op jit(solution)/shard_map/reduce_scatter | solution.py:308
  594.1 200.1 %reduce-scatter.23.cloned.1.call-start = ((), (), s32[]{:S(2)}) async-start(), calls=%async_computation.28 | async-start | bytes 7520256 | tf_op jit(solution)/shard_map/reduce_scatter | solution.py:306
  642.7 267.2 %reduce-scatter.27.cloned.1.call-start = ((), (), s32[]{:S(2)}) async-start(), calls=%async_computation.30 | async-start | bytes 10027008 | tf_op jit(solution)/shard_map/reduce_scatter | solution.py:310
  655.1 371.1 %reduce-scatter.29.cloned.1.call-start = ((), (), s32[]{:S(2)}) async-start(), calls=%async_computation.31 | async-start | bytes 10027008 | tf_op jit(solution)/shard_map/reduce_scatter | solution.py:312
  664.7 6.6 copy-start.91
  668.4 8.7 copy-start.92
  (123 other events, 419.1 us)
Sparse Core Ops, SparseCore 0:
  13.8 22.3 all-gather.14
  38.4 19.6 all-gather.12
  104.9 20.7 all-gather.18
  127.7 19.6 all-gather.16
  196.5 20.7 all-gather.26
  218.8 19.6 all-gather.24
  240.0 19.6 all-gather.30
  261.3 19.6 all-gather.34
  282.5 19.6 all-gather.28
  303.6 19.6 all-gather.32
  324.9 19.6 all-gather.22
  346.0 19.6 all-gather.20
  368.2 28.1 reduce-scatter.12
  399.0 28.1 reduce-scatter.10
  471.4 27.2 reduce-scatter.16
  501.2 28.1 reduce-scatter.14
  574.6 27.2 reduce-scatter.20
  604.5 28.1 reduce-scatter.18
  637.0 62.9 reduce-scatter.24
  705.0 89.2 reduce-scatter.22
  798.9 110.9 reduce-scatter.26
  915.1 111.0 reduce-scatter.28
where the time goes:
time: 1040 us; the launch traced here: 1030 us
  waiting for transfers between devices  417 us (40%)
  matrix products  288 us (28%)
  local copies, waits for them, and re-layouts  153 us (15%)
  other arithmetic  80.4 us (8%)
  blocking collectives  62.9 us (6%)
  between operations  17.8 us (2%)
  starting transfers between devices  13.7 us (1%)
    reduce_scatter x1, waiting for transfers between devices, local(): lax.psum_scatter(totals[6], ('seq', 'dp'), scatter_dimension=0, tiled=True)  116 us
    reduce_scatter x1, waiting for transfers between devices, local(): lax.psum_scatter(totals[4], ('seq', 'dp'), scatter_dimension=0, tiled=True)  116 us
    dot_general x21, matrix products, product(): return jnp.dot(first_arg, second_arg, preferred_element_type=jnp.float32)  103 us
    reduce_scatter x3, waiting for transfers between devices, backward_local(): lax.psum_scatter(grad_keys.reshape(batch, -1, width).astype(jnp.bfloat16)...  67.2 us
    unnamed x1, blocking collectives  62.9 us
    dot_general x12, matrix products, weight_product(): lax.dot_general(first_arg, second_arg, (((0,), (0,)), ((), ())), preferre...  42.8 us
    sub x6, matrix products, attention_parts(): exp_scores = jnp.exp(scores - row_top)  41.1 us
    ppermute x4, waiting for transfers between devices, from_behind(): return lax.ppermute(value, axis, pairs)  37.6 us
  transfers between devices with their start and end apart: 26, of which 15 were waited for; matrix products, arithmetic and copies ran while one was open for 36% of the time, Pallas kernels for 0%

commit v1 on v0

v1 whole, which is shorter than its diff:
```python
import functools

import jax
import jax.numpy as jnp
from jax import lax
from jax.experimental import pallas as pl
from jax.experimental.pallas import tpu as pltpu
from jax.sharding import PartitionSpec as P

H = 12
MICRO = 2
EPS = 1e-12
MESH = pl.DeviceIdType.MESH
BF = jnp.bfloat16
F32 = jnp.float32
LANES = 128
INV_SQRT_2PI = 0.3989422804014327
INV_SQRT_2 = 0.7071067811865476


def dot_nn(a, b):
    return lax.dot_general(a, b, (((1,), (0,)), ((), ())), preferred_element_type=F32)


def dot_nt(a, b):
    return lax.dot_general(a, b, (((1,), (1,)), ((), ())), preferred_element_type=F32)


def dot_tn(a, b):
    return lax.dot_general(a, b, (((0,), (0,)), ((), ())), preferred_element_type=F32)


def layers_kernel(
    len_ref, in_hbm, cot_hbm, wqkv_hbm, wout_hbm, wup_hbm, wdown_hbm,
    abias_ref, obias_ref, bup_ref, gain_ref, shift_ref,
    sout_hbm, sgrad_hbm, xs, os_, n1s, fs, dps, das, dus, dzs, bg,
    ab, wqkv, wout, wup, wdown, q_s, kv, lse, ot, xh1, xh2, rs1, rs2, gp, dr1, acc, do_s,
    dkv_own, dkv_send, dkv_recv, yb, gb,
    w_sem, loc_sem, ex_send, ex_recv, hop_send, hop_recv, kv_send, kv_rsem, dk_ssem, dk_rsem,
    out_loc, out_send, out_recv,
):
    width = wqkv.shape[0]
    ff = wup.shape[1]
    span = in_hbm.shape[1]
    rows = 2 * span
    keys = 2 * rows
    hd = width // H
    pairs = H // 2
    nff = ff // width
    sec = lax.axis_index("section")
    seq = lax.axis_index("seq")
    dp = lax.axis_index("dp")
    hi = seq // 2
    lo = seq % 2
    core_dev = (sec, hi * 2 + 1 - lo, dp)
    y_dev = (sec, (1 - hi) * 2 + lo, dp)
    x_dev = (1 - sec, seq, dp)

    weight_copies = [
        pltpu.make_async_copy(src.at[0], dst, w_sem.at[i])
        for i, (src, dst) in enumerate(
            ((wqkv_hbm, wqkv), (wout_hbm, wout), (wup_hbm, wup), (wdown_hbm, wdown))
        )
    ]
    for copy in weight_copies:
        copy.start()

    barrier = pltpu.get_barrier_semaphore()
    for dev in (core_dev, y_dev, x_dev):
        pl.semaphore_signal(barrier, inc=1, device_id=dev, device_id_type=MESH)
    pl.semaphore_wait(barrier, 3)

    def own_copy(src, m):
        return pltpu.make_async_copy(
            src.at[2 * hi + m], ab.at[0, pl.ds(m * rows, span)], loc_sem.at[m]
        )

    def y_copy(src, m):
        return pltpu.make_async_remote_copy(
            src_ref=src.at[2 * (1 - hi) + m],
            dst_ref=ab.at[0, pl.ds(m * rows + span, span)],
            send_sem=ex_send.at[m], recv_sem=ex_recv.at[m],
            device_id=y_dev, device_id_type=MESH,
        )

    for is_sec, src in ((0, in_hbm), (1, cot_hbm)):
        @pl.when(sec == is_sec)
        def _(src=src):
            for m in range(MICRO):
                y_copy(src, m).start()
                own_copy(src, m).start()

    bg[...] = jnp.zeros_like(bg)

    def mrows(m):
        return pl.ds(pl.multiple_of(m * rows, rows), rows)

    def hop_copy(src, m):
        return pltpu.make_async_remote_copy(
            src_ref=src.at[mrows(m)], dst_ref=ab.at[1, mrows(m)],
            send_sem=hop_send.at[m], recv_sem=hop_recv.at[m],
            device_id=x_dev, device_id_type=MESH,
        )

    def kv_copy(m):
        return pltpu.make_async_remote_copy(
            src_ref=kv.at[m, pl.ds(0, rows)], dst_ref=kv.at[m, pl.ds(rows, rows)],
            send_sem=kv_send.at[m], recv_sem=kv_rsem.at[m],
            device_id=core_dev, device_id_type=MESH,
        )

    def dkv_copy(m):
        return pltpu.make_async_remote_copy(
            src_ref=dkv_send.at[m], dst_ref=dkv_recv.at[m],
            send_sem=dk_ssem.at[m], recv_sem=dk_rsem.at[m],
            device_id=core_dev, device_id_type=MESH,
        )

    def out_copies(kind, src, dst, m):
        table = 2 * hi + m
        base = m * rows
        return (
            pltpu.make_async_copy(
                src.at[pl.ds(base, span)], dst.at[table], out_loc.at[kind, m]
            ),
            pltpu.make_async_remote_copy(
                src_ref=src.at[pl.ds(base + span, span)], dst_ref=dst.at[table],
                send_sem=out_send.at[kind, m], recv_sem=out_recv.at[kind, m],
                device_id=y_dev, device_id_type=MESH,
            ),
        )

    def wait_slot(which, m):
        @pl.when(which == 0)
        def _():
            own_copy(in_hbm, m).wait()
            y_copy(in_hbm, m).wait_recv()

        @pl.when(which == 1)
        def _():
            hop_copy(yb, m).wait_recv()

    def positions(shape):
        row = lax.broadcasted_iota(jnp.int32, shape, 0)
        block = row // span
        within = row % span
        half = jnp.where(block % 2 == 0, hi, 1 - hi)
        core = jnp.where(block < 2, lo, 1 - lo)
        return (half * 2 + core) * span + within

    def lane_masks():
        lane = lax.broadcasted_iota(jnp.int32, (1, LANES), 1)
        left = (lane < hd).astype(F32).astype(BF)
        right = (lane >= hd).astype(F32).astype(BF)
        return left, right

    def split_heads(value):
        left, right = lane_masks()
        return jnp.concatenate([value * left, value * right], axis=0)

    def norm(resid, gain, shift):
        average = jnp.mean(resid, axis=-1, keepdims=True)
        centred = resid - average
        spread = jnp.mean(centred * centred, axis=-1, keepdims=True)
        scale = lax.rsqrt(spread + EPS)
        hat = centred * scale
        return hat, scale, hat * gain + shift

    def norm_back(grad, hat, scale, gain):
        dh = grad * gain
        return scale * (
            dh
            - jnp.mean(dh, axis=-1, keepdims=True)
            - hat * jnp.mean(dh * hat, axis=-1, keepdims=True)
        )

    def vec(ref, part):
        return ref[0:1, part * width:(part + 1) * width].astype(F32)

    def add_bias_grad(row, value):
        bg[row] += jnp.sum(value, axis=0, keepdims=True)

    def forward(step, m):
        r = mrows(m)
        wait_slot(sec, m)
        xs[r] = ab[sec, r]

        @pl.when(step == 0)
        def _():
            weight_copies[0].wait()

        x = xs[r]
        kv[m, pl.ds(0, rows), 0:width] = dot_nn(x, wqkv[:, width:2 * width]).astype(BF)
        kv[m, pl.ds(0, rows), width:2 * width] = (
            dot_nn(x, wqkv[:, 2 * width:3 * width]) + vec(abias_ref, 1)
        ).astype(BF)
        kv_copy(m).start()
        queries = (dot_nn(x, wqkv[:, 0:width]) + vec(abias_ref, 0)).astype(BF)
        q_s[r] = queries * (hd ** -0.5)

        @pl.when(step == 0)
        def _():
            for copy in weight_copies[1:]:
                copy.wait()

        kv_copy(m).wait_recv()
        key_bias = jnp.where(positions((keys, 1)) < len_ref[2 * hi + m], 0.0, -1e30)

        def head_pair(p, carry):
            cols = pl.ds(pl.multiple_of(p * LANES, LANES), LANES)
            vcols = pl.ds(pl.multiple_of(width + p * LANES, LANES), LANES)
            qq = split_heads(q_s[r, cols])
            st = dot_nt(kv[m, :, cols], qq) + key_bias
            top = jnp.max(st, axis=0, keepdims=True)
            e = jnp.exp(st - top)
            total = jnp.sum(e, axis=0, keepdims=True)
            lse[m, p] = top + jnp.log(total)
            o_t = dot_tn(kv[m, :, vcols], e.astype(BF)) * (1.0 / total)
            o_pair = jnp.concatenate([o_t[0:hd, 0:rows], o_t[hd:2 * hd, rows:2 * rows]], axis=0)
            os_[r, cols] = o_pair.T.astype(BF)
            return carry

        lax.fori_loop(0, pairs, head_pair, 0)

        r1 = x.astype(F32) + dot_nn(os_[r], wout[...]) + vec(obias_ref, 0)
        hat, scale, n1 = norm(r1, vec(gain_ref, 0), vec(shift_ref, 0))
        xh1[r] = hat
        rs1[r] = jnp.broadcast_to(scale, (rows, LANES))
        n1s[r] = n1.astype(BF)
        acc[...] = n1 + vec(obias_ref, 1)

        def ff_chunk(j, carry):
            cols = pl.ds(pl.multiple_of(j * width, width), width)
            u = dot_nn(n1s[r], wup[:, cols]) + bup_ref[0:1, cols].astype(F32)
            phi = 0.5 + 0.5 * lax.erf(u * INV_SQRT_2)
            f = (u * phi).astype(BF)
            fs[r, cols] = f
            gp[r, cols] = (phi + u * (jnp.exp(-0.5 * u * u) * INV_SQRT_2PI)).astype(BF)
            acc[...] += dot_nn(f, wdown[cols, :])
            return carry

        lax.fori_loop(0, nff, ff_chunk, 0)
        hat, scale, result = norm(acc[...], vec(gain_ref, 1), vec(shift_ref, 1))
        xh2[r] = hat
        rs2[r] = jnp.broadcast_to(scale, (rows, LANES))
        yb[r] = result.astype(BF)

        @pl.when(sec == 0)
        def _():
            hop_copy(yb, m).start()

        for copy in out_copies(0, yb, sout_hbm, m):
            copy.start()

    def backward(step, m):
        r = mrows(m)
        wait_slot(1 - sec, m)
        length = len_ref[2 * hi + m]
        row_pos = positions((rows, 1))
        row_scale = jnp.where((sec == 0) | (row_pos < length), 1.0, 0.0)
        dy = ab[1 - sec, r].astype(F32) * row_scale
        hat = xh2[r]
        add_bias_grad(9, dy * hat)
        add_bias_grad(11, dy)
        dr2 = norm_back(dy, hat, rs2[r, 0:1], vec(gain_ref, 1))
        dz = dr2.astype(BF)
        dzs[r] = dz
        add_bias_grad(3, dz.astype(F32))
        acc[...] = dr2

        def ff_chunk(j, carry):
            cols = pl.ds(pl.multiple_of(j * width, width), width)
            du = (dot_nt(dzs[r], wdown[cols, :]) * gp[r, cols].astype(F32)).astype(BF)
            dus[r, cols] = du
            bg[4 + j] += jnp.sum(du.astype(F32), axis=0, keepdims=True)
            acc[...] += dot_nt(du, wup[:, cols])
            return carry

        lax.fori_loop(0, nff, ff_chunk, 0)
        dn1 = acc[...]
        hat = xh1[r]
        add_bias_grad(8, dn1 * hat)
        add_bias_grad(10, dn1)
        grad1 = norm_back(dn1, hat, rs1[r, 0:1], vec(gain_ref, 0))
        dr1[...] = grad1
        da = grad1.astype(BF)
        das[r] = da
        add_bias_grad(2, da.astype(F32))
        do_s[...] = dot_nt(da, wout[...]).astype(BF)
        key_bias = jnp.where(positions((keys, 1)) < length, 0.0, -1e30)

        def head_pair(p, carry):
            cols = pl.ds(pl.multiple_of(p * LANES, LANES), LANES)
            vcols = pl.ds(pl.multiple_of(width + p * LANES, LANES), LANES)
            qq = split_heads(q_s[r, cols])
            dd = split_heads(do_s[:, cols])
            kp = kv[m, :, cols]
            pt = jnp.exp(dot_nt(kp, qq) + key_bias - lse[m, p])
            dv = dot_nn(pt.astype(BF), dd)
            dpt = dot_nt(kv[m, :, vcols], dd)
            inner = jnp.sum(pt * dpt, axis=0, keepdims=True)
            ds = (pt * (dpt - inner)).astype(BF)
            dk = dot_nn(ds, qq)
            dq_t = dot_tn(kp, ds)
            dq_pair = jnp.concatenate([dq_t[0:hd, 0:rows], dq_t[hd:2 * hd, rows:2 * rows]], axis=0)
            dps[r, cols] = (dq_pair.T * (hd ** -0.5)).astype(BF)
            dkv_own[:, cols] = dk[0:rows]
            dkv_own[:, vcols] = dv[0:rows]
            dkv_send[m, :, cols] = dk[rows:keys].astype(BF)
            dkv_send[m, :, vcols] = dv[rows:keys].astype(BF)
            return carry

        lax.fori_loop(0, pairs, head_pair, 0)
        dkv_copy(m).start()
        dq = dps[r, 0:width]
        add_bias_grad(0, dq.astype(F32))
        dr1[...] += dot_nt(dq, wqkv[:, 0:width])
        dkv_copy(m).wait_recv()
        dk = (dkv_own[:, 0:width] + dkv_recv[m, :, 0:width].astype(F32)).astype(BF)
        dv = (dkv_own[:, width:2 * width] + dkv_recv[m, :, width:2 * width].astype(F32)).astype(BF)
        dps[r, width:2 * width] = dk
        dps[r, 2 * width:3 * width] = dv
        add_bias_grad(1, dv.astype(F32))
        dx = dr1[...] + dot_nt(dk, wqkv[:, width:2 * width]) + dot_nt(dv, wqkv[:, 2 * width:3 * width])
        gb[r] = dx.astype(BF)

        @pl.when(sec == 1)
        def _():
            hop_copy(gb, m).start()

        for copy in out_copies(1, gb, sgrad_hbm, m):
            copy.start()

    def one_step(step, carry):
        is_forward = (step == 0) | ((step == 1) & (sec == 0)) | ((step == 2) & (sec == 1))
        m = jnp.where(sec == 0, step % 2, step // 2)

        @pl.when(is_forward)
        def _():
            forward(step, m)

        @pl.when(jnp.logical_not(is_forward))
        def _():
            backward(step, m)

        return carry

    lax.fori_loop(0, 2 * MICRO, one_step, 0)

    for m in range(MICRO):
        y_copy(in_hbm, m).wait_send()
        hop_copy(yb, m).wait_send()
        kv_copy(m).wait_send()
        dkv_copy(m).wait_send()
        for kind, src, dst in ((0, yb, sout_hbm), (1, gb, sgrad_hbm)):
            local_out, remote_out = out_copies(kind, src, dst, m)
            local_out.wait()
            remote_out.wait()


def run_layers(args, shapes):
    (inputs, cotangent, lengths, w_qkv, attn_bias, w_out, out_bias, w_up, bias_up, w_down,
     norm_gain, norm_bias) = args
    tables, span, width = inputs.shape
    ff = w_up.shape[2]
    rows = 2 * span
    total = MICRO * rows
    keys = 2 * rows
    any_spec = pl.BlockSpec(memory_space=pl.ANY)
    vmem = pl.BlockSpec(memory_space=pltpu.VMEM)
    smem = pl.BlockSpec(memory_space=pltpu.SMEM)
    dma = pltpu.SemaphoreType.DMA
    return pl.pallas_call(
        layers_kernel,
        name="layers",
        out_shape=(
            jax.ShapeDtypeStruct((tables, span, width), BF),
            jax.ShapeDtypeStruct((tables, span, width), BF),
            jax.ShapeDtypeStruct((total, width), BF),
            jax.ShapeDtypeStruct((total, width), BF),
            jax.ShapeDtypeStruct((total, width), BF),
            jax.ShapeDtypeStruct((total, ff), BF),
            jax.ShapeDtypeStruct((total, 3 * width), BF),
            jax.ShapeDtypeStruct((total, width), BF),
            jax.ShapeDtypeStruct((total, ff), BF),
            jax.ShapeDtypeStruct((total, width), BF),
            jax.ShapeDtypeStruct((12, 1, width), F32),
        ),
        in_specs=[smem] + [any_spec] * 6 + [vmem] * 5,
        out_specs=(any_spec, any_spec) + (vmem,) * 9,
        scratch_shapes=[
            pltpu.VMEM((2, total, width), BF),
            pltpu.VMEM((width, 3 * width), BF),
            pltpu.VMEM((width, width), BF),
            pltpu.VMEM((width, ff), BF),
            pltpu.VMEM((ff, width), BF),
            pltpu.VMEM((total, width), BF),
            pltpu.VMEM((MICRO, keys, 2 * width), BF),
            pltpu.VMEM((MICRO, H // 2, 1, 2 * rows), F32),
            pltpu.VMEM((8, LANES), BF),
            pltpu.VMEM((total, width), F32),
            pltpu.VMEM((total, width), F32),
            pltpu.VMEM((total, LANES), F32),
            pltpu.VMEM((total, LANES), F32),
            pltpu.VMEM((total, ff), BF),
            pltpu.VMEM((rows, width), F32),
            pltpu.VMEM((rows, width), F32),
            pltpu.VMEM((rows, width), BF),
            pltpu.VMEM((rows, 2 * width), F32),
            pltpu.VMEM((MICRO, rows, 2 * width), BF),
            pltpu.VMEM((MICRO, rows, 2 * width), BF),
            pltpu.VMEM((total, width), BF),
            pltpu.VMEM((total, width), BF),
            dma((4,)), dma((MICRO,)), dma((MICRO,)), dma((MICRO,)), dma((MICRO,)), dma((MICRO,)),
            dma((MICRO,)), dma((MICRO,)), dma((MICRO,)), dma((MICRO,)),
            dma((2, MICRO)), dma((2, MICRO)), dma((2, MICRO)),
        ],
        compiler_params=pltpu.CompilerParams(
            collective_id=0, has_side_effects=True, vmem_limit_bytes=60 * 2 ** 20
        ),
    )(lengths, inputs, cotangent, w_qkv, w_out, w_up, w_down,
      attn_bias, out_bias, bias_up, norm_gain, norm_bias)


def local(*args):
    (sout, sgrad, xs, os_, n1s, fs, dps, das, dus, dzs, bg) = run_layers(args, None)
    width = xs.shape[1]
    index = lax.axis_index("seq") * lax.axis_size("dp") + lax.axis_index("dp")
    count = lax.axis_size("seq") * lax.axis_size("dp")

    def weight_grad(a, b):
        full = dot_tn(a, b).astype(BF)
        return lax.psum_scatter(full, ("seq", "dp"), scatter_dimension=0, tiled=True).astype(F32)

    sums = lax.psum(bg.reshape(12 * width), ("seq", "dp"))

    def piece(start, rows):
        part = sums[start * width:(start + rows) * width]
        size = rows * width // count
        return lax.dynamic_slice_in_dim(part, index * size, size, 0)[None]

    return (
        sout[None],
        sgrad.astype(F32)[None],
        weight_grad(xs, dps)[None],
        piece(0, 2),
        weight_grad(os_, das)[None],
        piece(2, 2),
        weight_grad(n1s, dus)[None],
        piece(4, 4),
        weight_grad(fs, dzs)[None],
        piece(8, 2),
        piece(10, 2),
    )


def solution(mesh):
    return jax.shard_map(
        local,
        mesh=mesh,
        in_specs=(
            P("dp", "seq", None),
            P("dp", "seq", None),
            P("dp"),
            P("section", None, None),
            P("section", None),
            P("section", None, None),
            P("section", None),
            P("section", None, None),
            P("section", None),
            P("section", None, None),
            P("section", None),
            P("section", None),
        ),
        out_specs=(
            P("section", "dp", "seq", None),
            P("section", "dp", "seq", None),
            P("section", ("seq", "dp"), None),
            P("section", ("seq", "dp")),
            P("section", ("seq", "dp"), None),
            P("section", ("seq", "dp")),
            P("section", ("seq", "dp"), None),
            P("section", ("seq", "dp")),
            P("section", ("seq", "dp"), None),
            P("section", ("seq", "dp")),
            P("section", ("seq", "dp")),
        ),
        check_vma=False,
    )
```

time: 1040 us -> 431 us (0.41)
  matrix products: 288 us -> 18.2 us
  waiting for transfers between devices: 417 us -> 197 us
  local copies, waits for them, and re-layouts: 153 us -> 6.94 us
  Pallas kernels: 0 us -> 124 us
  other arithmetic: 80.4 us -> 8.18 us
  starting transfers between devices: 13.7 us -> 0.34 us
    dot_general x63 -> x4, matrix products: 247 us -> 18.2 us  [dot_tn(): lax.dot_general(a, b, (((0,), (0,)), ((), ())), preferred_element_type=F32)]
    reduce_scatter x10 -> x4, waiting for transfers between devices: 331 us -> 197 us  [weight_grad(): lax.psum_scatter(full, ('seq', 'dp'), scatter_dimension=0, tiled=True)]
    pallas_call x0 -> x1, Pallas kernels: none -> 124 us  [run_layers(): pl.pallas_call(layers_kernel, name='layers', out_shape=(jax.ShapeDtypeStr...]
    unnamed x1 -> x0, blocking collectives: 62.9 us -> none
    psum x0 -> x1, blocking collectives: none -> 62 us  [local(): sums = lax.psum(bg.reshape(12 * width), ('seq', 'dp'))]
    convert_element_type x30 -> x0, local copies, waits for them, and re-layouts: 50.9 us -> none  [the longest x6 11.5 us: project_qkv(): queries = (projected[:, :width] + weights[1][:width]).astype(jnp.bfloat16)]
    all_gather x12 -> x0, waiting for transfers between devices: 47 us -> none  [the longest x6 24.6 us: local(): lax.all_gather(value_rows.reshape(per_batch, span, width), 'seq', axis=1,...]
    sub x6 -> x0, matrix products: 41.1 us -> none  [attention_parts(): exp_scores = jnp.exp(scores - row_top)]
  transfers between devices with their start and end apart: 26 -> 4, of which waited for: 15 -> 3; matrix products, arithmetic and copies ran while one was open for 36% -> 5% of each run, Pallas kernels for 0% -> 0%
where the time goes in v1:
time: 431 us
  waiting for transfers between devices  197 us (46%)
  Pallas kernels  124 us (29%)
  blocking collectives  62 us (14%)
  matrix products  18.2 us (4%)
  between operations  13.8 us (3%)
  other arithmetic  8.18 us (2%)
  local copies, waits for them, and re-layouts  6.94 us (2%)
    reduce_scatter x4, waiting for transfers between devices, weight_grad(): lax.psum_scatter(full, ('seq', 'dp'), scatter_dimension=0, tiled=True)  197 us
    pallas_call x1, Pallas kernels, run_layers(): pl.pallas_call(layers_kernel, name='layers', out_shape=(jax.ShapeDtypeStr...  124 us
    psum x1, blocking collectives, local(): sums = lax.psum(bg.reshape(12 * width), ('seq', 'dp'))  62 us
    dot_general x4, matrix products, dot_tn(): lax.dot_general(a, b, (((0,), (0,)), ((), ())), preferred_element_type=F32)  18.2 us
  transfers between devices with their start and end apart: 4, of which 3 were waited for; matrix products, arithmetic and copies ran while one was open for 5% of the time, Pallas kernels for 0%

profile of v1, /device:TPU:0, one launch (start us, length us, event | category | flops | bytes accessed | tf_op | source)
XLA Modules:
  0.0 430.9 jit_solution(13180038800128307695)
XLA Ops:
  7.2 0.0 reduce-scatter.7.cloned.1.call-start
  7.2 124.4 %layers.1 = (bf16[4,128,768]{2,1,0:T(8,128)(2,1)}, bf16[4,128,768]{2,1,0:T(8,128)(2,1)}, bf16[512,768]{1,0:T(8,128)(2,1)}, bf16[512,768]{1,0:T(8,128)(2,1)}, bf1...) custom-call(s32[4]{0:T(128)} %len_ref.1, ...), custom_call_target="tpu_custom_call" | custom-call | tf_op jit(solution)/shard_map/layers/pallas_call | solution.py:373
  131.7 0.0 copy-start.5
  131.7 0.0 copy-start.6
  131.7 3.3 convolution_convert_fusion.3
  135.0 0.0 reduce-scatter.7.cloned.1.call-update
  135.1 0.0 reduce-scatter.5.cloned.1.call-start
  135.1 0.0 copy-done.5
  135.1 0.0 copy-done.6
  135.1 3.8 convolution_convert_fusion.2
  139.0 0.0 copy-start.4
  139.0 0.0 reduce-scatter.5.cloned.1.call-update
  139.0 0.2 reduce-scatter.9.cloned.1.call-start
  139.2 1.6 copy-done.4
  140.9 5.5 %convolution_convert_fusion.1 = bf16[768,3072]{1,0:T(8,128)(2,1)} fusion(bf16[512,768]{1,0:T(8,128)(2,1)} %get-tuple-element.29, bf16[512,3072]{1,0:T(8,128)(2,1)S(1)} %copy-done.4), kind=kOutput, calls=%fused_computation.1 | convolution fusion | flops 2418278400 | bytes 8650752 | tf_op jit(solution)/shard_map/dot_general | solution.py:30
  146.4 0.0 copy-start.3
  146.4 0.0 reduce-scatter.9.cloned.1.call-update
  146.4 0.0 reduce-scatter.11.cloned.1.call-start
  146.4 1.9 copy-done.3
  148.3 5.5 %convolution_convert_fusion = bf16[3072,768]{1,0:T(8,128)(2,1)} fusion(bf16[512,3072]{1,0:T(8,128)(2,1)S(1)} %copy-done.3, bf16[512,768]{1,0:T(8,128)(2,1)} %get-tuple-element.32), kind=kOutput, calls=%fused_computation | convolution fusion | flops 2418278400 | bytes 8650752 | tf_op jit(solution)/shard_map/dot_general | solution.py:30
  153.8 0.0 copy-start.2
  153.8 0.0 copy-start.1
  153.8 0.0 reduce-scatter.11.cloned.1.call-update
  153.9 0.0 copy-start
  153.9 0.7 copy-done.2
  154.6 62.0 %psum.7 = f32[9216]{0:T(1024)S(1)} all-reduce(f32[9216]{0:T(1024)S(1)} %bitcast.35), channel_id=1, replica_groups=mesh['section'=2,'seq'=4,'dp'=4] {'seq','dp'}, use_global_device_ids=true, to_apply=%region_1.0 | all-reduce | flops 9216 | bytes 73728 | tf_op jit(solution)/shard_map/psum | solution.py:435
  216.6 0.6 dynamic_slice.17
  217.2 0.6 dynamic-slice_bitcast_fusion
  217.8 0.6 dynamic-slice_bitcast_fusion.2
  218.4 0.0 copy-done.1
  218.4 1.3 bitcast_convert_fusion
  219.7 0.0 reduce-scatter.7.cloned.1.call-done
  219.7 1.6 bitcast_convert_fusion.4
  221.2 43.4 %reduce-scatter.5.cloned.1.call-done = bf16[48,2304]{1,0:T(8,128)(2,1)} async-done(((bf16[768,2304]{1,0:T(8,128)(2,1)}), bf16[48,2304]{1,0:T(8,128)(2,1)}) %reduce-scatter.5.cloned.1.call-update) | async-done | bytes 221200 | tf_op jit(solution)/shard_map/reduce_scatter | solution.py:433
  264.6 1.7 bitcast_convert_fusion.3
  266.3 76.5 %reduce-scatter.9.cloned.1.call-done = bf16[48,3072]{1,0:T(8,128)(2,1)} async-done(((bf16[768,3072]{1,0:T(8,128)(2,1)}), bf16[48,3072]{1,0:T(8,128)(2,1)}) %reduce-scatter.9.cloned.1.call-update) | async-done | bytes 294928 | tf_op jit(solution)/shard_map/reduce_scatter | solution.py:433
  342.8 1.8 bitcast_convert_fusion.2
  344.7 77.0 %reduce-scatter.11.cloned.1.call-done = bf16[192,768]{1,0:T(8,128)(2,1)} async-done(((bf16[3072,768]{1,0:T(8,128)(2,1)}), bf16[192,768]{1,0:T(8,128)(2,1)}) %reduce-scatter.11.cloned.1.call-update) | async-done | bytes 294928 | tf_op jit(solution)/shard_map/reduce_scatter | solution.py:433
  421.7 1.8 bitcast_convert_fusion.1
  423.5 0.0 copy-done
  423.5 0.9 copy.24
  (2 shorter events, 0.0 us)
Async XLA Ops:
  7.2 212.5 %reduce-scatter.7.cloned.1.call-start = ((), (), s32[]{:S(2)}) async-start(), calls=%async_computation.5 | async-start | bytes 1253376 | tf_op jit(solution)/shard_map/reduce_scatter | solution.py:433
  131.7 3.4 copy-start.5
  131.7 3.4 copy-start.6
  135.1 129.5 %reduce-scatter.5.cloned.1.call-start = ((), (), s32[]{:S(2)}) async-start(), calls=%async_computation.4 | async-start | bytes 3760128 | tf_op jit(solution)/shard_map/reduce_scatter | solution.py:433
  139.0 1.9 copy-start.4
  139.0 203.8 %reduce-scatter.9.cloned.1.call-start = ((), (), s32[]{:S(2)}) async-start(), calls=%async_computation.6 | async-start | bytes 5013504 | tf_op jit(solution)/shard_map/reduce_scatter | solution.py:433
  146.4 1.9 copy-start.3
  146.4 275.3 %reduce-scatter.11.cloned.1.call-start = ((), (), s32[]{:S(2)}) async-start(), calls=%async_computation.7 | async-start | bytes 5013504 | tf_op jit(solution)/shard_map/reduce_scatter | solution.py:433
  153.8 0.8 copy-start.2
  153.8 64.6 %copy-start.1 = (bf16[4,128,768]{2,1,0:T(8,128)(2,1)S(1)}, bf16[4,128,768]{2,1,0:T(8,128)(2,1)}, u32[]{:S(2)}) copy-start(bf16[4,128,768]{2,1,0:T(8,128)(2,1)} %get-tuple-element.23) | copy-start | bytes 2359300
  153.9 269.7 %copy-start = (bf16[4,128,768]{2,1,0:T(8,128)(2,1)S(1)}, bf16[4,128,768]{2,1,0:T(8,128)(2,1)}, u32[]{:S(2)}) copy-start(bf16[4,128,768]{2,1,0:T(8,128)(2,1)} %get-tuple-element.22) | copy-start | bytes 2359300
Sparse Core Ops, SparseCore 0:
  135.2 58.3 reduce-scatter.6
  197.4 67.1 reduce-scatter.4
  268.5 74.3 reduce-scatter.8
  347.0 74.6 reduce-scatter.10

commit v2 on v1

--- a/solution.py
+++ b/solution.py
@@ -16,6 +16,10 @@
 LANES = 128
 INV_SQRT_2PI = 0.3989422804014327
 INV_SQRT_2 = 0.7071067811865476
+L_F, L_N, L_O, L_X, L_COUNT = 0, 4, 5, 6, 7
+R_P, R_A, R_U, R_Z, R_COUNT = 0, 3, 4, 8, 9
+CHUNKS = 12
+Z_FIRST = 2
 
 
 def dot_nn(a, b):
@@ -33,8 +37,8 @@
 def layers_kernel(
     len_ref, in_hbm, cot_hbm, wqkv_hbm, wout_hbm, wup_hbm, wdown_hbm,
     abias_ref, obias_ref, bup_ref, gain_ref, shift_ref,
-    sout_hbm, sgrad_hbm, xs, os_, n1s, fs, dps, das, dus, dzs, bg,
-    ab, wqkv, wout, wup, wdown, q_s, kv, lse, ot, xh1, xh2, rs1, rs2, gp, dr1, acc, do_s,
+    sout_hbm, sgrad_hbm, lt, rt, bg,
+    ab, wqkv, wout, wup, wdown, q_s, kv, lse, o_s, n_s, xh1, xh2, rs1, rs2, gp, dr1, acc, do_s,
     dkv_own, dkv_send, dkv_recv, yb, gb,
     w_sem, loc_sem, ex_send, ex_recv, hop_send, hop_recv, kv_send, kv_rsem, dk_ssem, dk_rsem,
     out_loc, out_send, out_recv,
@@ -47,6 +51,8 @@
     hd = width // H
     pairs = H // 2
     nff = ff // width
+    dp_size = 4
+    unit = width // 16
     sec = lax.axis_index("section")
     seq = lax.axis_index("seq")
     dp = lax.axis_index("dp")
@@ -183,13 +189,12 @@
     def forward(step, m):
         r = mrows(m)
         wait_slot(sec, m)
-        xs[r] = ab[sec, r]
 
         @pl.when(step == 0)
         def _():
             weight_copies[0].wait()
 
-        x = xs[r]
+        x = ab[sec, r]
         kv[m, pl.ds(0, rows), 0:width] = dot_nn(x, wqkv[:, width:2 * width]).astype(BF)
         kv[m, pl.ds(0, rows), width:2 * width] = (
             dot_nn(x, wqkv[:, 2 * width:3 * width]) + vec(abias_ref, 1)
@@ -217,24 +222,30 @@
             lse[m, p] = top + jnp.log(total)
             o_t = dot_tn(kv[m, :, vcols], e.astype(BF)) * (1.0 / total)
             o_pair = jnp.concatenate([o_t[0:hd, 0:rows], o_t[hd:2 * hd, rows:2 * rows]], axis=0)
-            os_[r, cols] = o_pair.T.astype(BF)
+            lt[L_O, cols, r] = o_pair.astype(BF)
+            o_s[:, cols] = o_pair.T.astype(BF)
             return carry
 
         lax.fori_loop(0, pairs, head_pair, 0)
 
-        r1 = x.astype(F32) + dot_nn(os_[r], wout[...]) + vec(obias_ref, 0)
+        r1 = x.astype(F32) + dot_nn(o_s[...], wout[...]) + vec(obias_ref, 0)
         hat, scale, n1 = norm(r1, vec(gain_ref, 0), vec(shift_ref, 0))
         xh1[r] = hat
         rs1[r] = jnp.broadcast_to(scale, (rows, LANES))
-        n1s[r] = n1.astype(BF)
+        n_s[...] = n1.astype(BF)
         acc[...] = n1 + vec(obias_ref, 1)
 
         def ff_chunk(j, carry):
             cols = pl.ds(pl.multiple_of(j * width, width), width)
-            u = dot_nn(n1s[r], wup[:, cols]) + bup_ref[0:1, cols].astype(F32)
+            u = dot_nn(n_s[...], wup[:, cols]) + bup_ref[0:1, cols].astype(F32)
             phi = 0.5 + 0.5 * lax.erf(u * INV_SQRT_2)
             f = (u * phi).astype(BF)
-            fs[r, cols] = f
+            f_t = f.T
+            for z in range(dp_size):
+                for part in range(nff):
+                    lt[part, pl.ds((j * dp_size + z) * unit, unit), r] = f_t[
+                        (z * nff + part) * unit:(z * nff + part + 1) * unit
+                    ]
             gp[r, cols] = (phi + u * (jnp.exp(-0.5 * u * u) * INV_SQRT_2PI)).astype(BF)
             acc[...] += dot_nn(f, wdown[cols, :])
             return carry
@@ -251,6 +262,8 @@
 
         for copy in out_copies(0, yb, sout_hbm, m):
             copy.start()
+        lt[L_X, :, r] = ab[sec, r].T
+        lt[L_N, :, r] = n_s[...].T
 
     def backward(step, m):
         r = mrows(m)
@@ -264,14 +277,14 @@
         add_bias_grad(11, dy)
         dr2 = norm_back(dy, hat, rs2[r, 0:1], vec(gain_ref, 1))
         dz = dr2.astype(BF)
-        dzs[r] = dz
+        rt[R_Z, r] = dz
         add_bias_grad(3, dz.astype(F32))
         acc[...] = dr2
 
         def ff_chunk(j, carry):
             cols = pl.ds(pl.multiple_of(j * width, width), width)
-            du = (dot_nt(dzs[r], wdown[cols, :]) * gp[r, cols].astype(F32)).astype(BF)
-            dus[r, cols] = du
+            du = (dot_nt(rt[R_Z, r], wdown[cols, :]) * gp[r, cols].astype(F32)).astype(BF)
+            rt[R_U + j, r] = du
             bg[4 + j] += jnp.sum(du.astype(F32), axis=0, keepdims=True)
             acc[...] += dot_nt(du, wup[:, cols])
             return carry
@@ -284,7 +297,7 @@
         grad1 = norm_back(dn1, hat, rs1[r, 0:1], vec(gain_ref, 0))
         dr1[...] = grad1
         da = grad1.astype(BF)
-        das[r] = da
+        rt[R_A, r] = da
         add_bias_grad(2, da.astype(F32))
         do_s[...] = dot_nt(da, wout[...]).astype(BF)
         key_bias = jnp.where(positions((keys, 1)) < length, 0.0, -1e30)
@@ -303,7 +316,7 @@
             dk = dot_nn(ds, qq)
             dq_t = dot_tn(kp, ds)
             dq_pair = jnp.concatenate([dq_t[0:hd, 0:rows], dq_t[hd:2 * hd, rows:2 * rows]], axis=0)
-            dps[r, cols] = (dq_pair.T * (hd ** -0.5)).astype(BF)
+            rt[R_P, r, cols] = (dq_pair.T * (hd ** -0.5)).astype(BF)
             dkv_own[:, cols] = dk[0:rows]
             dkv_own[:, vcols] = dv[0:rows]
             dkv_send[m, :, cols] = dk[rows:keys].astype(BF)
@@ -312,14 +325,14 @@
 
         lax.fori_loop(0, pairs, head_pair, 0)
         dkv_copy(m).start()
-        dq = dps[r, 0:width]
+        dq = rt[R_P, r]
         add_bias_grad(0, dq.astype(F32))
         dr1[...] += dot_nt(dq, wqkv[:, 0:width])
         dkv_copy(m).wait_recv()
         dk = (dkv_own[:, 0:width] + dkv_recv[m, :, 0:width].astype(F32)).astype(BF)
         dv = (dkv_own[:, width:2 * width] + dkv_recv[m, :, width:2 * width].astype(F32)).astype(BF)
-        dps[r, width:2 * width] = dk
-        dps[r, 2 * width:3 * width] = dv
+        rt[R_P + 1, r] = dk
+        rt[R_P + 2, r] = dv
         add_bias_grad(1, dv.astype(F32))
         dx = dr1[...] + dot_nt(dk, wqkv[:, width:2 * width]) + dot_nt(dv, wqkv[:, 2 * width:3 * width])
         gb[r] = dx.astype(BF)
@@ -376,18 +389,12 @@
         out_shape=(
             jax.ShapeDtypeStruct((tables, span, width), BF),
             jax.ShapeDtypeStruct((tables, span, width), BF),
-            jax.ShapeDtypeStruct((total, width), BF),
-            jax.ShapeDtypeStruct((total, width), BF),
-            jax.ShapeDtypeStruct((total, width), BF),
-            jax.ShapeDtypeStruct((total, ff), BF),
-            jax.ShapeDtypeStruct((total, 3 * width), BF),
-            jax.ShapeDtypeStruct((total, width), BF),
-            jax.ShapeDtypeStruct((total, ff), BF),
-            jax.ShapeDtypeStruct((total, width), BF),
+            jax.ShapeDtypeStruct((L_COUNT, width, total), BF),
+            jax.ShapeDtypeStruct((R_COUNT, total, width), BF),
             jax.ShapeDtypeStruct((12, 1, width), F32),
         ),
         in_specs=[smem] + [any_spec] * 6 + [vmem] * 5,
-        out_specs=(any_spec, any_spec) + (vmem,) * 9,
+        out_specs=(any_spec, any_spec) + (vmem,) * 3,
         scratch_shapes=[
             pltpu.VMEM((2, total, width), BF),
             pltpu.VMEM((width, 3 * width), BF),
@@ -397,7 +404,8 @@
             pltpu.VMEM((total, width), BF),
             pltpu.VMEM((MICRO, keys, 2 * width), BF),
             pltpu.VMEM((MICRO, H // 2, 1, 2 * rows), F32),
-            pltpu.VMEM((8, LANES), BF),
+            pltpu.VMEM((rows, width), BF),
+            pltpu.VMEM((rows, width), BF),
             pltpu.VMEM((total, width), F32),
             pltpu.VMEM((total, width), F32),
             pltpu.VMEM((total, LANES), F32),
@@ -422,17 +430,323 @@
       attn_bias, out_bias, bias_up, norm_gain, norm_bias)
 
 
+def grads_kernel(
+    lt, rt, bg,
+    out, bg_out,
+    core_src, chip, own, y_buf, up, down, turn_src, turn_buf, b_src, b_core, b_y, b_z,
+    core_ss, core_rs, y_ss, y_rs, up_ss, up_rs, down_ss, down_rs, turn_ss, turn_rs,
+    bc_ss, bc_rs, bz_ss, bz_rs,
+):
+    count = b_z.shape[0]
+    unit = out.shape[1]
+    block = count * unit
+    sec = lax.axis_index("section")
+    seq = lax.axis_index("seq")
+    z = lax.axis_index("dp")
+    hi = seq // 2
+    lo = seq % 2
+    core_dev = (sec, hi * 2 + 1 - lo, z)
+    y_dev = (sec, (1 - hi) * 2 + lo, z)
+
+    def z_dev(index):
+        return (sec, seq, index)
+
+    barrier = pltpu.get_barrier_semaphore()
+    for dev in (core_dev, y_dev):
+        pl.semaphore_signal(barrier, inc=1, device_id=dev, device_id_type=MESH)
+    for by in range(1, count):
+        pl.semaphore_signal(
+            barrier, inc=1, device_id=z_dev((z + by) % count), device_id_type=MESH
+        )
+    pl.semaphore_wait(barrier, 1 + count)
+
+    def remote(src, dst, send, recv, dev):
+        return pltpu.make_async_remote_copy(
+            src_ref=src, dst_ref=dst, send_sem=send, recv_sem=recv,
+            device_id=dev, device_id_type=MESH,
+        )
+
+    def core_copy(k, half):
+        return remote(
+            core_src.at[k, half], chip.at[k, half], core_ss.at[k, half], core_rs.at[k, half], core_dev
+        )
+
+    def y_copy(k):
+        return remote(chip.at[k, 1 - hi], y_buf.at[k], y_ss.at[k], y_rs.at[k], y_dev)
+
+    def turn_copy(k):
+        return remote(turn_src.at[k], turn_buf.at[k], turn_ss.at[k], turn_rs.at[k], y_dev)
+
+    def piece(k, half, target):
+        return chip.at[k, half, pl.ds(pl.multiple_of(target * unit, unit), unit)]
+
+    def up_copy(job, k, half, target):
+        return remote(
+            piece(k, half, target), up.at[job, target], up_ss.at[job, target],
+            up_rs.at[job, target], z_dev(jnp.minimum(z + 1, count - 1)),
+        )
+
+    def down_copy(job, k, half, target):
+        return remote(
+            piece(k, half, target), down.at[job, target], down_ss.at[job, target],
+            down_rs.at[job, target], z_dev(jnp.maximum(z - 1, 0)),
+        )
+
+    def add_piece(k, half, target, landed):
+        ref = piece(k, half, target)
+        ref[...] = (ref[...].astype(F32) + landed[...].astype(F32)).astype(BF)
+
+    def hop(number, job, k, half):
+        @pl.when(z == number - 1)
+        def _():
+            for target in range(count - 1, number - 1, -1):
+                if number > 1:
+                    up_copy(job, k, half, target).wait_recv()
+                    add_piece(k, half, target, up.at[job, target])
+                up_copy(job, k, half, target).start()
+
+        @pl.when(z == count - number)
+        def _():
+            for target in range(0, count - number):
+                if number > 1:
+                    down_copy(job, k, half, target).wait_recv()
+                    add_piece(k, half, target, down.at[job, target])
+                down_copy(job, k, half, target).start()
+
+    def arrive(job, k, half, dst):
+        dst[...] = piece(k, half, z)[...].astype(F32)
+
+        @pl.when(z > 0)
+        def _():
+            up_copy(job, k, half, z).wait_recv()
+            dst[...] += up[job, z].astype(F32)
+
+        @pl.when(z < count - 1)
+        def _():
+            down_copy(job, k, half, z).wait_recv()
+            dst[...] += down[job, z].astype(F32)
+
+    def product(k):
+        left = jnp.where(k < 8, jnp.minimum(k, L_N), jnp.where(k == 8, L_O, L_X))
+        right = jnp.where(k < 4, R_Z, jnp.where(k < 8, k, jnp.where(k == 8, R_A, k - 9)))
+        for half in range(2):
+            base = pl.multiple_of((half * 2 + 1 - lo) * block, block)
+            core_src[k, half] = dot_nn(lt[left, pl.ds(base, block), :], rt[right]).astype(BF)
+            core_copy(k, half).start()
+        for half in range(2):
+            base = pl.multiple_of((half * 2 + lo) * block, block)
+            own[k % 2, half] = dot_nn(lt[left, pl.ds(base, block), :], rt[right])
+
+    def chip_sum(k):
+        for half in range(2):
+            core_copy(k, half).wait_recv()
+            chip[k, half] = (own[k % 2, half] + chip[k, half].astype(F32)).astype(BF)
+
+    def bias_core():
+        return remote(b_src.at[0], b_core, bc_ss.at[0], bc_rs.at[0], core_dev)
+
+    def bias_y():
+        return remote(b_src.at[1], b_y, bc_ss.at[1], bc_rs.at[1], y_dev)
+
+    def bias_z(by):
+        return remote(
+            b_src.at[2], b_z.at[by], bz_ss.at[by], bz_rs.at[by], z_dev((z + by) % count)
+        )
+
+    def step(t, carry):
+        def at(first, last):
+            return (t >= first) & (t <= last)
+
+        @pl.when(t == 0)
+        def _():
+            b_src[0] = bg[...]
+            bias_core().start()
+
+        @pl.when(t < CHUNKS)
+        def _():
+            product(t)
+
+        @pl.when(at(1, CHUNKS))
+        def _():
+            chip_sum(t - 1)
+
+        @pl.when(at(1, Z_FIRST))
+        def _():
+            for half in range(2):
+                hop(1, 2 * (t - 1) + half, t - 1, half)
+
+        @pl.when(at(Z_FIRST + 1, CHUNKS))
+        def _():
+            y_copy(t - 1).start()
+
+        @pl.when(t == 2)
+        def _():
+            bias_core().wait_recv()
+            b_src[1] = b_src[0] + b_core[...]
+            bias_y().start()
+
+        @pl.when(t == 4)
+        def _():
+            bias_y().wait_recv()
+            b_src[2] = b_src[1] + b_y[...]
+            for by in range(1, count):
+                bias_z(by).start()
+
+        @pl.when(at(Z_FIRST + 3, CHUNKS + 2))
+        def _():
+            k = t - 3
+            y_copy(k).wait_recv()
+            chip[k, hi] = (chip[k, hi].astype(F32) + y_buf[k].astype(F32)).astype(BF)
+            hop(1, k + Z_FIRST, k, hi)
+
+        for number in range(2, count):
+            @pl.when(at(Z_FIRST + 2 + number, CHUNKS + 1 + number))
+            def _(number=number):
+                k = t - 2 - number
+                hop(number, k + Z_FIRST, k, hi)
+
+            @pl.when(at(2 * number, 2 * number + Z_FIRST - 1))
+            def _(number=number):
+                k = t - 2 * number
+                for half in range(2):
+                    hop(number, 2 * k + half, k, half)
+
+        @pl.when(at(Z_FIRST + 2 + count, CHUNKS + 1 + count))
+        def _():
+            k = t - 2 - count
+            arrive(k + Z_FIRST, k, hi, out.at[k])
+
+        @pl.when(at(2 * count, 2 * count + Z_FIRST - 1))
+        def _():
+            k = t - 2 * count
+            arrive(2 * k + 1 - hi, k, 1 - hi, out.at[k])
+            turn_src[k] = out[k].astype(BF)
+            turn_copy(k).start()
+            arrive(2 * k + hi, k, hi, out.at[k])
+
+        @pl.when(at(2 * count + 2, 2 * count + 1 + Z_FIRST))
+        def _():
+            k = t - 2 * count - 2
+            turn_copy(k).wait_recv()
+            out[k] += turn_buf[k].astype(F32)
+
+        return carry
+
+    lax.fori_loop(0, CHUNKS + 2 + count, step, 0)
+
+    for by in range(1, count):
+        bias_z(by).wait_recv()
+    total = b_src[2]
+    for by in range(1, count):
+        total = total + b_z[by]
+    bg_out[...] = total
+    bias_core().wait_send()
+    bias_y().wait_send()
+    for by in range(1, count):
+        bias_z(by).wait_send()
+
+    def sent(job, k, half):
+        for target in range(count):
+            @pl.when(target > z)
+            def _(target=target):
+                up_copy(job, k, half, target).wait_send()
+
+            @pl.when(target < z)
+            def _(target=target):
+                down_copy(job, k, half, target).wait_send()
+
+    def drain(k, carry):
+        for half in range(2):
+            core_copy(k, half).wait_send()
+
+        @pl.when(k < Z_FIRST)
+        def _():
+            turn_copy(k).wait_send()
+            for half in range(2):
+                sent(2 * k + half, k, half)
+
+        @pl.when(k >= Z_FIRST)
+        def _():
+            y_copy(k).wait_send()
+            sent(k + Z_FIRST, k, hi)
+
+        return carry
+
+    lax.fori_loop(0, CHUNKS, drain, 0)
+
+
+def run_grads(lt, rt, bg):
+    count = lax.axis_size("dp")
+    width = lt.shape[1]
+    unit = width // (4 * count)
+    block = count * unit
+    jobs = CHUNKS + Z_FIRST
+    vmem = pl.BlockSpec(memory_space=pltpu.VMEM)
+    dma = pltpu.SemaphoreType.DMA
+    return pl.pallas_call(
+        grads_kernel,
+        name="grads",
+        out_shape=(
+            jax.ShapeDtypeStruct((CHUNKS, unit, width), F32),
+            jax.ShapeDtypeStruct((12, 1, width), F32),
+        ),
+        in_specs=[vmem] * 3,
+        out_specs=(vmem,) * 2,
+        scratch_shapes=[
+            pltpu.VMEM((CHUNKS, 2, block, width), BF),
+            pltpu.VMEM((CHUNKS, 2, block, width), BF),
+            pltpu.VMEM((2, 2, block, width), F32),
+            pltpu.VMEM((CHUNKS, block, width), BF),
+            pltpu.VMEM((jobs, count, unit, width), BF),
+            pltpu.VMEM((jobs, count, unit, width), BF),
+            pltpu.VMEM((Z_FIRST, unit, width), BF),
+            pltpu.VMEM((Z_FIRST, unit, width), BF),
+            pltpu.VMEM((3, 12, 1, width), F32),
+            pltpu.VMEM((12, 1, width), F32),
+            pltpu.VMEM((12, 1, width), F32),
+            pltpu.VMEM((count, 12, 1, width), F32),
+            dma((CHUNKS, 2)), dma((CHUNKS, 2)), dma((CHUNKS,)), dma((CHUNKS,)),
+            dma((jobs, count)), dma((jobs, count)), dma((jobs, count)), dma((jobs, count)),
+            dma((Z_FIRST,)), dma((Z_FIRST,)), dma((2,)), dma((2,)), dma((count,)), dma((count,)),
+        ],
+        compiler_params=pltpu.CompilerParams(
+            collective_id=1, has_side_effects=True, vmem_limit_bytes=60 * 2 ** 20
+        ),
+    )(lt, rt, bg)
+
+
+def grads_by_scatter(lt, rt, bg, ff):
+    width = lt.shape[1]
+    parts = ff // width
+
+    def scatter(full):
+        return lax.psum_scatter(
+            full.astype(BF), ("seq", "dp"), scatter_dimension=0, tiled=True
+        ).astype(F32)
+
+    left_f = lt[:parts].reshape(parts, 4, 4, width // 16, -1).transpose(1, 2, 0, 3, 4)
+    down = scatter(dot_nn(left_f.reshape(ff, -1), rt[R_Z]))
+    up = scatter(jnp.concatenate([dot_nn(lt[L_N], rt[R_U + j]) for j in range(parts)], axis=1))
+    wout = scatter(dot_nn(lt[L_O], rt[R_A]))
+    qkv = scatter(jnp.concatenate([dot_nn(lt[L_X], rt[R_P + j]) for j in range(3)], axis=1))
+    return qkv, wout, up, down, lax.psum(bg, ("seq", "dp"))
+
+
 def local(*args):
-    (sout, sgrad, xs, os_, n1s, fs, dps, das, dus, dzs, bg) = run_layers(args, None)
-    width = xs.shape[1]
+    sout, sgrad, lt, rt, bg = run_layers(args, None)
+    width = lt.shape[1]
+    ff = args[7].shape[2]
     index = lax.axis_index("seq") * lax.axis_size("dp") + lax.axis_index("dp")
     count = lax.axis_size("seq") * lax.axis_size("dp")
-
-    def weight_grad(a, b):
-        full = dot_tn(a, b).astype(BF)
-        return lax.psum_scatter(full, ("seq", "dp"), scatter_dimension=0, tiled=True).astype(F32)
-
-    sums = lax.psum(bg.reshape(12 * width), ("seq", "dp"))
+    if lax.axis_size("dp") == 4:
+        out, sums = run_grads(lt, rt, bg)
+        down = out[0:4].reshape(-1, width)
+        up = jnp.concatenate([out[4], out[5], out[6], out[7]], axis=1)
+        wout = out[8]
+        qkv = jnp.concatenate([out[9], out[10], out[11]], axis=1)
+    else:
+        qkv, wout, up, down, sums = grads_by_scatter(lt, rt, bg, ff)
+    sums = sums.reshape(-1)
 
     def piece(start, rows):
         part = sums[start * width:(start + rows) * width]
@@ -442,13 +756,13 @@
     return (
         sout[None],
         sgrad.astype(F32)[None],
-        weight_grad(xs, dps)[None],
+        qkv[None],
         piece(0, 2),
-        weight_grad(os_, das)[None],
+        wout[None],
         piece(2, 2),
-        weight_grad(n1s, dus)[None],
+        up[None],
         piece(4, 4),
-        weight_grad(fs, dzs)[None],
+        down[None],
         piece(8, 2),
         piece(10, 2),
     )

time: 431 us -> 233 us (0.54)
  waiting for transfers between devices: 197 us -> 0 us
  Pallas kernels: 124 us -> 222 us
  blocking collectives: 62 us -> 0 us
  matrix products: 18.2 us -> 0 us
  between operations: 13.8 us -> 0.71 us
  other arithmetic: 8.18 us -> 2.91 us
    reduce_scatter x4 -> x0, waiting for transfers between devices: 197 us -> none  [weight_grad(): lax.psum_scatter(full, ('seq', 'dp'), scatter_dimension=0, tiled=True)]
    pallas_call x0 -> x1, Pallas kernels: none -> 96.9 us  [run_grads(): pl.pallas_call(grads_kernel, name='grads', out_shape=(jax.ShapeDtypeStruc...]
    psum x1 -> x0, blocking collectives: 62 us -> none  [local(): sums = lax.psum(bg.reshape(12 * width), ('seq', 'dp'))]
    dot_general x4 -> x0, matrix products: 18.2 us -> none  [dot_tn(): lax.dot_general(a, b, (((0,), (0,)), ((), ())), preferred_element_type=F32)]
    broadcast_in_dim x4 -> x2, other arithmetic: 6.91 us -> 1.64 us  [the longest x1 0.85 us: local(): up[None]]
  transfers between devices with their start and end apart: 4 -> 0, of which waited for: 3 -> 0; matrix products, arithmetic and copies ran while one was open for 5% -> 0% of each run, Pallas kernels for 0% -> 0%
where the time goes in v2:
time: 233 us
  Pallas kernels  222 us (95%)
  local copies, waits for them, and re-layouts  6.94 us (3%)
  other arithmetic  2.91 us (1%)
    pallas_call x1, Pallas kernels, run_layers(): pl.pallas_call(layers_kernel, name='layers', out_shape=(jax.ShapeDtypeStr...  125 us
    pallas_call x1, Pallas kernels, run_grads(): pl.pallas_call(grads_kernel, name='grads', out_shape=(jax.ShapeDtypeStruc...  96.9 us

profile of v2, /device:TPU:0, one launch (start us, length us, event | category | flops | bytes accessed | tf_op | source)
XLA Modules:
  0.0 232.9 jit_solution(9915615817124529624)
XLA Ops:
  0.6 125.4 %layers.1 = (bf16[4,128,768]{2,1,0:T(8,128)(2,1)}, bf16[4,128,768]{2,1,0:T(8,128)(2,1)}, bf16[7,768,512]{2,1,0:T(8,128)(2,1)}, bf16[9,512,768]{2,1,0:T(8,128)(2,1)}, f32[12,1,768]{2,1,0:T(1,128)}) custom-call(s32[4]{0:T(128)} %len_ref.1, bf16[4,128,768]{2,1,0:T(8,128)(2,1)} %in_hbm.1, bf16[4,128,768]{2,1,0:T(8,128)(2,1)} %cot_hbm.1, ...), custom_call_target="tpu_custom_call" | custom-call | tf_op jit(solution)/shard_map/layers/pallas_call | solution.py:386
  126.1 96.9 %grads.1 = (f32[12,48,768]{2,1,0:T(8,128)}, f32[12,1,768]{2,1,0:T(1,128)}) custom-call(bf16[7,768,512]{2,1,0:T(8,128)(2,1)} %get-tuple-element.20.lt, bf16[9,512,768]{2,1,0:T(8,128)(2,1)} %get-tuple-element.21.rt, f32[12,1,768]{2,1,0:T(1,128)} %get-tuple-element.22.bg), custom_call_target="tpu_custom_call" | custom-call | tf_op jit(solution)/shard_map/grads/pallas_call | solution.py:686
  223.0 0.0 copy-start.2
  223.0 0.0 copy-start.1
  223.1 0.0 copy-start
  223.1 2.2 slice_bitcast_fusion.3
  225.2 0.9 maximum_bitcast_fusion
  226.1 0.8 maximum_bitcast_fusion.1
  226.9 0.0 copy-done.2
  226.9 0.1 slice_reduce_fusion
  227.0 0.6 dynamic-slice_bitcast_fusion
  227.6 0.6 dynamic-slice_bitcast_fusion.2
  228.2 0.6 dynamic_slice.17
  228.9 1.9 slice.71
  230.8 0.0 copy-done.1
  230.8 1.3 bitcast_convert_fusion
  232.0 0.0 copy-done
  232.1 0.9 copy.24
  (5 shorter events, 0.0 us)
Async XLA Ops:
  223.0 3.9 %copy-start.2 = (f32[12,1,768]{2,1,0:T(1,128)S(1)}, f32[12,1,768]{2,1,0:T(1,128)}, u32[]{:S(2)}) copy-start(f32[12,1,768]{2,1,0:T(1,128)} %get-tuple-element.24) | copy-start | bytes 110596
  223.0 7.7 %copy-start.1 = (bf16[4,128,768]{2,1,0:T(8,128)(2,1)S(1)}, bf16[4,128,768]{2,1,0:T(8,128)(2,1)}, u32[]{:S(2)}) copy-start(bf16[4,128,768]{2,1,0:T(8,128)(2,1)} %get-tuple-element.19) | copy-start | bytes 2359300
  223.1 9.0 %copy-start = (bf16[4,128,768]{2,1,0:T(8,128)(2,1)S(1)}, bf16[4,128,768]{2,1,0:T(8,128)(2,1)}, u32[]{:S(2)}) copy-start(bf16[4,128,768]{2,1,0:T(8,128)(2,1)} %get-tuple-element.18) | copy-start | bytes 2359300

commit v3 on v2

--- a/solution.py
+++ b/solution.py
@@ -50,6 +50,7 @@
     keys = 2 * rows
     hd = width // H
     pairs = H // 2
+    half_pairs = H // 4
     nff = ff // width
     dp_size = 4
     unit = width // 16
@@ -108,17 +109,17 @@
             device_id=x_dev, device_id_type=MESH,
         )
 
-    def kv_copy(m):
+    def kv_copy(m, part):
         return pltpu.make_async_remote_copy(
-            src_ref=kv.at[m, pl.ds(0, rows)], dst_ref=kv.at[m, pl.ds(rows, rows)],
-            send_sem=kv_send.at[m], recv_sem=kv_rsem.at[m],
+            src_ref=kv.at[m, part, pl.ds(0, rows)], dst_ref=kv.at[m, part, pl.ds(rows, rows)],
+            send_sem=kv_send.at[m, part], recv_sem=kv_rsem.at[m, part],
             device_id=core_dev, device_id_type=MESH,
         )
 
-    def dkv_copy(m):
+    def dkv_copy(m, group):
         return pltpu.make_async_remote_copy(
-            src_ref=dkv_send.at[m], dst_ref=dkv_recv.at[m],
-            send_sem=dk_ssem.at[m], recv_sem=dk_rsem.at[m],
+            src_ref=dkv_send.at[m, group], dst_ref=dkv_recv.at[m, group],
+            send_sem=dk_ssem.at[m, group], recv_sem=dk_rsem.at[m, group],
             device_id=core_dev, device_id_type=MESH,
         )
 
@@ -195,11 +196,12 @@
             weight_copies[0].wait()
 
         x = ab[sec, r]
-        kv[m, pl.ds(0, rows), 0:width] = dot_nn(x, wqkv[:, width:2 * width]).astype(BF)
-        kv[m, pl.ds(0, rows), width:2 * width] = (
+        kv[m, 0, pl.ds(0, rows)] = dot_nn(x, wqkv[:, width:2 * width]).astype(BF)
+        kv_copy(m, 0).start()
+        kv[m, 1, pl.ds(0, rows)] = (
             dot_nn(x, wqkv[:, 2 * width:3 * width]) + vec(abias_ref, 1)
         ).astype(BF)
-        kv_copy(m).start()
+        kv_copy(m, 1).start()
         queries = (dot_nn(x, wqkv[:, 0:width]) + vec(abias_ref, 0)).astype(BF)
         q_s[r] = queries * (hd ** -0.5)
 
@@ -208,25 +210,26 @@
             for copy in weight_copies[1:]:
                 copy.wait()
 
-        kv_copy(m).wait_recv()
+        lt[L_X, :, r] = x.T
+        kv_copy(m, 0).wait_recv()
+        kv_copy(m, 1).wait_recv()
         key_bias = jnp.where(positions((keys, 1)) < len_ref[2 * hi + m], 0.0, -1e30)
 
         def head_pair(p, carry):
             cols = pl.ds(pl.multiple_of(p * LANES, LANES), LANES)
-            vcols = pl.ds(pl.multiple_of(width + p * LANES, LANES), LANES)
             qq = split_heads(q_s[r, cols])
-            st = dot_nt(kv[m, :, cols], qq) + key_bias
+            st = dot_nt(kv[m, 0, :, cols], qq) + key_bias
             top = jnp.max(st, axis=0, keepdims=True)
             e = jnp.exp(st - top)
             total = jnp.sum(e, axis=0, keepdims=True)
             lse[m, p] = top + jnp.log(total)
-            o_t = dot_tn(kv[m, :, vcols], e.astype(BF)) * (1.0 / total)
+            o_t = dot_tn(kv[m, 1, :, cols], e.astype(BF)) * (1.0 / total)
             o_pair = jnp.concatenate([o_t[0:hd, 0:rows], o_t[hd:2 * hd, rows:2 * rows]], axis=0)
             lt[L_O, cols, r] = o_pair.astype(BF)
             o_s[:, cols] = o_pair.T.astype(BF)
             return carry
 
-        lax.fori_loop(0, pairs, head_pair, 0)
+        lax.fori_loop(0, pairs, head_pair, 0, unroll=True)
 
         r1 = x.astype(F32) + dot_nn(o_s[...], wout[...]) + vec(obias_ref, 0)
         hat, scale, n1 = norm(r1, vec(gain_ref, 0), vec(shift_ref, 0))
@@ -250,7 +253,7 @@
             acc[...] += dot_nn(f, wdown[cols, :])
             return carry
 
-        lax.fori_loop(0, nff, ff_chunk, 0)
+        lax.fori_loop(0, nff, ff_chunk, 0, unroll=True)
         hat, scale, result = norm(acc[...], vec(gain_ref, 1), vec(shift_ref, 1))
         xh2[r] = hat
         rs2[r] = jnp.broadcast_to(scale, (rows, LANES))
@@ -262,7 +265,6 @@
 
         for copy in out_copies(0, yb, sout_hbm, m):
             copy.start()
-        lt[L_X, :, r] = ab[sec, r].T
         lt[L_N, :, r] = n_s[...].T
 
     def backward(step, m):
@@ -289,7 +291,7 @@
             acc[...] += dot_nt(du, wup[:, cols])
             return carry
 
-        lax.fori_loop(0, nff, ff_chunk, 0)
+        lax.fori_loop(0, nff, ff_chunk, 0, unroll=True)
         dn1 = acc[...]
         hat = xh1[r]
         add_bias_grad(8, dn1 * hat)
@@ -302,39 +304,45 @@
         do_s[...] = dot_nt(da, wout[...]).astype(BF)
         key_bias = jnp.where(positions((keys, 1)) < length, 0.0, -1e30)
 
-        def head_pair(p, carry):
-            cols = pl.ds(pl.multiple_of(p * LANES, LANES), LANES)
-            vcols = pl.ds(pl.multiple_of(width + p * LANES, LANES), LANES)
+        def head_pair(group, index):
+            p = group * half_pairs + index
+            cols = pl.ds(p * LANES, LANES)
+            kcols = pl.ds(index * LANES, LANES)
+            vcols = pl.ds((half_pairs + index) * LANES, LANES)
             qq = split_heads(q_s[r, cols])
             dd = split_heads(do_s[:, cols])
-            kp = kv[m, :, cols]
+            kp = kv[m, 0, :, cols]
             pt = jnp.exp(dot_nt(kp, qq) + key_bias - lse[m, p])
             dv = dot_nn(pt.astype(BF), dd)
-            dpt = dot_nt(kv[m, :, vcols], dd)
+            dpt = dot_nt(kv[m, 1, :, cols], dd)
             inner = jnp.sum(pt * dpt, axis=0, keepdims=True)
             ds = (pt * (dpt - inner)).astype(BF)
             dk = dot_nn(ds, qq)
             dq_t = dot_tn(kp, ds)
             dq_pair = jnp.concatenate([dq_t[0:hd, 0:rows], dq_t[hd:2 * hd, rows:2 * rows]], axis=0)
             rt[R_P, r, cols] = (dq_pair.T * (hd ** -0.5)).astype(BF)
-            dkv_own[:, cols] = dk[0:rows]
-            dkv_own[:, vcols] = dv[0:rows]
-            dkv_send[m, :, cols] = dk[rows:keys].astype(BF)
-            dkv_send[m, :, vcols] = dv[rows:keys].astype(BF)
-            return carry
-
-        lax.fori_loop(0, pairs, head_pair, 0)
-        dkv_copy(m).start()
+            dkv_own[group, :, kcols] = dk[0:rows]
+            dkv_own[group, :, vcols] = dv[0:rows]
+            dkv_send[m, group, :, kcols] = dk[rows:keys].astype(BF)
+            dkv_send[m, group, :, vcols] = dv[rows:keys].astype(BF)
+
+        for group in range(2):
+            for index in range(half_pairs):
+                head_pair(group, index)
+            dkv_copy(m, group).start()
         dq = rt[R_P, r]
         add_bias_grad(0, dq.astype(F32))
-        dr1[...] += dot_nt(dq, wqkv[:, 0:width])
-        dkv_copy(m).wait_recv()
-        dk = (dkv_own[:, 0:width] + dkv_recv[m, :, 0:width].astype(F32)).astype(BF)
-        dv = (dkv_own[:, width:2 * width] + dkv_recv[m, :, width:2 * width].astype(F32)).astype(BF)
-        rt[R_P + 1, r] = dk
-        rt[R_P + 2, r] = dv
-        add_bias_grad(1, dv.astype(F32))
-        dx = dr1[...] + dot_nt(dk, wqkv[:, width:2 * width]) + dot_nt(dv, wqkv[:, 2 * width:3 * width])
+        dx = dr1[...] + dot_nt(dq, wqkv[:, 0:width])
+        part = width // 2
+        for group in range(2):
+            dkv_copy(m, group).wait_recv()
+            both = (dkv_own[group] + dkv_recv[m, group].astype(F32)).astype(BF)
+            for which in range(2):
+                at = (1 + which) * width + group * part
+                piece = both[:, which * part:(which + 1) * part]
+                rt[R_P + 1 + which, r, group * part:(group + 1) * part] = piece
+                dx = dx + dot_nt(piece, wqkv[:, at:at + part])
+        add_bias_grad(1, rt[R_P + 2, r].astype(F32))
         gb[r] = dx.astype(BF)
 
         @pl.when(sec == 1)
@@ -363,8 +371,9 @@
     for m in range(MICRO):
         y_copy(in_hbm, m).wait_send()
         hop_copy(yb, m).wait_send()
-        kv_copy(m).wait_send()
-        dkv_copy(m).wait_send()
+        for part in range(2):
+            kv_copy(m, part).wait_send()
+            dkv_copy(m, part).wait_send()
         for kind, src, dst in ((0, yb, sout_hbm), (1, gb, sgrad_hbm)):
             local_out, remote_out = out_copies(kind, src, dst, m)
             local_out.wait()
@@ -402,7 +411,7 @@
             pltpu.VMEM((width, ff), BF),
             pltpu.VMEM((ff, width), BF),
             pltpu.VMEM((total, width), BF),
-            pltpu.VMEM((MICRO, keys, 2 * width), BF),
+            pltpu.VMEM((MICRO, 2, keys, width), BF),
             pltpu.VMEM((MICRO, H // 2, 1, 2 * rows), F32),
             pltpu.VMEM((rows, width), BF),
             pltpu.VMEM((rows, width), BF),
@@ -414,13 +423,13 @@
             pltpu.VMEM((rows, width), F32),
             pltpu.VMEM((rows, width), F32),
             pltpu.VMEM((rows, width), BF),
-            pltpu.VMEM((rows, 2 * width), F32),
-            pltpu.VMEM((MICRO, rows, 2 * width), BF),
-            pltpu.VMEM((MICRO, rows, 2 * width), BF),
+            pltpu.VMEM((2, rows, width), F32),
+            pltpu.VMEM((MICRO, 2, rows, width), BF),
+            pltpu.VMEM((MICRO, 2, rows, width), BF),
             pltpu.VMEM((total, width), BF),
             pltpu.VMEM((total, width), BF),
             dma((4,)), dma((MICRO,)), dma((MICRO,)), dma((MICRO,)), dma((MICRO,)), dma((MICRO,)),
-            dma((MICRO,)), dma((MICRO,)), dma((MICRO,)), dma((MICRO,)),
+            dma((MICRO, 2)), dma((MICRO, 2)), dma((MICRO, 2)), dma((MICRO, 2)),
             dma((2, MICRO)), dma((2, MICRO)), dma((2, MICRO)),
         ],
         compiler_params=pltpu.CompilerParams(
@@ -732,6 +741,75 @@
     return qkv, wout, up, down, lax.psum(bg, ("seq", "dp"))
 
 
+def finish_kernel(
+    sout, sgrad, grads, sums,
+    sout_ref, sgrad_ref, qkv_ref, abias_ref, wout_ref, obias_ref, up_ref, bup_ref, down_ref,
+    gain_ref, shift_ref, sem,
+):
+    copy = pltpu.make_async_copy(sout, sout_ref.at[0], sem)
+    copy.start()
+    width = grads.shape[2]
+    unit = grads.shape[1]
+    size = abias_ref.shape[1]
+    index = lax.axis_index("seq") * lax.axis_size("dp") + lax.axis_index("dp")
+    for k in range(CHUNKS):
+        if k < 4:
+            down_ref[0, k * unit:(k + 1) * unit, :] = grads[k]
+        elif k < 8:
+            up_ref[0, :, (k - 4) * width:(k - 3) * width] = grads[k]
+        elif k == 8:
+            wout_ref[0] = grads[k]
+        else:
+            qkv_ref[0, :, (k - 9) * width:(k - 8) * width] = grads[k]
+    sgrad_ref[0] = sgrad[...].astype(F32)
+    whole = width // size
+    low = index < whole
+    pairs = [jnp.where(low, sums[row], sums[row + 1]) for row in (0, 2, 8, 10)]
+    block = jnp.concatenate(pairs + pairs, axis=0)
+    block = pltpu.roll(block, (width - (index % whole) * size) % width, axis=1)
+    for row, ref in enumerate((abias_ref, obias_ref, gain_ref, shift_ref)):
+        ref[...] = block[row:row + 1, 0:size]
+    wide = 2 * size
+    per = width // wide
+    rows = sums[4]
+    for row in range(1, 4):
+        rows = jnp.where(index // per == row, sums[4 + row], rows)
+    rows = pltpu.roll(
+        jnp.concatenate([rows] * 8, axis=0), (width - (index % per) * wide) % width, axis=1
+    )
+    bup_ref[...] = rows[0:1, 0:wide]
+    copy.wait()
+
+
+def run_finish(sout, sgrad, grads, sums):
+    unit, width = grads.shape[1:]
+    size = width // 8
+    vmem = pl.BlockSpec(memory_space=pltpu.VMEM)
+    any_spec = pl.BlockSpec(memory_space=pl.ANY)
+    shape = jax.ShapeDtypeStruct
+    return pl.pallas_call(
+        finish_kernel,
+        name="finish",
+        out_shape=(
+            shape((1,) + sout.shape, BF),
+            shape((1,) + sgrad.shape, F32),
+            shape((1, unit, 3 * width), F32),
+            shape((1, size), F32),
+            shape((1, unit, width), F32),
+            shape((1, size), F32),
+            shape((1, unit, 4 * width), F32),
+            shape((1, 2 * size), F32),
+            shape((1, 4 * unit, width), F32),
+            shape((1, size), F32),
+            shape((1, size), F32),
+        ),
+        in_specs=[any_spec] + [vmem] * 3,
+        out_specs=(any_spec,) + (vmem,) * 10,
+        scratch_shapes=[pltpu.SemaphoreType.DMA],
+        compiler_params=pltpu.CompilerParams(vmem_limit_bytes=32 * 2 ** 20),
+    )(sout, sgrad, grads, sums)
+
+
 def local(*args):
     sout, sgrad, lt, rt, bg = run_layers(args, None)
     width = lt.shape[1]
@@ -740,12 +818,8 @@
     count = lax.axis_size("seq") * lax.axis_size("dp")
     if lax.axis_size("dp") == 4:
         out, sums = run_grads(lt, rt, bg)
-        down = out[0:4].reshape(-1, width)
-        up = jnp.concatenate([out[4], out[5], out[6], out[7]], axis=1)
-        wout = out[8]
-        qkv = jnp.concatenate([out[9], out[10], out[11]], axis=1)
-    else:
-        qkv, wout, up, down, sums = grads_by_scatter(lt, rt, bg, ff)
+        return run_finish(sout, sgrad, out, sums)
+    qkv, wout, up, down, sums = grads_by_scatter(lt, rt, bg, ff)
     sums = sums.reshape(-1)
 
     def piece(start, rows):

time: 233 us -> 208 us (0.89)
  Pallas kernels: 222 us -> 205 us
  local copies, waits for them, and re-layouts: 6.94 us -> 2.25 us
  other arithmetic: 2.91 us -> 0 us
    pallas_call x1, Pallas kernels: 125 us -> 105 us  [run_layers(): pl.pallas_call(layers_kernel, name='layers', out_shape=(jax.ShapeDtypeStr...]
    broadcast_in_dim x3 -> x0, other arithmetic: 2.91 us -> none  [the longest x1 1.27 us: local(): sgrad.astype(F32)[None]]
    pallas_call x0 -> x1, Pallas kernels: none -> 2.63 us  [run_finish(): pl.pallas_call(finish_kernel, name='finish', out_shape=(shape((1,) + sout...]
where the time goes in v3:
time: 208 us
  Pallas kernels  205 us (99%)
  local copies, waits for them, and re-layouts  2.25 us (1%)
    pallas_call x1, Pallas kernels, run_layers(): pl.pallas_call(layers_kernel, name='layers', out_shape=(jax.ShapeDtypeStr...  105 us
    pallas_call x1, Pallas kernels, run_grads(): pl.pallas_call(grads_kernel, name='grads', out_shape=(jax.ShapeDtypeStruc...  97 us

profile of v3, /device:TPU:0, one launch (start us, length us, event | category | flops | bytes accessed | tf_op | source)
XLA Modules:
  0.0 208.1 jit_solution(2702951123953214260)
XLA Ops:
  0.6 105.3 %layers.1 = (bf16[4,128,768]{2,1,0:T(8,128)(2,1)}, bf16[4,128,768]{2,1,0:T(8,128)(2,1)}, bf16[7,768,512]{2,1,0:T(8,128)(2,1)}, bf16[9,512,768]{2,1,0:T(8,128)(2,1)}, f32[12,1,768]{2,1,0:T(1,128)}) custom-call(s32[4]{0:T(128)} %len_ref.1, bf16[4,128,768]{2,1,0:T(8,128)(2,1)} %in_hbm.1, bf16[4,128,768]{2,1,0:T(8,128)(2,1)} %cot_hbm.1, ...), custom_call_target="tpu_custom_call" | custom-call | tf_op jit(solution)/shard_map/layers/pallas_call | solution.py:395
  106.0 0.0 copy-start.1
  106.0 0.0 copy-start.2
  106.0 97.0 %grads.1 = (f32[12,48,768]{2,1,0:T(8,128)}, f32[12,1,768]{2,1,0:T(1,128)}) custom-call(bf16[7,768,512]{2,1,0:T(8,128)(2,1)} %get-tuple-element.20.lt, bf16[9,512,768]{2,1,0:T(8,128)(2,1)} %get-tuple-element.21.rt, f32[12,1,768]{2,1,0:T(1,128)} %get-tuple-element.22.bg), custom_call_target="tpu_custom_call" | custom-call | tf_op jit(solution)/shard_map/grads/pallas_call | solution.py:695
  203.0 0.0 copy-done.1
  203.0 0.0 copy-done.2
  203.0 0.0 copy-start
  203.0 1.5 copy-done
  204.5 0.0 copy-start.3
  204.5 0.8 copy-done.3
  205.3 2.6 %finish.1 = (bf16[1,4,128,768]{3,2,1,0:T(8,128)(2,1)}, f32[1,4,128,768]{3,2,1,0:T(8,128)}, f32[1,48,2304]{2,1,0:T(8,128)}, f32[1,96]{1,0:T(1,128)}, f32[1,48,768...) custom-call(bf16[4,128,768]{2,1,0:T(8,128)(2,1)S(1)} %copy-done.1, ...), custom_call_target="tpu_custom_call" | custom-call | tf_op jit(solution)/shard_map/finish/pallas_call | solution.py:790
Async XLA Ops:
  106.0 97.0 %copy-start.1 = (bf16[4,128,768]{2,1,0:T(8,128)(2,1)S(1)}, bf16[4,128,768]{2,1,0:T(8,128)(2,1)}, u32[]{:S(2)}) copy-start(bf16[4,128,768]{2,1,0:T(8,128)(2,1)} %get-tuple-element.18.sout) | copy-start | bytes 2359300
  106.0 97.0 %copy-start.2 = (bf16[4,128,768]{2,1,0:T(8,128)(2,1)S(1)}, bf16[4,128,768]{2,1,0:T(8,128)(2,1)}, u32[]{:S(2)}) copy-start(bf16[4,128,768]{2,1,0:T(8,128)(2,1)} %get-tuple-element.19.sgrad) | copy-start | bytes 2359300
  203.0 1.5 copy-start
  204.5 0.8 copy-start.3

commit v4 on v1

v4 whole, which is shorter than its diff:
```python
import functools

import jax
import jax.numpy as jnp
from jax import lax
from jax.experimental import pallas as pl
from jax.experimental.pallas import tpu as pltpu
from jax.sharding import PartitionSpec as P

H = 12
MICRO = 2
EPS = 1e-12
MESH = pl.DeviceIdType.MESH
BF = jnp.bfloat16
F32 = jnp.float32
LANES = 128
INV_SQRT_2PI = 0.3989422804014327
INV_SQRT_2 = 0.7071067811865476
L_F, L_N, L_O, L_X, L_COUNT = 0, 4, 5, 6, 7
R_P, R_A, R_U, R_Z, R_COUNT = 0, 3, 4, 8, 9
CHUNKS = 12
Z_FIRST = (1, 3)
EARLY = 6
DEDICATED = 6
Y_SLOTS = 8
STEPS = 20
VMEM_LIMIT = 63 * 2 ** 20


def dot_nn(a, b):
    return lax.dot_general(a, b, (((1,), (0,)), ((), ())), preferred_element_type=F32)


def dot_nt(a, b):
    return lax.dot_general(a, b, (((1,), (1,)), ((), ())), preferred_element_type=F32)


def dot_tn(a, b):
    return lax.dot_general(a, b, (((0,), (0,)), ((), ())), preferred_element_type=F32)


def train_kernel(with_sums, *refs):
    refs = iter(refs)

    def take(number):
        return [next(refs) for _ in range(number)]

    (len_ref, in_hbm, cot_hbm, wqkv_hbm, wout_hbm, wup_hbm, wdown_hbm,
     abias_ref, obias_ref, bup_ref, gain_ref, shift_ref) = take(12)
    sout_hbm, sgrad_hbm = take(2)
    if with_sums:
        out, bg_out = take(2)
    else:
        lt, rt, bg = take(3)
    (ab, wqkv, wout, pool, wdown, q_s, kv, lse, o_s, n_s, xh1, xh2, rs1, rs2, dr1, acc, do_s,
     dkv_own, dkv_send, dkv_recv, yb) = take(21)
    (w_sem, loc_sem, ex_send, ex_recv, hop_send, hop_recv, kv_ss, kv_rs, dk_ss, dk_rs,
     out_loc, out_ss, out_rs) = take(13)
    if with_sums:
        (lt, rt, bg, core_src, y_buf, up, down, turn_src, turn_buf,
         b_src, b_core, b_y, b_z) = take(13)
        (core_ss, core_rs, y_ss, y_rs, up_ss, up_rs, down_ss, down_rs, turn_ss, turn_rs,
         bc_ss, bc_rs, bz_ss, bz_rs) = take(14)

    width = wqkv.shape[0]
    ff = wdown.shape[0]
    span = in_hbm.shape[1]
    rows = 2 * span
    keys = 2 * rows
    hd = width // H
    pairs = H // 2
    half_pairs = H // 4
    nff = ff // width
    quarter = 4
    unit = width // 16
    sec = lax.axis_index("section")
    seq = lax.axis_index("seq")
    z = lax.axis_index("dp")
    count = lax.axis_size("dp")
    hi = seq // 2
    lo = seq % 2
    core_dev = (sec, hi * 2 + 1 - lo, z)
    y_dev = (sec, (1 - hi) * 2 + lo, z)
    x_dev = (1 - sec, seq, z)

    def z_dev(index):
        return (sec, seq, index)

    def remote(src, dst, send, recv, dev):
        return pltpu.make_async_remote_copy(
            src_ref=src, dst_ref=dst, send_sem=send, recv_sem=recv,
            device_id=dev, device_id_type=MESH,
        )

    weight_copies = [
        pltpu.make_async_copy(src.at[0], dst, w_sem.at[i])
        for i, (src, dst) in enumerate(((wqkv_hbm, wqkv), (wout_hbm, wout), (wdown_hbm, wdown)))
    ]
    tall = width // 4
    for j in range(nff):
        for part in range(4):
            weight_copies.append(
                pltpu.make_async_copy(
                    wup_hbm.at[0, pl.ds(part * tall, tall), pl.ds(j * width, width)],
                    pool.at[j * 4 + part],
                    w_sem.at[3 + j * 4 + part],
                )
            )
    for copy in weight_copies:
        copy.start()

    partners = [core_dev, y_dev, x_dev]
    if with_sums:
        partners += [z_dev((z + by) % count) for by in range(1, count)]
    barrier = pltpu.get_barrier_semaphore()
    for dev in partners:
        pl.semaphore_signal(barrier, inc=1, device_id=dev, device_id_type=MESH)
    pl.semaphore_wait(barrier, len(partners))

    def mrows(m):
        return pl.ds(pl.multiple_of(m * rows, rows), rows)

    def own_copy(src, m):
        return pltpu.make_async_copy(
            src.at[2 * hi + m], ab.at[0, pl.ds(m * rows, span)], loc_sem.at[m]
        )

    def seq_copy(src, m):
        return remote(
            src.at[2 * (1 - hi) + m], ab.at[0, pl.ds(m * rows + span, span)],
            ex_send.at[m], ex_recv.at[m], y_dev,
        )

    for is_sec, src in ((0, in_hbm), (1, cot_hbm)):
        @pl.when(sec == is_sec)
        def _(src=src):
            for m in range(MICRO):
                seq_copy(src, m).start()
                own_copy(src, m).start()

    bg[...] = jnp.zeros_like(bg)

    def hop_copy(src, m):
        return remote(src.at[mrows(m)], ab.at[1, mrows(m)], hop_send.at[m], hop_recv.at[m], x_dev)

    def kv_copy(m, part):
        return remote(
            kv.at[m, part, pl.ds(0, rows)], kv.at[m, part, pl.ds(rows, rows)],
            kv_ss.at[m, part], kv_rs.at[m, part], core_dev,
        )

    def dkv_copy(m, group):
        return remote(
            dkv_send.at[group], dkv_recv.at[m, group],
            dk_ss.at[m, group], dk_rs.at[m, group], core_dev,
        )

    def out_copies(kind, src, dst, m):
        table = 2 * hi + m
        base = m * rows
        return (
            pltpu.make_async_copy(src.at[pl.ds(base, span)], dst.at[table], out_loc.at[kind, m]),
            remote(
                src.at[pl.ds(base + span, span)], dst.at[table],
                out_ss.at[kind, m], out_rs.at[kind, m], y_dev,
            ),
        )

    def wait_slot(which, m):
        @pl.when(which == 0)
        def _():
            own_copy(in_hbm, m).wait()
            seq_copy(in_hbm, m).wait_recv()

        @pl.when(which == 1)
        def _():
            hop_copy(yb, m).wait_recv()

    def positions(shape, dim):
        row = lax.broadcasted_iota(jnp.int32, shape, dim)
        block = row // span
        within = row % span
        half = jnp.where(block % 2 == 0, hi, 1 - hi)
        core = jnp.where(block < 2, lo, 1 - lo)
        return (half * 2 + core) * span + within

    def left_lanes():
        return lax.broadcasted_iota(jnp.int32, (1, LANES), 1) < hd

    def split_heads(value):
        left = left_lanes().astype(F32)
        return jnp.concatenate([value * left.astype(BF), value * (1.0 - left).astype(BF)], axis=0)

    def norm(resid, gain, shift):
        average = jnp.mean(resid, axis=-1, keepdims=True)
        centred = resid - average
        spread = jnp.mean(centred * centred, axis=-1, keepdims=True)
        scale = lax.rsqrt(spread + EPS)
        hat = centred * scale
        return hat, scale, hat * gain + shift

    def norm_back(grad, hat, scale, gain):
        dh = grad * gain
        return scale * (
            dh
            - jnp.mean(dh, axis=-1, keepdims=True)
            - hat * jnp.mean(dh * hat, axis=-1, keepdims=True)
        )

    def wup(j):
        return pool[4 * j:4 * j + 4].reshape(width, width)

    def vec(ref, part):
        return ref[0:1, part * width:(part + 1) * width].astype(F32)

    def add_bias_grad(row, value):
        bg[row] += jnp.sum(value, axis=0, keepdims=True)


    def project(step, m):
        r = mrows(m)
        wait_slot(sec, m)

        @pl.when(step == 0)
        def _():
            weight_copies[0].wait()

        x = ab[sec, r]
        kv[m, 0, pl.ds(0, rows)] = dot_nn(x, wqkv[:, width:2 * width]).astype(BF)
        kv_copy(m, 0).start()
        kv[m, 1, pl.ds(0, rows)] = (
            dot_nn(x, wqkv[:, 2 * width:3 * width]) + vec(abias_ref, 1)
        ).astype(BF)
        kv_copy(m, 1).start()
        queries = (dot_nn(x, wqkv[:, 0:width]) + vec(abias_ref, 0)).astype(BF)
        q_s[r] = queries * (hd ** -0.5)
        lt[L_X, :, r] = x.T

        @pl.when(step == 0)
        def _():
            for copy in weight_copies[1:]:
                copy.wait()

    def forward(m):
        r = mrows(m)
        kv_copy(m, 0).wait_recv()
        kv_copy(m, 1).wait_recv()
        key_bias = jnp.where(positions((1, keys), 1) < len_ref[2 * hi + m], 0.0, -1e30)
        lane = lax.broadcasted_iota(jnp.int32, (1, LANES), 1)
        stats = jnp.zeros((keys, LANES), F32)
        for p in range(pairs):
            cols = pl.ds(p * LANES, LANES)
            scores = dot_nt(split_heads(q_s[r, cols]), kv[m, 0, :, cols]) + key_bias
            top = jnp.max(scores, axis=1, keepdims=True)
            e = jnp.exp(scores - top)
            total = jnp.sum(e, axis=1, keepdims=True)
            stats = jnp.where(lane == p, top + jnp.log(total), stats)
            o = dot_nn(e.astype(BF), kv[m, 1, :, cols]) * (1.0 / total)
            o_s[r, cols] = jnp.where(left_lanes(), o[0:rows], o[rows:2 * rows]).astype(BF)
        lse[m] = stats.T[0:8]

        r1 = ab[sec, r].astype(F32) + dot_nn(o_s[r], wout[...]) + vec(obias_ref, 0)
        hat, scale, n1 = norm(r1, vec(gain_ref, 0), vec(shift_ref, 0))
        xh1[r] = hat.astype(BF)
        rs1[r] = jnp.broadcast_to(scale, (rows, LANES))
        n_s[...] = n1.astype(BF)
        acc[...] = n1 + vec(obias_ref, 1)
        for j in range(nff):
            cols = pl.ds(j * width, width)
            u = dot_nn(n_s[...], wup(j)) + bup_ref[0:1, cols].astype(F32)
            phi = 0.5 + 0.5 * lax.erf(u * INV_SQRT_2)
            f = (u * phi).astype(BF)
            f_t = f.T
            for owner in range(quarter):
                for part in range(nff):
                    at = (owner * nff + part) * unit
                    lt[part, pl.ds((j * quarter + owner) * unit, unit), r] = f_t[at:at + unit]
            rt[R_U + j, r] = (phi + u * (jnp.exp(-0.5 * u * u) * INV_SQRT_2PI)).astype(BF)
            acc[...] += dot_nn(f, wdown[cols, :])
        hat, scale, result = norm(acc[...], vec(gain_ref, 1), vec(shift_ref, 1))
        xh2[r] = hat.astype(BF)
        rs2[r] = jnp.broadcast_to(scale, (rows, LANES))
        yb[r] = result.astype(BF)

        @pl.when(sec == 0)
        def _():
            hop_copy(yb, m).start()

        for copy in out_copies(0, yb, sout_hbm, m):
            copy.start()
        lt[L_N, :, r] = n_s[...].T
        lt[L_O, :, r] = o_s[r].T

    def backward(m, serve):
        r = mrows(m)
        wait_slot(1 - sec, m)
        length = len_ref[2 * hi + m]
        row_scale = jnp.where((sec == 0) | (positions((rows, 1), 0) < length), 1.0, 0.0)
        dy = ab[1 - sec, r].astype(F32) * row_scale
        hat = xh2[r].astype(F32)
        add_bias_grad(9, dy * hat)
        add_bias_grad(11, dy)
        dr2 = norm_back(dy, hat, rs2[r, 0:1], vec(gain_ref, 1))
        dz = dr2.astype(BF)
        rt[R_Z, r] = dz
        add_bias_grad(3, dz.astype(F32))
        acc[...] = dr2
        serve(0, 3)
        for j in range(nff):
            cols = pl.ds(j * width, width)
            du = (dot_nt(rt[R_Z, r], wdown[cols, :]) * rt[R_U + j, r].astype(F32)).astype(BF)
            rt[R_U + j, r] = du
            bg[4 + j] += jnp.sum(du.astype(F32), axis=0, keepdims=True)
            acc[...] += dot_nt(du, wup(j))
        serve(3, 4)
        dn1 = acc[...]
        hat = xh1[r].astype(F32)
        add_bias_grad(8, dn1 * hat)
        add_bias_grad(10, dn1)
        grad1 = norm_back(dn1, hat, rs1[r, 0:1], vec(gain_ref, 0))
        dr1[...] = grad1
        da = grad1.astype(BF)
        rt[R_A, r] = da
        add_bias_grad(2, da.astype(F32))
        do_s[...] = dot_nt(da, wout[...]).astype(BF)
        serve(4, 5)
        key_bias = jnp.where(positions((keys, 1), 0) < length, 0.0, -1e30)

        def head_pair(group, index):
            p = group * half_pairs + index
            cols = pl.ds(p * LANES, LANES)
            kcols = pl.ds(index * LANES, LANES)
            vcols = pl.ds((half_pairs + index) * LANES, LANES)
            qq = split_heads(q_s[r, cols])
            dd = split_heads(do_s[:, cols])
            kp = kv[m, 0, :, cols]
            pt = jnp.exp(dot_nt(kp, qq) + key_bias - lse[m, p:p + 1])
            dv = dot_nn(pt.astype(BF), dd)
            dpt = dot_nt(kv[m, 1, :, cols], dd)
            sums = jnp.sum(pt * dpt, axis=0, keepdims=True)
            ds = (pt * (dpt - sums)).astype(BF)
            dk = dot_nn(ds, qq)
            dq_t = dot_tn(kp, ds)
            dq_pair = jnp.concatenate([dq_t[0:hd, 0:rows], dq_t[hd:2 * hd, rows:2 * rows]], axis=0)
            rt[R_P, r, cols] = (dq_pair.T * (hd ** -0.5)).astype(BF)
            dkv_own[group, :, kcols] = dk[0:rows]
            dkv_own[group, :, vcols] = dv[0:rows]
            dkv_send[group, :, kcols] = dk[rows:keys].astype(BF)
            dkv_send[group, :, vcols] = dv[rows:keys].astype(BF)

        for group in range(2):
            for index in range(half_pairs):
                head_pair(group, index)
            dkv_copy(m, group).start()
            if group == 0:
                serve(5, EARLY)
        dq = rt[R_P, r]
        add_bias_grad(0, dq.astype(F32))
        dr1[...] += dot_nt(dq, wqkv[:, 0:width])

    def input_grad(m):
        r = mrows(m)
        dx = dr1[...]
        part = width // 2
        for group in range(2):
            dkv_copy(m, group).wait_recv()
            both = (dkv_own[group] + dkv_recv[m, group].astype(F32)).astype(BF)
            for which in range(2):
                at = (1 + which) * width + group * part
                piece = both[:, which * part:(which + 1) * part]
                rt[R_P + 1 + which, r, group * part:(group + 1) * part] = piece
                dx = dx + dot_nt(piece, wqkv[:, at:at + part])
        local_out, remote_out = out_copies(0, yb, sout_hbm, m)
        local_out.wait()
        remote_out.wait_send()

        @pl.when(sec == 0)
        def _():
            hop_copy(yb, m).wait_send()

        yb[r] = dx.astype(BF)

        @pl.when(sec == 1)
        def _():
            hop_copy(yb, m).start()

        for copy in out_copies(1, yb, sgrad_hbm, m):
            copy.start()
        for group in range(2):
            dkv_copy(m, group).wait_send()
        add_bias_grad(1, rt[R_P + 2, r].astype(F32))


    if with_sums:
        block = count * unit

        def slot_of(k, half):
            blocks = ff // tall
            return jnp.where(k < DEDICATED, blocks + 2 * k, 2 * (k - DEDICATED)) + half

        def core_copy(k, half):
            return remote(
                core_src.at[k % 2, half], pool.at[slot_of(k, half)],
                core_ss.at[k, half], core_rs.at[k, half], core_dev,
            )

        def y_copy(k):
            return remote(
                pool.at[slot_of(k, 1 - hi)], y_buf.at[k % Y_SLOTS], y_ss.at[k], y_rs.at[k], y_dev
            )

        def turn_copy(k):
            i = k // 2
            return remote(turn_src.at[i], turn_buf.at[i], turn_ss.at[i], turn_rs.at[i], y_dev)

        def piece(k, half, target):
            return pool.at[slot_of(k, half), pl.ds(pl.multiple_of(target * unit, unit), unit)]

        def up_copy(job, k, half, target):
            i = target - 1
            return remote(
                piece(k, half, target), up.at[job, i], up_ss.at[job, i], up_rs.at[job, i],
                z_dev(jnp.minimum(z + 1, count - 1)),
            )

        def down_copy(job, k, half, target):
            return remote(
                piece(k, half, target), down.at[job, target], down_ss.at[job, target],
                down_rs.at[job, target], z_dev(jnp.maximum(z - 1, 0)),
            )

        def add_piece(k, half, target, landed):
            ref = piece(k, half, target)
            ref[...] = (ref[...].astype(F32) + landed[...].astype(F32)).astype(BF)

        def hop(number, job, k, half):
            @pl.when(z == number - 1)
            def _():
                for target in range(count - 1, number - 1, -1):
                    if number > 1:
                        up_copy(job, k, half, target).wait_recv()
                        add_piece(k, half, target, up.at[job, target - 1])
                    up_copy(job, k, half, target).start()

            @pl.when(z == count - number)
            def _():
                for target in range(0, count - number):
                    if number > 1:
                        down_copy(job, k, half, target).wait_recv()
                        add_piece(k, half, target, down.at[job, target])
                    down_copy(job, k, half, target).start()

        def arrive(job, k, half):
            out[k] = piece(k, half, z)[...].astype(F32)

            @pl.when(z > 0)
            def _():
                up_copy(job, k, half, z).wait_recv()
                out[k] += up[job, jnp.maximum(z - 1, 0)].astype(F32)

            @pl.when(z < count - 1)
            def _():
                down_copy(job, k, half, z).wait_recv()
                out[k] += down[job, jnp.minimum(z, count - 2)].astype(F32)

        def along_z_first(k):
            return (k == Z_FIRST[0]) | (k == Z_FIRST[1])

        def jobs_of(k):
            return ((k, hi), (CHUNKS + k // 2, 1 - hi))

        def product(k, half):
            left = jnp.where(k < 8, jnp.minimum(k, L_N), jnp.where(k == 8, L_O, L_X))
            right = jnp.where(k < 4, R_Z, jnp.where(k < 8, k, jnp.where(k == 8, R_A, k - 9)))
            base = pl.multiple_of(half * block, block)
            return dot_nn(lt[left, pl.ds(base, block), :], rt[right])

        def for_core(k):
            @pl.when(k >= 2)
            def _():
                for half in range(2):
                    core_copy(k - 2, half).wait_send()

            for half in range(2):
                core_src[k % 2, half] = product(k, half * 2 + 1 - lo).astype(BF)
                core_copy(k, half).start()

        def chip_sum(k):
            for half in range(2):
                core_copy(k, half).wait_recv()
                slot = slot_of(k, half)
                pool[slot] = (product(k, half * 2 + lo) + pool[slot].astype(F32)).astype(BF)

            @pl.when(along_z_first(k))
            def _():
                for job, half in jobs_of(k):
                    hop(1, job, k, half)

            @pl.when(jnp.logical_not(along_z_first(k)))
            def _():
                y_copy(k).start()

        def bias_core():
            return remote(b_src.at[0], b_core, bc_ss.at[0], bc_rs.at[0], core_dev)

        def bias_y():
            return remote(b_src.at[1], b_y, bc_ss.at[1], bc_rs.at[1], y_dev)

        def bias_z(by):
            return remote(
                b_src.at[2], b_z.at[by - 1], bz_ss.at[by - 1], bz_rs.at[by - 1],
                z_dev((z + by) % count),
            )

        def sum_step(t):
            @pl.when(t < CHUNKS)
            def _():
                for_core(t)

            @pl.when((t >= 1) & (t <= CHUNKS))
            def _():
                chip_sum(t - 1)

            def y_first_at(lag, action):
                k = t - lag

                @pl.when((k >= 0) & (k < CHUNKS) & jnp.logical_not(along_z_first(k)))
                def _():
                    action(k)

            def z_first_at(lag, action):
                k = t - lag

                @pl.when(along_z_first(k))
                def _():
                    action(k)

            def from_y(k):
                y_copy(k).wait_recv()
                slot = slot_of(k, hi)
                pool[slot] = (pool[slot].astype(F32) + y_buf[k % Y_SLOTS].astype(F32)).astype(BF)
                hop(1, k, k, hi)

            y_first_at(4, from_y)
            for number in range(2, count):
                y_first_at(3 + number, lambda k, number=number: hop(number, k, k, hi))

                def both_halves(k, number=number):
                    for job, half in jobs_of(k):
                        hop(number, job, k, half)

                z_first_at(1 + 2 * number, both_halves)

            def turn(k):
                stays, goes = jobs_of(k)
                arrive(goes[0], k, goes[1])
                turn_src[k // 2] = out[k].astype(BF)
                turn_copy(k).start()
                arrive(stays[0], k, stays[1])

            def turned(k):
                turn_copy(k).wait_recv()
                out[k] += turn_buf[k // 2].astype(F32)

            y_first_at(4 + count, lambda k: arrive(k, k, hi))
            z_first_at(1 + 2 * count, turn)
            z_first_at(3 + 2 * count, turned)

            @pl.when(t == 7)
            def _():
                b_src[0] = bg[...]
                bias_core().start()

            @pl.when(t == 9)
            def _():
                bias_core().wait_recv()
                b_src[1] = b_src[0] + b_core[...]
                bias_y().start()

            @pl.when(t == 11)
            def _():
                bias_y().wait_recv()
                b_src[2] = b_src[1] + b_y[...]
                for by in range(1, count):
                    bias_z(by).start()

    def one_step(step, carry):
        first = sec == 0

        def among(*steps):
            hit = step == steps[0]
            for value in steps[1:]:
                hit = hit | (step == value)
            return hit

        late_forward = ((step == 3) & first) | ((step == 4) & jnp.logical_not(first))
        early_backward = ((step == 4) & first) | ((step == 3) & jnp.logical_not(first))
        m = jnp.where(among(2, 6, 7) | late_forward, 1, 0)

        def serve(start, stop):
            if with_sums:
                @pl.when((step == 6) & first)
                def _():
                    def body(t, c):
                        sum_step(t)
                        return c

                    lax.fori_loop(start, stop, body, 0)

        @pl.when(among(0, 2))
        def _():
            project(step, m)

        @pl.when((step == 1) | late_forward)
        def _():
            forward(m)

        @pl.when((step == 6) | early_backward)
        def _():
            backward(m, serve)

        @pl.when(among(5, 7))
        def _():
            input_grad(m)

        return carry

    lax.fori_loop(0, 8, one_step, 0)

    if with_sums:
        def rest(t, carry):
            sum_step(t)
            return carry

        lax.fori_loop(jnp.where(sec == 0, EARLY, 0), STEPS, rest, 0)

        total = b_src[2]
        for by in range(1, count):
            bias_z(by).wait_recv()
            total = total + b_z[by - 1]
        bg_out[...] = total
        bias_core().wait_send()
        bias_y().wait_send()
        for by in range(1, count):
            bias_z(by).wait_send()

        def sent(job, k, half):
            for target in range(count):
                if target > 0:
                    @pl.when(target > z)
                    def _(target=target):
                        up_copy(job, k, half, target).wait_send()

                if target < count - 1:
                    @pl.when(target < z)
                    def _(target=target):
                        down_copy(job, k, half, target).wait_send()

        def drain(k, carry):
            @pl.when(k >= CHUNKS - 2)
            def _():
                for half in range(2):
                    core_copy(k, half).wait_send()

            sent(k, k, hi)

            @pl.when(along_z_first(k))
            def _():
                turn_copy(k).wait_send()
                sent(CHUNKS + k // 2, k, 1 - hi)

            @pl.when(jnp.logical_not(along_z_first(k)))
            def _():
                y_copy(k).wait_send()

            return carry

        lax.fori_loop(0, CHUNKS, drain, 0)

    for m in range(MICRO):
        seq_copy(in_hbm, m).wait_send()
        for part in range(2):
            kv_copy(m, part).wait_send()
        out_copies(0, yb, sout_hbm, m)[1].wait_recv()
        local_out, remote_out = out_copies(1, yb, sgrad_hbm, m)
        local_out.wait()
        remote_out.wait()

        @pl.when(sec == 1)
        def _():
            hop_copy(yb, m).wait_send()


def run_train(args, with_sums):
    (inputs, cotangent, lengths, w_qkv, attn_bias, w_out, out_bias, w_up, bias_up, w_down,
     norm_gain, norm_bias) = args
    tables, span, width = inputs.shape
    ff = w_up.shape[2]
    rows = 2 * span
    total = MICRO * rows
    keys = 2 * rows
    count = lax.axis_size("dp")
    unit = width // 16
    block = count * unit
    tall = width // 4
    jobs = CHUNKS + len(Z_FIRST)
    any_spec = pl.BlockSpec(memory_space=pl.ANY)
    vmem = pl.BlockSpec(memory_space=pltpu.VMEM)
    smem = pl.BlockSpec(memory_space=pltpu.SMEM)
    dma = pltpu.SemaphoreType.DMA
    shape = jax.ShapeDtypeStruct
    stacks = (
        ((L_COUNT, width, total), BF),
        ((R_COUNT, total, width), BF),
        ((12, 1, width), F32),
    )
    if with_sums:
        results = (((CHUNKS, unit, width), F32), ((12, 1, width), F32))
    else:
        results = stacks
    scratch = [
        pltpu.VMEM((2, total, width), BF),
        pltpu.VMEM((width, 3 * width), BF),
        pltpu.VMEM((width, width), BF),
        pltpu.VMEM((ff // tall + (2 * DEDICATED if with_sums else 0), tall, width), BF),
        pltpu.VMEM((ff, width), BF),
        pltpu.VMEM((total, width), BF),
        pltpu.VMEM((MICRO, 2, keys, width), BF),
        pltpu.VMEM((MICRO, 8, keys), F32),
        pltpu.VMEM((total, width), BF),
        pltpu.VMEM((rows, width), BF),
        pltpu.VMEM((total, width), BF),
        pltpu.VMEM((total, width), BF),
        pltpu.VMEM((total, LANES), F32),
        pltpu.VMEM((total, LANES), F32),
        pltpu.VMEM((rows, width), F32),
        pltpu.VMEM((rows, width), F32),
        pltpu.VMEM((rows, width), BF),
        pltpu.VMEM((2, rows, width), F32),
        pltpu.VMEM((2, rows, width), BF),
        pltpu.VMEM((MICRO, 2, rows, width), BF),
        pltpu.VMEM((total, width), BF),
        dma((3 + 4 * (ff // width),)), dma((MICRO,)), dma((MICRO,)), dma((MICRO,)), dma((MICRO,)), dma((MICRO,)),
        dma((MICRO, 2)), dma((MICRO, 2)), dma((MICRO, 2)), dma((MICRO, 2)),
        dma((2, MICRO)), dma((2, MICRO)), dma((2, MICRO)),
    ]
    if with_sums:
        scratch += [pltpu.VMEM(dims, kind) for dims, kind in stacks]
        scratch += [
            pltpu.VMEM((2, 2, block, width), BF),
            pltpu.VMEM((Y_SLOTS, block, width), BF),
            pltpu.VMEM((jobs, count - 1, unit, width), BF),
            pltpu.VMEM((jobs, count - 1, unit, width), BF),
            pltpu.VMEM((len(Z_FIRST), unit, width), BF),
            pltpu.VMEM((len(Z_FIRST), unit, width), BF),
            pltpu.VMEM((3, 12, 1, width), F32),
            pltpu.VMEM((12, 1, width), F32),
            pltpu.VMEM((12, 1, width), F32),
            pltpu.VMEM((count - 1, 12, 1, width), F32),
            dma((CHUNKS, 2)), dma((CHUNKS, 2)), dma((CHUNKS,)), dma((CHUNKS,)),
            dma((jobs, count - 1)), dma((jobs, count - 1)),
            dma((jobs, count - 1)), dma((jobs, count - 1)),
            dma((len(Z_FIRST),)), dma((len(Z_FIRST),)), dma((2,)), dma((2,)),
            dma((count - 1,)), dma((count - 1,)),
        ]
    return pl.pallas_call(
        functools.partial(train_kernel, with_sums),
        name="train",
        out_shape=(shape((tables, span, width), BF), shape((tables, span, width), BF))
        + tuple(shape(dims, kind) for dims, kind in results),
        in_specs=[smem] + [any_spec] * 6 + [vmem] * 5,
        out_specs=(any_spec, any_spec) + (vmem,) * len(results),
        scratch_shapes=scratch,
        compiler_params=pltpu.CompilerParams(
            collective_id=0, has_side_effects=True, vmem_limit_bytes=VMEM_LIMIT
        ),
    )(lengths, inputs, cotangent, w_qkv, w_out, w_up, w_down,
      attn_bias, out_bias, bias_up, norm_gain, norm_bias)


def grads_by_scatter(lt, rt, bg, ff):
    width = lt.shape[1]
    parts = ff // width

    def scatter(full):
        return lax.psum_scatter(
            full.astype(BF), ("seq", "dp"), scatter_dimension=0, tiled=True
        ).astype(F32)

    left_f = lt[:parts].reshape(parts, 4, 4, width // 16, -1).transpose(1, 2, 0, 3, 4)
    down = scatter(dot_nn(left_f.reshape(ff, -1), rt[R_Z]))
    up = scatter(jnp.concatenate([dot_nn(lt[L_N], rt[R_U + j]) for j in range(parts)], axis=1))
    wout = scatter(dot_nn(lt[L_O], rt[R_A]))
    qkv = scatter(jnp.concatenate([dot_nn(lt[L_X], rt[R_P + j]) for j in range(3)], axis=1))
    return qkv, wout, up, down, lax.psum(bg, ("seq", "dp"))


def finish_kernel(
    sout, sgrad, grads, sums,
    sout_ref, sgrad_ref, qkv_ref, abias_ref, wout_ref, obias_ref, up_ref, bup_ref, down_ref,
    gain_ref, shift_ref, sem,
):
    copy = pltpu.make_async_copy(sout, sout_ref.at[0], sem)
    copy.start()
    width = grads.shape[2]
    unit = grads.shape[1]
    size = abias_ref.shape[1]
    index = lax.axis_index("seq") * lax.axis_size("dp") + lax.axis_index("dp")
    for k in range(CHUNKS):
        if k < 4:
            down_ref[0, k * unit:(k + 1) * unit, :] = grads[k]
        elif k < 8:
            up_ref[0, :, (k - 4) * width:(k - 3) * width] = grads[k]
        elif k == 8:
            wout_ref[0] = grads[k]
        else:
            qkv_ref[0, :, (k - 9) * width:(k - 8) * width] = grads[k]
    sgrad_ref[0] = sgrad[...].astype(F32)
    whole = width // size
    low = index < whole
    pairs = [jnp.where(low, sums[row], sums[row + 1]) for row in (0, 2, 8, 10)]
    block = jnp.concatenate(pairs + pairs, axis=0)
    block = pltpu.roll(block, (width - (index % whole) * size) % width, axis=1)
    for row, ref in enumerate((abias_ref, obias_ref, gain_ref, shift_ref)):
        ref[...] = block[row:row + 1, 0:size]
    wide = 2 * size
    per = width // wide
    rows = sums[4]
    for row in range(1, 4):
        rows = jnp.where(index // per == row, sums[4 + row], rows)
    rows = pltpu.roll(
        jnp.concatenate([rows] * 8, axis=0), (width - (index % per) * wide) % width, axis=1
    )
    bup_ref[...] = rows[0:1, 0:wide]
    copy.wait()


def run_finish(sout, sgrad, grads, sums):
    unit, width = grads.shape[1:]
    size = width // 8
    vmem = pl.BlockSpec(memory_space=pltpu.VMEM)
    any_spec = pl.BlockSpec(memory_space=pl.ANY)
    shape = jax.ShapeDtypeStruct
    return pl.pallas_call(
        finish_kernel,
        name="finish",
        out_shape=(
            shape((1,) + sout.shape, BF),
            shape((1,) + sgrad.shape, F32),
            shape((1, unit, 3 * width), F32),
            shape((1, size), F32),
            shape((1, unit, width), F32),
            shape((1, size), F32),
            shape((1, unit, 4 * width), F32),
            shape((1, 2 * size), F32),
            shape((1, 4 * unit, width), F32),
            shape((1, size), F32),
            shape((1, size), F32),
        ),
        in_specs=[any_spec] + [vmem] * 3,
        out_specs=(any_spec,) + (vmem,) * 10,
        scratch_shapes=[pltpu.SemaphoreType.DMA],
        compiler_params=pltpu.CompilerParams(vmem_limit_bytes=32 * 2 ** 20),
    )(sout, sgrad, grads, sums)


def local(*args):
    if lax.axis_size("dp") == 4:
        sout, sgrad, out, sums = run_train(args, True)
        return run_finish(sout, sgrad, out, sums)
    sout, sgrad, lt, rt, bg = run_train(args, False)
    width = lt.shape[1]
    ff = args[7].shape[2]
    index = lax.axis_index("seq") * lax.axis_size("dp") + lax.axis_index("dp")
    count = lax.axis_size("seq") * lax.axis_size("dp")
    qkv, wout, up, down, sums = grads_by_scatter(lt, rt, bg, ff)
    sums = sums.reshape(-1)

    def piece(start, rows):
        part = sums[start * width:(start + rows) * width]
        size = rows * width // count
        return lax.dynamic_slice_in_dim(part, index * size, size, 0)[None]

    return (
        sout[None],
        sgrad.astype(F32)[None],
        qkv[None],
        piece(0, 2),
        wout[None],
        piece(2, 2),
        up[None],
        piece(4, 4),
        down[None],
        piece(8, 2),
        piece(10, 2),
    )


def solution(mesh):
    return jax.shard_map(
        local,
        mesh=mesh,
        in_specs=(
            P("dp", "seq", None),
            P("dp", "seq", None),
            P("dp"),
            P("section", None, None),
            P("section", None),
            P("section", None, None),
            P("section", None),
            P("section", None, None),
            P("section", None),
            P("section", None, None),
            P("section", None),
            P("section", None),
        ),
        out_specs=(
            P("section", "dp", "seq", None),
            P("section", "dp", "seq", None),
            P("section", ("seq", "dp"), None),
            P("section", ("seq", "dp")),
            P("section", ("seq", "dp"), None),
            P("section", ("seq", "dp")),
            P("section", ("seq", "dp"), None),
            P("section", ("seq", "dp")),
            P("section", ("seq", "dp"), None),
            P("section", ("seq", "dp")),
            P("section", ("seq", "dp")),
        ),
        check_vma=False,
    )
```

time: 431 us -> 194 us (0.45)
  waiting for transfers between devices: 197 us -> 0 us
  Pallas kernels: 124 us -> 189 us
  blocking collectives: 62 us -> 0 us
  matrix products: 18.2 us -> 0 us
  between operations: 13.8 us -> 0.83 us
  other arithmetic: 8.18 us -> 0 us
    reduce_scatter x4 -> x0, waiting for transfers between devices: 197 us -> none  [weight_grad(): lax.psum_scatter(full, ('seq', 'dp'), scatter_dimension=0, tiled=True)]
    pallas_call x1 -> x2, Pallas kernels: 124 us -> 189 us  [the longest x1 186 us: run_train(): pl.pallas_call(functools.partial(train_kernel, with_sums), name='train',...]
    psum x1 -> x0, blocking collectives: 62 us -> none  [local(): sums = lax.psum(bg.reshape(12 * width), ('seq', 'dp'))]
    dot_general x4 -> x0, matrix products: 18.2 us -> none  [dot_tn(): lax.dot_general(a, b, (((0,), (0,)), ((), ())), preferred_element_type=F32)]
    broadcast_in_dim x5 -> x0, other arithmetic: 8.18 us -> none  [the longest x1 1.81 us: local(): weight_grad(n1s, dus)[None]]
  transfers between devices with their start and end apart: 4 -> 0, of which waited for: 3 -> 0; matrix products, arithmetic and copies ran while one was open for 5% -> 0% of each run, Pallas kernels for 0% -> 0%
where the time goes in v4:
time: 194 us
  Pallas kernels  189 us (97%)
  local copies, waits for them, and re-layouts  4.5 us (2%)
    pallas_call x1, Pallas kernels, run_train(): pl.pallas_call(functools.partial(train_kernel, with_sums), name='train',...  186 us
    unnamed x8, local copies, waits for them, and re-layouts  4.5 us

profile of v4, /device:TPU:0, one launch (start us, length us, event | category | flops | bytes accessed | tf_op | source)
XLA Modules:
  0.0 194.1 jit_solution(12226853542733535772)
XLA Ops:
  0.6 186.1 %train.1 = (bf16[4,128,768]{2,1,0:T(8,128)(2,1)}, bf16[4,128,768]{2,1,0:T(8,128)(2,1)}, f32[12,48,768]{2,1,0:T(8,128)}, f32[12,1,768]{2,1,0:T(1,128)}) custom-call(s32[4]{0:T(128)} %refs_0_.1, bf16[4,128,768]{2,1,0:T(8,128)(2,1)} %refs_1_.1, bf16[4,128,768]{2,1,0:T(8,128)(2,1)} %refs_2_.1, bf16[1,768,2304]{2,1,0:T(8,128)(2,1)} %refs_3_.1, ...), custom_call_target="tpu_custom_call" | custom-call | tf_op jit(solution)/shard_map/train/pallas_call | solution.py:766
  186.8 0.0 copy-start
  186.8 1.5 copy-done
  188.3 0.0 copy-start.1
  188.3 1.1 copy-done.1
  189.4 0.0 copy-start.2
  189.4 1.1 copy-done.2
  190.5 0.0 copy-start.3
  190.5 0.8 copy-done.3
  191.3 2.6 %finish.1 = (bf16[1,4,128,768]{3,2,1,0:T(8,128)(2,1)}, f32[1,4,128,768]{3,2,1,0:T(8,128)}, f32[1,48,2304]{2,1,0:T(8,128)}, f32[1,96]{1,0:T(1,128)}, f32[1,48,768...) custom-call(bf16[4,128,768]{2,1,0:T(8,128)(2,1)S(1)} %copy-done.1, ...), custom_call_target="tpu_custom_call" | custom-call | tf_op jit(solution)/shard_map/finish/pallas_call | solution.py:844
Async XLA Ops:
  186.8 1.5 copy-start
  188.3 1.1 copy-start.1
  189.4 1.1 copy-start.2
  190.5 0.8 copy-start.3

commit v5 on v4

--- a/solution.py
+++ b/solution.py
@@ -19,11 +19,11 @@
 L_F, L_N, L_O, L_X, L_COUNT = 0, 4, 5, 6, 7
 R_P, R_A, R_U, R_Z, R_COUNT = 0, 3, 4, 8, 9
 CHUNKS = 12
-Z_FIRST = (1, 3)
+Z_FIRST = (1, 5)
 EARLY = 6
 DEDICATED = 6
-Y_SLOTS = 8
-STEPS = 20
+Y_SLOTS = 10
+STEPS = 19
 VMEM_LIMIT = 63 * 2 ** 20
 
 
@@ -49,7 +49,7 @@
      abias_ref, obias_ref, bup_ref, gain_ref, shift_ref) = take(12)
     sout_hbm, sgrad_hbm = take(2)
     if with_sums:
-        out, bg_out = take(2)
+        out_hbm, bg_out = take(2)
     else:
         lt, rt, bg = take(3)
     (ab, wqkv, wout, pool, wdown, q_s, kv, lse, o_s, n_s, xh1, xh2, rs1, rs2, dr1, acc, do_s,
@@ -57,10 +57,10 @@
     (w_sem, loc_sem, ex_send, ex_recv, hop_send, hop_recv, kv_ss, kv_rs, dk_ss, dk_rs,
      out_loc, out_ss, out_rs) = take(13)
     if with_sums:
-        (lt, rt, bg, core_src, y_buf, up, down, turn_src, turn_buf,
-         b_src, b_core, b_y, b_z) = take(13)
+        (lt, rt, bg, out, core_src, y_buf, up, down, turn_src, turn_buf,
+         b_src, b_core, b_y, b_z) = take(14)
         (core_ss, core_rs, y_ss, y_rs, up_ss, up_rs, down_ss, down_rs, turn_ss, turn_rs,
-         bc_ss, bc_rs, bz_ss, bz_rs) = take(14)
+         bc_ss, bc_rs, bz_ss, bz_rs, part_sem) = take(15)
 
     width = wqkv.shape[0]
     ff = wdown.shape[0]
@@ -384,11 +384,17 @@
         def _():
             hop_copy(yb, m).start()
 
-        for copy in out_copies(1, yb, sgrad_hbm, m):
-            copy.start()
+        @pl.when(m == 0)
+        def _():
+            send_input_grad(m)
+
         for group in range(2):
             dkv_copy(m, group).wait_send()
         add_bias_grad(1, rt[R_P + 2, r].astype(F32))
+
+    def send_input_grad(m):
+        for copy in out_copies(1, yb, sgrad_hbm, m):
+            copy.start()
 
 
     if with_sums:
@@ -404,13 +410,22 @@
                 core_ss.at[k, half], core_rs.at[k, half], core_dev,
             )
 
-        def y_copy(k):
-            return remote(
-                pool.at[slot_of(k, 1 - hi)], y_buf.at[k % Y_SLOTS], y_ss.at[k], y_rs.at[k], y_dev
+        def y_copy(k, i):
+            target = jnp.where(z < count // 2, count - 1 - i, i)
+            rows_of = pl.ds(pl.multiple_of(target * unit, unit), unit)
+            return target, remote(
+                pool.at[slot_of(k, 1 - hi), rows_of], y_buf.at[k % Y_SLOTS, i],
+                y_ss.at[k, i], y_rs.at[k, i], y_dev,
             )
 
+        def turn_index(k):
+            index = 0
+            for i in range(1, len(Z_FIRST)):
+                index = jnp.where(k == Z_FIRST[i], i, index)
+            return index
+
         def turn_copy(k):
-            i = k // 2
+            i = turn_index(k)
             return remote(turn_src.at[i], turn_buf.at[i], turn_ss.at[i], turn_rs.at[i], y_dev)
 
         def piece(k, half, target):
@@ -464,10 +479,13 @@
                 out[k] += down[job, jnp.minimum(z, count - 2)].astype(F32)
 
         def along_z_first(k):
-            return (k == Z_FIRST[0]) | (k == Z_FIRST[1])
+            hit = k == Z_FIRST[0]
+            for other in Z_FIRST[1:]:
+                hit = hit | (k == other)
+            return hit
 
         def jobs_of(k):
-            return ((k, hi), (CHUNKS + k // 2, 1 - hi))
+            return ((k, hi), (CHUNKS + turn_index(k), 1 - hi))
 
         def product(k, half):
             left = jnp.where(k < 8, jnp.minimum(k, L_N), jnp.where(k == 8, L_O, L_X))
@@ -498,7 +516,11 @@
 
             @pl.when(jnp.logical_not(along_z_first(k)))
             def _():
-                y_copy(k).start()
+                for i in range(count):
+                    y_copy(k, i)[1].start()
+
+        def part_copy(k):
+            return pltpu.make_async_copy(out.at[k], out_hbm.at[k], part_sem.at[k])
 
         def bias_core():
             return remote(b_src.at[0], b_core, bc_ss.at[0], bc_rs.at[0], core_dev)
@@ -536,35 +558,44 @@
                     action(k)
 
             def from_y(k):
-                y_copy(k).wait_recv()
-                slot = slot_of(k, hi)
-                pool[slot] = (pool[slot].astype(F32) + y_buf[k % Y_SLOTS].astype(F32)).astype(BF)
-                hop(1, k, k, hi)
+                for i in range(count):
+                    target, copy = y_copy(k, i)
+                    copy.wait_recv()
+                    add_piece(k, hi, target, y_buf.at[k % Y_SLOTS, i])
+                    if i < count - 1:
+                        @pl.when(z == 0)
+                        def _(target=count - 1 - i):
+                            up_copy(k, k, hi, target).start()
+
+                        @pl.when(z == count - 1)
+                        def _(target=i):
+                            down_copy(k, k, hi, target).start()
 
             y_first_at(4, from_y)
             for number in range(2, count):
-                y_first_at(3 + number, lambda k, number=number: hop(number, k, k, hi))
+                y_first_at(4 + number, lambda k, number=number: hop(number, k, k, hi))
 
                 def both_halves(k, number=number):
                     for job, half in jobs_of(k):
                         hop(number, job, k, half)
 
-                z_first_at(1 + 2 * number, both_halves)
+                z_first_at(2 + 2 * number, both_halves)
 
             def turn(k):
                 stays, goes = jobs_of(k)
                 arrive(goes[0], k, goes[1])
-                turn_src[k // 2] = out[k].astype(BF)
+                turn_src[turn_index(k)] = out[k].astype(BF)
                 turn_copy(k).start()
                 arrive(stays[0], k, stays[1])
 
-            def turned(k):
-                turn_copy(k).wait_recv()
-                out[k] += turn_buf[k // 2].astype(F32)
-
-            y_first_at(4 + count, lambda k: arrive(k, k, hi))
-            z_first_at(1 + 2 * count, turn)
-            z_first_at(3 + 2 * count, turned)
+            @pl.when(t == CHUNKS + 1)
+            def _():
+                send_input_grad(MICRO - 1)
+
+            for i, k in enumerate(Z_FIRST):
+                @pl.when(t == CHUNKS + 4 + i)
+                def _(k=k):
+                    turn(k)
 
             @pl.when(t == 7)
             def _():
@@ -627,12 +658,29 @@
 
     lax.fori_loop(0, 8, one_step, 0)
 
+    if not with_sums:
+        send_input_grad(MICRO - 1)
+
     if with_sums:
         def rest(t, carry):
             sum_step(t)
             return carry
 
         lax.fori_loop(jnp.where(sec == 0, EARLY, 0), STEPS, rest, 0)
+
+        def last_sum(k, carry):
+            @pl.when(jnp.logical_not(along_z_first(k)))
+            def _():
+                arrive(k, k, hi)
+                part_copy(k).start()
+
+            return carry
+
+        lax.fori_loop(0, CHUNKS, last_sum, 0)
+        for k in Z_FIRST:
+            turn_copy(k).wait_recv()
+            out[k] += turn_buf[turn_index(k)].astype(F32)
+            part_copy(k).start()
 
         total = b_src[2]
         for by in range(1, count):
@@ -657,6 +705,7 @@
                         down_copy(job, k, half, target).wait_send()
 
         def drain(k, carry):
+            part_copy(k).wait()
             @pl.when(k >= CHUNKS - 2)
             def _():
                 for half in range(2):
@@ -667,11 +716,12 @@
             @pl.when(along_z_first(k))
             def _():
                 turn_copy(k).wait_send()
-                sent(CHUNKS + k // 2, k, 1 - hi)
+                sent(CHUNKS + turn_index(k), k, 1 - hi)
 
             @pl.when(jnp.logical_not(along_z_first(k)))
             def _():
-                y_copy(k).wait_send()
+                for i in range(count):
+                    y_copy(k, i)[1].wait_send()
 
             return carry
 
@@ -747,8 +797,9 @@
     if with_sums:
         scratch += [pltpu.VMEM(dims, kind) for dims, kind in stacks]
         scratch += [
+            pltpu.VMEM((CHUNKS, unit, width), F32),
             pltpu.VMEM((2, 2, block, width), BF),
-            pltpu.VMEM((Y_SLOTS, block, width), BF),
+            pltpu.VMEM((Y_SLOTS, count, unit, width), BF),
             pltpu.VMEM((jobs, count - 1, unit, width), BF),
             pltpu.VMEM((jobs, count - 1, unit, width), BF),
             pltpu.VMEM((len(Z_FIRST), unit, width), BF),
@@ -757,11 +808,11 @@
             pltpu.VMEM((12, 1, width), F32),
             pltpu.VMEM((12, 1, width), F32),
             pltpu.VMEM((count - 1, 12, 1, width), F32),
-            dma((CHUNKS, 2)), dma((CHUNKS, 2)), dma((CHUNKS,)), dma((CHUNKS,)),
+            dma((CHUNKS, 2)), dma((CHUNKS, 2)), dma((CHUNKS, count)), dma((CHUNKS, count)),
             dma((jobs, count - 1)), dma((jobs, count - 1)),
             dma((jobs, count - 1)), dma((jobs, count - 1)),
             dma((len(Z_FIRST),)), dma((len(Z_FIRST),)), dma((2,)), dma((2,)),
-            dma((count - 1,)), dma((count - 1,)),
+            dma((count - 1,)), dma((count - 1,)), dma((CHUNKS,)),
         ]
     return pl.pallas_call(
         functools.partial(train_kernel, with_sums),
@@ -769,7 +820,8 @@
         out_shape=(shape((tables, span, width), BF), shape((tables, span, width), BF))
         + tuple(shape(dims, kind) for dims, kind in results),
         in_specs=[smem] + [any_spec] * 6 + [vmem] * 5,
-        out_specs=(any_spec, any_spec) + (vmem,) * len(results),
+        out_specs=(any_spec, any_spec)
+        + ((any_spec, vmem) if with_sums else (vmem,) * len(results)),
         scratch_shapes=scratch,
         compiler_params=pltpu.CompilerParams(
             collective_id=0, has_side_effects=True, vmem_limit_bytes=VMEM_LIMIT
@@ -796,29 +848,43 @@
 
 
 def finish_kernel(
-    sout, sgrad, grads, sums,
+    sout, sgrad, grads, sums_hbm,
     sout_ref, sgrad_ref, qkv_ref, abias_ref, wout_ref, obias_ref, up_ref, bup_ref, down_ref,
-    gain_ref, shift_ref, sem,
+    gain_ref, shift_ref,
+    kept, low, wide_grad, parts, sums, sem,
 ):
-    copy = pltpu.make_async_copy(sout, sout_ref.at[0], sem)
-    copy.start()
-    width = grads.shape[2]
-    unit = grads.shape[1]
+    unit, width = grads.shape[1:]
     size = abias_ref.shape[1]
-    index = lax.axis_index("seq") * lax.axis_size("dp") + lax.axis_index("dp")
+
+    def copy(i, src, dst):
+        started = pltpu.make_async_copy(src, dst, sem.at[i])
+        started.start()
+        return started
+
+    sums_in = copy(0, sums_hbm, sums)
+    grad_in = copy(1, sgrad, low)
+    out_in = copy(2, sout, kept)
+    parts_in = copy(3, grads, parts)
+    grad_in.wait()
+    wide_grad[...] = low[...].astype(F32)
+    copies = [copy(4, wide_grad, sgrad_ref.at[0])]
+    out_in.wait()
+    copies.append(copy(5, kept, sout_ref.at[0]))
+    parts_in.wait()
     for k in range(CHUNKS):
         if k < 4:
-            down_ref[0, k * unit:(k + 1) * unit, :] = grads[k]
+            dst = down_ref.at[0, pl.ds(k * unit, unit), :]
         elif k < 8:
-            up_ref[0, :, (k - 4) * width:(k - 3) * width] = grads[k]
+            dst = up_ref.at[0, :, pl.ds((k - 4) * width, width)]
         elif k == 8:
-            wout_ref[0] = grads[k]
+            dst = wout_ref.at[0]
         else:
-            qkv_ref[0, :, (k - 9) * width:(k - 8) * width] = grads[k]
-    sgrad_ref[0] = sgrad[...].astype(F32)
+            dst = qkv_ref.at[0, :, pl.ds((k - 9) * width, width)]
+        copies.append(copy(6 + k, parts.at[k], dst))
+    sums_in.wait()
+    index = lax.axis_index("seq") * lax.axis_size("dp") + lax.axis_index("dp")
     whole = width // size
-    low = index < whole
-    pairs = [jnp.where(low, sums[row], sums[row + 1]) for row in (0, 2, 8, 10)]
+    pairs = [jnp.where(index < whole, sums[row], sums[row + 1]) for row in (0, 2, 8, 10)]
     block = jnp.concatenate(pairs + pairs, axis=0)
     block = pltpu.roll(block, (width - (index % whole) * size) % width, axis=1)
     for row, ref in enumerate((abias_ref, obias_ref, gain_ref, shift_ref)):
@@ -832,7 +898,8 @@
         jnp.concatenate([rows] * 8, axis=0), (width - (index % per) * wide) % width, axis=1
     )
     bup_ref[...] = rows[0:1, 0:wide]
-    copy.wait()
+    for started in copies:
+        started.wait()
 
 
 def run_finish(sout, sgrad, grads, sums):
@@ -857,10 +924,18 @@
             shape((1, size), F32),
             shape((1, size), F32),
         ),
-        in_specs=[any_spec] + [vmem] * 3,
-        out_specs=(any_spec,) + (vmem,) * 10,
-        scratch_shapes=[pltpu.SemaphoreType.DMA],
-        compiler_params=pltpu.CompilerParams(vmem_limit_bytes=32 * 2 ** 20),
+        in_specs=[any_spec] * 4,
+        out_specs=(any_spec, any_spec, any_spec, vmem, any_spec, vmem, any_spec, vmem, any_spec,
+                   vmem, vmem),
+        scratch_shapes=[
+            pltpu.VMEM(sout.shape, BF),
+            pltpu.VMEM(sgrad.shape, BF),
+            pltpu.VMEM(sgrad.shape, F32),
+            pltpu.VMEM(grads.shape, F32),
+            pltpu.VMEM(sums.shape, F32),
+            pltpu.SemaphoreType.DMA((6 + CHUNKS,)),
+        ],
+        compiler_params=pltpu.CompilerParams(vmem_limit_bytes=VMEM_LIMIT),
     )(sout, sgrad, grads, sums)
 
 

time: 194 us -> 176 us (0.907)
  Pallas kernels: 189 us -> 175 us
  local copies, waits for them, and re-layouts: 4.5 us -> 0 us
    pallas_call x1, Pallas kernels: 186 us -> 171 us  [run_train(): pl.pallas_call(functools.partial(train_kernel, with_sums), name='train',...]
    unnamed x8 -> x0, local copies, waits for them, and re-layouts: 4.5 us -> none
where the time goes in v5:
time: 176 us
  Pallas kernels  175 us (99%)
    pallas_call x1, Pallas kernels, run_train(): pl.pallas_call(functools.partial(train_kernel, with_sums), name='train',...  171 us
    pallas_call x1, Pallas kernels, run_finish(): pl.pallas_call(finish_kernel, name='finish', out_shape=(shape((1,) + sout...  3.96 us

profile of v5, /device:TPU:0, one launch (start us, length us, event | category | flops | bytes accessed | tf_op | source)
XLA Modules:
  0.0 176.0 jit_solution(11555860351072836708)
XLA Ops:
  0.6 171.3 %train.1 = (bf16[4,128,768]{2,1,0:T(8,128)(2,1)}, bf16[4,128,768]{2,1,0:T(8,128)(2,1)}, f32[12,48,768]{2,1,0:T(8,128)}, f32[12,1,768]{2,1,0:T(1,128)}) custom-call(s32[4]{0:T(128)} %refs_0_.1, bf16[4,128,768]{2,1,0:T(8,128)(2,1)} %refs_1_.1, bf16[4,128,768]{2,1,0:T(8,128)(2,1)} %refs_2_.1, bf16[1,768,2304]{2,1,0:T(8,128)(2,1)} %refs_3_.1, ...), custom_call_target="tpu_custom_call" | custom-call | tf_op jit(solution)/shard_map/train/pallas_call | solution.py:817
  171.9 4.0 %finish.1 = (bf16[1,4,128,768]{3,2,1,0:T(8,128)(2,1)}, f32[1,4,128,768]{3,2,1,0:T(8,128)}, f32[1,48,2304]{2,1,0:T(8,128)}, f32[1,96]{1,0:T(1,128)}, f32[1,48,768...) custom-call(bf16[4,128,768]{2,1,0:T(8,128)(2,1)} %get-tuple-element., ...), custom_call_target="tpu_custom_call" | custom-call | tf_op jit(solution)/shard_map/finish/pallas_call | solution.py:911

commit v6 on v5

--- a/solution.py
+++ b/solution.py
@@ -19,11 +19,22 @@
 L_F, L_N, L_O, L_X, L_COUNT = 0, 4, 5, 6, 7
 R_P, R_A, R_U, R_Z, R_COUNT = 0, 3, 4, 8, 9
 CHUNKS = 12
-Z_FIRST = (1, 5)
-EARLY = 6
-DEDICATED = 6
-Y_SLOTS = 10
-STEPS = 19
+OUT = 8
+QKV = 9
+EARLY = 5
+FROM_Y = (
+    {5: 1, 8: 2, 11: 4, 13: 6, 15: 8, 16: 9, 17: 10, 19: 11},
+    {k + 4: k for k in range(1, CHUNKS)},
+)
+SECOND = (
+    {8: 3, 10: 1, 11: 5, 12: 7, 13: 2, 14: 4, 15: 6, 17: 8, 18: 9, 19: 10, 20: 11},
+    {k + 5: k for k in range(1, CHUNKS)},
+)
+THIRD = tuple(
+    {t + lag: k for t, k in table.items()} for lag, table in zip((2, 1), SECOND)
+)
+STEPS = 23
+LANDINGS = 5
 VMEM_LIMIT = 63 * 2 ** 20
 
 
@@ -57,10 +68,10 @@
     (w_sem, loc_sem, ex_send, ex_recv, hop_send, hop_recv, kv_ss, kv_rs, dk_ss, dk_rs,
      out_loc, out_ss, out_rs) = take(13)
     if with_sums:
-        (lt, rt, bg, out, core_src, y_buf, up, down, turn_src, turn_buf,
-         b_src, b_core, b_y, b_z) = take(14)
-        (core_ss, core_rs, y_ss, y_rs, up_ss, up_rs, down_ss, down_rs, turn_ss, turn_rs,
-         bc_ss, bc_rs, bz_ss, bz_rs, part_sem) = take(15)
+        (lt, rt, bg, out, lt_y, dz_y, core_src, y_buf, land, turn_src, turn_buf,
+         b_src, b_core, b_y, b_z) = take(15)
+        (core_ss, core_rs, y_ss, y_rs, z_ss, z_rs, turn_ss, turn_rs,
+         bc_ss, bc_rs, bz_ss, bz_rs, part_sem, lt_ss, lt_rs, dz_ss, dz_rs) = take(17)
 
     width = wqkv.shape[0]
     ff = wdown.shape[0]
@@ -103,7 +114,7 @@
                 pltpu.make_async_copy(
                     wup_hbm.at[0, pl.ds(part * tall, tall), pl.ds(j * width, width)],
                     pool.at[j * 4 + part],
-                    w_sem.at[3 + j * 4 + part],
+                    w_sem.at[3],
                 )
             )
     for copy in weight_copies:
@@ -134,8 +145,8 @@
     for is_sec, src in ((0, in_hbm), (1, cot_hbm)):
         @pl.when(sec == is_sec)
         def _(src=src):
+            seq_copy(src, 0).start()
             for m in range(MICRO):
-                seq_copy(src, m).start()
                 own_copy(src, m).start()
 
     bg[...] = jnp.zeros_like(bg)
@@ -172,6 +183,11 @@
             own_copy(in_hbm, m).wait()
             seq_copy(in_hbm, m).wait_recv()
 
+            for is_sec, src in ((0, in_hbm), (1, cot_hbm)):
+                @pl.when((m == 0) & (sec == is_sec))
+                def _(src=src):
+                    seq_copy(src, 1).start()
+
         @pl.when(which == 1)
         def _():
             hop_copy(yb, m).wait_recv()
@@ -215,6 +231,16 @@
 
     def add_bias_grad(row, value):
         bg[row] += jnp.sum(value, axis=0, keepdims=True)
+
+    def left_copy(m):
+        tall_half = 2 * tall
+        return remote(
+            lt.at[pl.ds(L_F, nff), pl.ds((1 - hi) * tall_half, tall_half), mrows(m)],
+            lt_y.at[:, :, mrows(m)], lt_ss.at[m], lt_rs.at[m], y_dev,
+        )
+
+    def right_copy(m):
+        return remote(rt.at[R_Z, mrows(m)], dz_y.at[mrows(m)], dz_ss.at[m], dz_rs.at[m], y_dev)
 
 
     def project(step, m):
@@ -238,8 +264,10 @@
 
         @pl.when(step == 0)
         def _():
-            for copy in weight_copies[1:]:
+            for copy in weight_copies[1:3]:
                 copy.wait()
+            whole = pool.at[pl.ds(0, 4 * nff)]
+            pltpu.make_async_copy(whole, whole, w_sem.at[3]).wait()
 
     def forward(m):
         r = mrows(m)
@@ -288,6 +316,11 @@
 
         for copy in out_copies(0, yb, sout_hbm, m):
             copy.start()
+        if with_sums:
+            @pl.when(sec == 0)
+            def _():
+                left_copy(m).start()
+
         lt[L_N, :, r] = n_s[...].T
         lt[L_O, :, r] = o_s[r].T
 
@@ -303,16 +336,21 @@
         dr2 = norm_back(dy, hat, rs2[r, 0:1], vec(gain_ref, 1))
         dz = dr2.astype(BF)
         rt[R_Z, r] = dz
+        if with_sums:
+            @pl.when(sec == 0)
+            def _():
+                right_copy(m).start()
+
         add_bias_grad(3, dz.astype(F32))
         acc[...] = dr2
-        serve(0, 3)
+        serve(0, 1)
         for j in range(nff):
             cols = pl.ds(j * width, width)
             du = (dot_nt(rt[R_Z, r], wdown[cols, :]) * rt[R_U + j, r].astype(F32)).astype(BF)
             rt[R_U + j, r] = du
             bg[4 + j] += jnp.sum(du.astype(F32), axis=0, keepdims=True)
             acc[...] += dot_nt(du, wup(j))
-        serve(3, 4)
+        serve(1, 3)
         dn1 = acc[...]
         hat = xh1[r].astype(F32)
         add_bias_grad(8, dn1 * hat)
@@ -323,7 +361,6 @@
         rt[R_A, r] = da
         add_bias_grad(2, da.astype(F32))
         do_s[...] = dot_nt(da, wout[...]).astype(BF)
-        serve(4, 5)
         key_bias = jnp.where(positions((keys, 1), 0) < length, 0.0, -1e30)
 
         def head_pair(group, index):
@@ -353,7 +390,7 @@
                 head_pair(group, index)
             dkv_copy(m, group).start()
             if group == 0:
-                serve(5, EARLY)
+                serve(3, EARLY)
         dq = rt[R_P, r]
         add_bias_grad(0, dq.astype(F32))
         dr1[...] += dot_nt(dq, wqkv[:, 0:width])
@@ -399,34 +436,33 @@
 
     if with_sums:
         block = count * unit
+        two = 2 * unit
+
+        def of_down(k):
+            return (k == 0) | ((k % 2 == 1) & (k >= 3) & (k < OUT))
+
+        def is_down(k):
+            return (sec == 0) & of_down(k) & (k > 0)
 
         def slot_of(k, half):
-            blocks = ff // tall
-            return jnp.where(k < DEDICATED, blocks + 2 * k, 2 * (k - DEDICATED)) + half
-
-        def core_copy(k, half):
+            return jnp.where(k < 4, 4 * nff + 2 * k, 2 * k - 8) + half
+
+        def core_copy(k, i, half):
             return remote(
-                core_src.at[k % 2, half], pool.at[slot_of(k, half)],
-                core_ss.at[k, half], core_rs.at[k, half], core_dev,
+                core_src.at[k % 2, i], pool.at[slot_of(k, half)],
+                core_ss.at[k % 2, i], core_rs.at[k % 4, i], core_dev,
             )
 
         def y_copy(k, i):
-            target = jnp.where(z < count // 2, count - 1 - i, i)
-            rows_of = pl.ds(pl.multiple_of(target * unit, unit), unit)
-            return target, remote(
-                pool.at[slot_of(k, 1 - hi), rows_of], y_buf.at[k % Y_SLOTS, i],
-                y_ss.at[k, i], y_rs.at[k, i], y_dev,
+            rows_of = pl.ds(pl.multiple_of(jnp.where(z < count // 2, 1 - i, i) * two, two), two)
+            slot = k - 1
+            return rows_of, y_buf.at[slot, i], remote(
+                pool.at[slot_of(k, 1 - hi), rows_of], y_buf.at[slot, i],
+                y_ss.at[slot, i], y_rs.at[slot, i], y_dev,
             )
 
-        def turn_index(k):
-            index = 0
-            for i in range(1, len(Z_FIRST)):
-                index = jnp.where(k == Z_FIRST[i], i, index)
-            return index
-
-        def turn_copy(k):
-            i = turn_index(k)
-            return remote(turn_src.at[i], turn_buf.at[i], turn_ss.at[i], turn_rs.at[i], y_dev)
+        def turn_copy():
+            return remote(turn_src, turn_buf, turn_ss, turn_rs, y_dev)
 
         def piece(k, half, target):
             return pool.at[slot_of(k, half), pl.ds(pl.multiple_of(target * unit, unit), unit)]
@@ -434,93 +470,138 @@
         def up_copy(job, k, half, target):
             i = target - 1
             return remote(
-                piece(k, half, target), up.at[job, i], up_ss.at[job, i], up_rs.at[job, i],
+                piece(k, half, target), land.at[job, i], z_ss.at[job, i], z_rs.at[job, i],
                 z_dev(jnp.minimum(z + 1, count - 1)),
             )
 
         def down_copy(job, k, half, target):
+            i = (target + count - 1) % LANDINGS
             return remote(
-                piece(k, half, target), down.at[job, target], down_ss.at[job, target],
-                down_rs.at[job, target], z_dev(jnp.maximum(z - 1, 0)),
+                piece(k, half, target), land.at[job, i], z_ss.at[job, target], z_rs.at[job, i],
+                z_dev(jnp.maximum(z - 1, 0)),
             )
 
-        def add_piece(k, half, target, landed):
-            ref = piece(k, half, target)
+        def add_to(ref, landed):
             ref[...] = (ref[...].astype(F32) + landed[...].astype(F32)).astype(BF)
 
         def hop(number, job, k, half):
             @pl.when(z == number - 1)
             def _():
                 for target in range(count - 1, number - 1, -1):
+                    copy = up_copy(job, k, half, target)
                     if number > 1:
-                        up_copy(job, k, half, target).wait_recv()
-                        add_piece(k, half, target, up.at[job, target - 1])
-                    up_copy(job, k, half, target).start()
+                        copy.wait_recv()
+                        add_to(piece(k, half, target), land.at[job, target - 1])
+                    copy.start()
 
             @pl.when(z == count - number)
             def _():
                 for target in range(0, count - number):
+                    copy = down_copy(job, k, half, target)
                     if number > 1:
-                        down_copy(job, k, half, target).wait_recv()
-                        add_piece(k, half, target, down.at[job, target])
-                    down_copy(job, k, half, target).start()
+                        copy.wait_recv()
+                        add_to(piece(k, half, target), land.at[job, (target + count - 1) % LANDINGS])
+                    copy.start()
 
         def arrive(job, k, half):
             out[k] = piece(k, half, z)[...].astype(F32)
 
             @pl.when(z > 0)
             def _():
-                up_copy(job, k, half, z).wait_recv()
-                out[k] += up[job, jnp.maximum(z - 1, 0)].astype(F32)
+                up_copy(job, k, half, jnp.maximum(z, 1)).wait_recv()
+                out[k] += land[job, jnp.maximum(z, 1) - 1].astype(F32)
 
             @pl.when(z < count - 1)
             def _():
                 down_copy(job, k, half, z).wait_recv()
-                out[k] += down[job, jnp.minimum(z, count - 2)].astype(F32)
-
-        def along_z_first(k):
-            hit = k == Z_FIRST[0]
-            for other in Z_FIRST[1:]:
-                hit = hit | (k == other)
-            return hit
-
-        def jobs_of(k):
-            return ((k, hi), (CHUNKS + turn_index(k), 1 - hi))
-
-        def product(k, half):
-            left = jnp.where(k < 8, jnp.minimum(k, L_N), jnp.where(k == 8, L_O, L_X))
-            right = jnp.where(k < 4, R_Z, jnp.where(k < 8, k, jnp.where(k == 8, R_A, k - 9)))
-            base = pl.multiple_of(half * block, block)
+                out[k] += land[job, (z + count - 1) % LANDINGS].astype(F32)
+
+        def product(k, number):
+            left = jnp.where(of_down(k), L_F + k // 2, L_N)
+            left = jnp.where(k < OUT, left, jnp.where(k == OUT, L_O, L_X))
+            right = jnp.where(of_down(k), R_Z, R_U + k // 2)
+            right = jnp.where(k < OUT, right, jnp.where(k == OUT, R_A, R_P + k - QKV))
+            base = pl.multiple_of(number * block, block)
             return dot_nn(lt[left, pl.ds(base, block), :], rt[right])
 
+        def down_product(k, core):
+            part = k // 2
+            own_rows = pl.ds(pl.multiple_of((hi * 2 + core) * block, block), block)
+            rows_y = pl.ds(pl.multiple_of(core * block, block), block)
+            return dot_nn(lt[L_F + part, own_rows, :], rt[R_Z]) + dot_nn(
+                lt_y[part, rows_y, :], dz_y[...]
+            )
+
         def for_core(k):
-            @pl.when(k >= 2)
+            @pl.when((k >= 2) & is_down(k - 2))
+            def _():
+                core_copy(k - 2, 0, hi).wait_send()
+
+            @pl.when((k >= 2) & jnp.logical_not(is_down(k - 2)))
             def _():
                 for half in range(2):
-                    core_copy(k - 2, half).wait_send()
-
-            for half in range(2):
-                core_src[k % 2, half] = product(k, half * 2 + 1 - lo).astype(BF)
-                core_copy(k, half).start()
+                    core_copy(k - 2, half, half).wait_send()
+
+            @pl.when((sec == 0) & (k == 3))
+            def _():
+                for m in range(MICRO):
+                    left_copy(m).wait_recv()
+                    right_copy(m).wait_recv()
+
+            @pl.when(is_down(k))
+            def _():
+                core_src[k % 2, 0] = down_product(k, 1 - lo).astype(BF)
+                core_copy(k, 0, hi).start()
+
+            @pl.when(jnp.logical_not(is_down(k)))
+            def _():
+                for half in range(2):
+                    core_src[k % 2, half] = product(k, half * 2 + 1 - lo).astype(BF)
+                    core_copy(k, half, half).start()
 
         def chip_sum(k):
-            for half in range(2):
-                core_copy(k, half).wait_recv()
-                slot = slot_of(k, half)
-                pool[slot] = (product(k, half * 2 + lo) + pool[slot].astype(F32)).astype(BF)
-
-            @pl.when(along_z_first(k))
-            def _():
-                for job, half in jobs_of(k):
-                    hop(1, job, k, half)
-
-            @pl.when(jnp.logical_not(along_z_first(k)))
-            def _():
-                for i in range(count):
-                    y_copy(k, i)[1].start()
+            @pl.when(is_down(k))
+            def _():
+                core_copy(k, 0, hi).wait_recv()
+                slot = slot_of(k, hi)
+                pool[slot] = (down_product(k, lo) + pool[slot].astype(F32)).astype(BF)
+                hop(1, k, k, hi)
+
+            @pl.when(jnp.logical_not(is_down(k)))
+            def _():
+                for half in range(2):
+                    core_copy(k, half, half).wait_recv()
+                    slot = slot_of(k, half)
+                    pool[slot] = (product(k, half * 2 + lo) + pool[slot].astype(F32)).astype(BF)
+
+                @pl.when(k == 0)
+                def _():
+                    for job, half in ((0, hi), (CHUNKS, 1 - hi)):
+                        hop(1, job, 0, half)
+
+                @pl.when(k > 0)
+                def _():
+                    for i in range(2):
+                        y_copy(k, i)[2].start()
+
+        def from_y(k):
+            for i in range(2):
+                rows_of, landed, copy = y_copy(k, i)
+                copy.wait_recv()
+                add_to(pool.at[slot_of(k, hi), rows_of], landed)
+
+                @pl.when(z == 0)
+                def _(i=i):
+                    for target in ((3, 2), (1,))[i]:
+                        up_copy(k, k, hi, target).start()
+
+                @pl.when(z == count - 1)
+                def _(i=i):
+                    for target in ((0, 1), (2,))[i]:
+                        down_copy(k, k, hi, target).start()
 
         def part_copy(k):
-            return pltpu.make_async_copy(out.at[k], out_hbm.at[k], part_sem.at[k])
+            return pltpu.make_async_copy(out.at[k], out_hbm.at[k], part_sem)
 
         def bias_core():
             return remote(b_src.at[0], b_core, bc_ss.at[0], bc_rs.at[0], core_dev)
@@ -539,76 +620,59 @@
             def _():
                 for_core(t)
 
-            @pl.when((t >= 1) & (t <= CHUNKS))
-            def _():
-                chip_sum(t - 1)
-
-            def y_first_at(lag, action):
-                k = t - lag
-
-                @pl.when((k >= 0) & (k < CHUNKS) & jnp.logical_not(along_z_first(k)))
+            @pl.when(((t >= 2) & (t <= CHUNKS)) | (t == 0))
+            def _():
+                chip_sum(jnp.maximum(t - 1, 0))
+
+            def at(tables, action):
+                k = -1
+                for section, table in enumerate(tables):
+                    for when, chunk in table.items():
+                        k = jnp.where((sec == section) & (t == when), chunk, k)
+
+                @pl.when(k >= 0)
                 def _():
                     action(k)
 
-            def z_first_at(lag, action):
-                k = t - lag
-
-                @pl.when(along_z_first(k))
-                def _():
-                    action(k)
-
-            def from_y(k):
-                for i in range(count):
-                    target, copy = y_copy(k, i)
-                    copy.wait_recv()
-                    add_piece(k, hi, target, y_buf.at[k % Y_SLOTS, i])
-                    if i < count - 1:
-                        @pl.when(z == 0)
-                        def _(target=count - 1 - i):
-                            up_copy(k, k, hi, target).start()
-
-                        @pl.when(z == count - 1)
-                        def _(target=i):
-                            down_copy(k, k, hi, target).start()
-
-            y_first_at(4, from_y)
-            for number in range(2, count):
-                y_first_at(4 + number, lambda k, number=number: hop(number, k, k, hi))
-
-                def both_halves(k, number=number):
-                    for job, half in jobs_of(k):
-                        hop(number, job, k, half)
-
-                z_first_at(2 + 2 * number, both_halves)
-
-            def turn(k):
-                stays, goes = jobs_of(k)
-                arrive(goes[0], k, goes[1])
-                turn_src[turn_index(k)] = out[k].astype(BF)
-                turn_copy(k).start()
-                arrive(stays[0], k, stays[1])
+            def both_halves(number):
+                for job, half in ((0, hi), (CHUNKS, 1 - hi)):
+                    hop(number, job, 0, half)
+
+            at(FROM_Y, from_y)
+            at(THIRD, lambda k: hop(3, k, k, hi))
+            at(SECOND, lambda k: hop(2, k, k, hi))
+
+            @pl.when(t == 6)
+            def _():
+                both_halves(2)
+
+            @pl.when(t == 10)
+            def _():
+                both_halves(3)
 
             @pl.when(t == CHUNKS + 1)
             def _():
                 send_input_grad(MICRO - 1)
 
-            for i, k in enumerate(Z_FIRST):
-                @pl.when(t == CHUNKS + 4 + i)
-                def _(k=k):
-                    turn(k)
-
-            @pl.when(t == 7)
+            @pl.when(t == CHUNKS + 1)
+            def _():
+                arrive(CHUNKS, 0, 1 - hi)
+                turn_src[...] = out[0].astype(BF)
+                turn_copy().start()
+                arrive(0, 0, hi)
+
+            @pl.when(t == 5)
             def _():
                 b_src[0] = bg[...]
                 bias_core().start()
 
-            @pl.when(t == 9)
+            @pl.when(t == 6)
             def _():
                 bias_core().wait_recv()
                 b_src[1] = b_src[0] + b_core[...]
                 bias_y().start()
 
-            @pl.when(t == 11)
+            @pl.when(t == 16)
             def _():
                 bias_y().wait_recv()
                 b_src[2] = b_src[1] + b_y[...]
@@ -669,18 +733,14 @@
         lax.fori_loop(jnp.where(sec == 0, EARLY, 0), STEPS, rest, 0)
 
         def last_sum(k, carry):
-            @pl.when(jnp.logical_not(along_z_first(k)))
-            def _():
-                arrive(k, k, hi)
-                part_copy(k).start()
-
+            arrive(k, k, hi)
+            part_copy(k).start()
             return carry
 
-        lax.fori_loop(0, CHUNKS, last_sum, 0)
-        for k in Z_FIRST:
-            turn_copy(k).wait_recv()
-            out[k] += turn_buf[turn_index(k)].astype(F32)
-            part_copy(k).start()
+        lax.fori_loop(1, CHUNKS, last_sum, 0)
+        turn_copy().wait_recv()
+        out[0] += turn_buf[...].astype(F32)
+        part_copy(0).start()
 
         total = b_src[2]
         for by in range(1, count):
@@ -705,27 +765,28 @@
                         down_copy(job, k, half, target).wait_send()
 
         def drain(k, carry):
-            part_copy(k).wait()
-            @pl.when(k >= CHUNKS - 2)
-            def _():
-                for half in range(2):
-                    core_copy(k, half).wait_send()
-
             sent(k, k, hi)
 
-            @pl.when(along_z_first(k))
-            def _():
-                turn_copy(k).wait_send()
-                sent(CHUNKS + turn_index(k), k, 1 - hi)
-
-            @pl.when(jnp.logical_not(along_z_first(k)))
-            def _():
-                for i in range(count):
-                    y_copy(k, i)[1].wait_send()
+            @pl.when((k > 0) & jnp.logical_not(is_down(k)))
+            def _():
+                for i in range(2):
+                    y_copy(k, i)[2].wait_send()
 
             return carry
 
         lax.fori_loop(0, CHUNKS, drain, 0)
+        pltpu.make_async_copy(out, out_hbm, part_sem).wait()
+        sent(CHUNKS, 0, 1 - hi)
+        turn_copy().wait_send()
+        for k in (CHUNKS - 2, CHUNKS - 1):
+            for half in range(2):
+                core_copy(k, half, half).wait_send()
+
+        @pl.when(sec == 0)
+        def _():
+            for m in range(MICRO):
+                left_copy(m).wait_send()
+                right_copy(m).wait_send()
 
     for m in range(MICRO):
         seq_copy(in_hbm, m).wait_send()
@@ -753,7 +814,6 @@
     unit = width // 16
     block = count * unit
     tall = width // 4
-    jobs = CHUNKS + len(Z_FIRST)
     any_spec = pl.BlockSpec(memory_space=pl.ANY)
     vmem = pl.BlockSpec(memory_space=pltpu.VMEM)
     smem = pl.BlockSpec(memory_space=pltpu.SMEM)
@@ -772,7 +832,7 @@
         pltpu.VMEM((2, total, width), BF),
         pltpu.VMEM((width, 3 * width), BF),
         pltpu.VMEM((width, width), BF),
-        pltpu.VMEM((ff // tall + (2 * DEDICATED if with_sums else 0), tall, width), BF),
+        pltpu.VMEM((ff // tall + (8 if with_sums else 0), tall, width), BF),
         pltpu.VMEM((ff, width), BF),
         pltpu.VMEM((total, width), BF),
         pltpu.VMEM((MICRO, 2, keys, width), BF),
@@ -790,7 +850,7 @@
         pltpu.VMEM((2, rows, width), BF),
         pltpu.VMEM((MICRO, 2, rows, width), BF),
         pltpu.VMEM((total, width), BF),
-        dma((3 + 4 * (ff // width),)), dma((MICRO,)), dma((MICRO,)), dma((MICRO,)), dma((MICRO,)), dma((MICRO,)),
+        dma((4,)), dma((MICRO,)), dma((MICRO,)), dma((MICRO,)), dma((MICRO,)), dma((MICRO,)),
         dma((MICRO, 2)), dma((MICRO, 2)), dma((MICRO, 2)), dma((MICRO, 2)),
         dma((2, MICRO)), dma((2, MICRO)), dma((2, MICRO)),
     ]
@@ -798,21 +858,21 @@
         scratch += [pltpu.VMEM(dims, kind) for dims, kind in stacks]
         scratch += [
             pltpu.VMEM((CHUNKS, unit, width), F32),
+            pltpu.VMEM((ff // width, 2 * block, total), BF),
+            pltpu.VMEM((total, width), BF),
             pltpu.VMEM((2, 2, block, width), BF),
-            pltpu.VMEM((Y_SLOTS, count, unit, width), BF),
-            pltpu.VMEM((jobs, count - 1, unit, width), BF),
-            pltpu.VMEM((jobs, count - 1, unit, width), BF),
-            pltpu.VMEM((len(Z_FIRST), unit, width), BF),
-            pltpu.VMEM((len(Z_FIRST), unit, width), BF),
+            pltpu.VMEM((CHUNKS - 1, 2, 2 * unit, width), BF),
+            pltpu.VMEM((CHUNKS + 1, LANDINGS, unit, width), BF),
+            pltpu.VMEM((unit, width), BF),
+            pltpu.VMEM((unit, width), BF),
             pltpu.VMEM((3, 12, 1, width), F32),
             pltpu.VMEM((12, 1, width), F32),
             pltpu.VMEM((12, 1, width), F32),
             pltpu.VMEM((count - 1, 12, 1, width), F32),
-            dma((CHUNKS, 2)), dma((CHUNKS, 2)), dma((CHUNKS, count)), dma((CHUNKS, count)),
-            dma((jobs, count - 1)), dma((jobs, count - 1)),
-            dma((jobs, count - 1)), dma((jobs, count - 1)),
-            dma((len(Z_FIRST),)), dma((len(Z_FIRST),)), dma((2,)), dma((2,)),
-            dma((count - 1,)), dma((count - 1,)), dma((CHUNKS,)),
+            dma((2, 2)), dma((4, 2)), dma((CHUNKS - 1, 2)), dma((CHUNKS - 1, 2)),
+            dma((CHUNKS + 1, count - 1)), dma((CHUNKS + 1, LANDINGS)), dma, dma,
+            dma((2,)), dma((2,)), dma((count - 1,)), dma((count - 1,)), dma,
+            dma((MICRO,)), dma((MICRO,)), dma((MICRO,)), dma((MICRO,)),
         ]
     return pl.pallas_call(
         functools.partial(train_kernel, with_sums),
@@ -872,14 +932,14 @@
     copies.append(copy(5, kept, sout_ref.at[0]))
     parts_in.wait()
     for k in range(CHUNKS):
-        if k < 4:
-            dst = down_ref.at[0, pl.ds(k * unit, unit), :]
-        elif k < 8:
-            dst = up_ref.at[0, :, pl.ds((k - 4) * width, width)]
-        elif k == 8:
+        if k in (0, 3, 5, 7):
+            dst = down_ref.at[0, pl.ds(k // 2 * unit, unit), :]
+        elif k < OUT:
+            dst = up_ref.at[0, :, pl.ds(k // 2 * width, width)]
+        elif k == OUT:
             dst = wout_ref.at[0]
         else:
-            dst = qkv_ref.at[0, :, pl.ds((k - 9) * width, width)]
+            dst = qkv_ref.at[0, :, pl.ds((k - QKV) * width, width)]
         copies.append(copy(6 + k, parts.at[k], dst))
     sums_in.wait()
     index = lax.axis_index("seq") * lax.axis_size("dp") + lax.axis_index("dp")

time: 176 us -> 169 us (0.960)
  Pallas kernels: 175 us -> 168 us
    pallas_call x1, Pallas kernels: 171 us -> 164 us  [run_train(): pl.pallas_call(functools.partial(train_kernel, with_sums), name='train',...]
where the time goes in v6:
time: 169 us
  Pallas kernels  168 us (99%)
    pallas_call x1, Pallas kernels, run_train(): pl.pallas_call(functools.partial(train_kernel, with_sums), name='train',...  164 us
    pallas_call x1, Pallas kernels, run_finish(): pl.pallas_call(finish_kernel, name='finish', out_shape=(shape((1,) + sout...  3.96 us

profile of v6, /device:TPU:0, one launch (start us, length us, event | category | flops | bytes accessed | tf_op | source)
XLA Modules:
  0.0 168.8 jit_solution(13754587478020218803)
XLA Ops:
  0.6 164.0 %train.1 = (bf16[4,128,768]{2,1,0:T(8,128)(2,1)}, bf16[4,128,768]{2,1,0:T(8,128)(2,1)}, f32[12,48,768]{2,1,0:T(8,128)}, f32[12,1,768]{2,1,0:T(1,128)}) custom-call(s32[4]{0:T(128)} %refs_0_.1, bf16[4,128,768]{2,1,0:T(8,128)(2,1)} %refs_1_.1, bf16[4,128,768]{2,1,0:T(8,128)(2,1)} %refs_2_.1, bf16[1,768,2304]{2,1,0:T(8,128)(2,1)} %refs_3_.1, ...), custom_call_target="tpu_custom_call" | custom-call | tf_op jit(solution)/shard_map/train/pallas_call | solution.py:877
  164.7 4.0 %finish.1 = (bf16[1,4,128,768]{3,2,1,0:T(8,128)(2,1)}, f32[1,4,128,768]{3,2,1,0:T(8,128)}, f32[1,48,2304]{2,1,0:T(8,128)}, f32[1,96]{1,0:T(1,128)}, f32[1,48,768...) custom-call(bf16[4,128,768]{2,1,0:T(8,128)(2,1)} %get-tuple-element., ...), custom_call_target="tpu_custom_call" | custom-call | tf_op jit(solution)/shard_map/finish/pallas_call | solution.py:971

commit v7 on v6

--- a/solution.py
+++ b/solution.py
@@ -21,21 +21,31 @@
 CHUNKS = 12
 OUT = 8
 QKV = 9
-EARLY = 5
+EARLY = 6
 FROM_Y = (
-    {5: 1, 8: 2, 11: 4, 13: 6, 15: 8, 16: 9, 17: 10, 19: 11},
-    {k + 4: k for k in range(1, CHUNKS)},
+    {5: 1, 7: 2, 10: 4, 13: 6, 15: 8, 16: 9, 17: 10, 19: 11},
+    {5: 1, 6: 2, 7: 3, 9: 5, 10: 6, 11: 7, 12: 8, 13: 9, 14: 10, 15: 11},
 )
 SECOND = (
     {8: 3, 10: 1, 11: 5, 12: 7, 13: 2, 14: 4, 15: 6, 17: 8, 18: 9, 19: 10, 20: 11},
-    {k + 5: k for k in range(1, CHUNKS)},
+    {7: 1, 8: 2, 9: 3, 10: 5, 11: 6, 12: 7, 13: 8, 14: 9, 15: 10, 16: 11},
 )
 THIRD = tuple(
     {t + lag: k for t, k in table.items()} for lag, table in zip((2, 1), SECOND)
 )
+ARRIVE = (
+    {14: 3, 15: 1, 16: 5, 17: 7, 18: 2, 19: 4, 20: 6, 21: 8},
+    {11: 1, 12: 2, 13: 3, 15: 5, 16: 6, 17: 7, 18: 8},
+)
+Z_FIRST = 2
+Z_SECOND = ({5: 0}, {6: 0, 9: 4})
+Z_THIRD = ({9: 0}, {8: 0, 11: 4})
+TURN = ({14: 0}, {13: 0, 14: 4})
+LAST = QKV
 STEPS = 23
 LANDINGS = 5
-VMEM_LIMIT = 63 * 2 ** 20
+Y_SLOTS = 10
+VMEM_LIMIT = 127 * 2 ** 19
 
 
 def dot_nn(a, b):
@@ -63,8 +73,8 @@
         out_hbm, bg_out = take(2)
     else:
         lt, rt, bg = take(3)
-    (ab, wqkv, wout, pool, wdown, q_s, kv, lse, o_s, n_s, xh1, xh2, rs1, rs2, dr1, acc, do_s,
-     dkv_own, dkv_send, dkv_recv, yb) = take(21)
+    (ab, wqkv, wout, pool, wdown, q_s, kv, lse, o_s, n_s, xh1, xh2, rs, dr1, acc, do_s,
+     dkv_own, dkv_send, dkv_recv, yb) = take(20)
     (w_sem, loc_sem, ex_send, ex_recv, hop_send, hop_recv, kv_ss, kv_rs, dk_ss, dk_rs,
      out_loc, out_ss, out_rs) = take(13)
     if with_sums:
@@ -232,6 +242,12 @@
     def add_bias_grad(row, value):
         bg[row] += jnp.sum(value, axis=0, keepdims=True)
 
+    def turn_left_sides(m):
+        r = mrows(m)
+        lt[L_X, :, r] = ab[sec, r].T
+        lt[L_N, :, r] = n_s[r].T
+        lt[L_O, :, r] = o_s[r].T
+
     def left_copy(m):
         tall_half = 2 * tall
         return remote(
@@ -260,7 +276,6 @@
         kv_copy(m, 1).start()
         queries = (dot_nn(x, wqkv[:, 0:width]) + vec(abias_ref, 0)).astype(BF)
         q_s[r] = queries * (hd ** -0.5)
-        lt[L_X, :, r] = x.T
 
         @pl.when(step == 0)
         def _():
@@ -290,12 +305,12 @@
         r1 = ab[sec, r].astype(F32) + dot_nn(o_s[r], wout[...]) + vec(obias_ref, 0)
         hat, scale, n1 = norm(r1, vec(gain_ref, 0), vec(shift_ref, 0))
         xh1[r] = hat.astype(BF)
-        rs1[r] = jnp.broadcast_to(scale, (rows, LANES))
-        n_s[...] = n1.astype(BF)
+        rs[r] = jnp.broadcast_to(scale, (rows, LANES))
+        n_s[r] = n1.astype(BF)
         acc[...] = n1 + vec(obias_ref, 1)
         for j in range(nff):
             cols = pl.ds(j * width, width)
-            u = dot_nn(n_s[...], wup(j)) + bup_ref[0:1, cols].astype(F32)
+            u = dot_nn(n_s[r], wup(j)) + bup_ref[0:1, cols].astype(F32)
             phi = 0.5 + 0.5 * lax.erf(u * INV_SQRT_2)
             f = (u * phi).astype(BF)
             f_t = f.T
@@ -307,7 +322,7 @@
             acc[...] += dot_nn(f, wdown[cols, :])
         hat, scale, result = norm(acc[...], vec(gain_ref, 1), vec(shift_ref, 1))
         xh2[r] = hat.astype(BF)
-        rs2[r] = jnp.broadcast_to(scale, (rows, LANES))
+        rs[r] = jnp.where(left_lanes(), rs[r], scale)
         yb[r] = result.astype(BF)
 
         @pl.when(sec == 0)
@@ -321,8 +336,11 @@
             def _():
                 left_copy(m).start()
 
-        lt[L_N, :, r] = n_s[...].T
-        lt[L_O, :, r] = o_s[r].T
+
+        @pl.when(sec == 0)
+        def _():
+            turn_left_sides(m)
+
 
     def backward(m, serve):
         r = mrows(m)
@@ -333,7 +351,7 @@
         hat = xh2[r].astype(F32)
         add_bias_grad(9, dy * hat)
         add_bias_grad(11, dy)
-        dr2 = norm_back(dy, hat, rs2[r, 0:1], vec(gain_ref, 1))
+        dr2 = norm_back(dy, hat, rs[r, hd:hd + 1], vec(gain_ref, 1))
         dz = dr2.astype(BF)
         rt[R_Z, r] = dz
         if with_sums:
@@ -355,12 +373,13 @@
         hat = xh1[r].astype(F32)
         add_bias_grad(8, dn1 * hat)
         add_bias_grad(10, dn1)
-        grad1 = norm_back(dn1, hat, rs1[r, 0:1], vec(gain_ref, 0))
+        grad1 = norm_back(dn1, hat, rs[r, 0:1], vec(gain_ref, 0))
         dr1[...] = grad1
         da = grad1.astype(BF)
         rt[R_A, r] = da
         add_bias_grad(2, da.astype(F32))
         do_s[...] = dot_nt(da, wout[...]).astype(BF)
+        serve(3, 5)
         key_bias = jnp.where(positions((keys, 1), 0) < length, 0.0, -1e30)
 
         def head_pair(group, index):
@@ -390,7 +409,7 @@
                 head_pair(group, index)
             dkv_copy(m, group).start()
             if group == 0:
-                serve(3, EARLY)
+                serve(5, EARLY)
         dq = rt[R_P, r]
         add_bias_grad(0, dq.astype(F32))
         dr1[...] += dot_nt(dq, wqkv[:, 0:width])
@@ -421,7 +440,7 @@
         def _():
             hop_copy(yb, m).start()
 
-        @pl.when(m == 0)
+        @pl.when((m == 0) & (sec == 1))
         def _():
             send_input_grad(m)
 
@@ -433,13 +452,25 @@
         for copy in out_copies(1, yb, sgrad_hbm, m):
             copy.start()
 
+    def send_late_grads():
+        @pl.when(sec == 0)
+        def _():
+            send_input_grad(0)
+
+        send_input_grad(1)
+
 
     if with_sums:
         block = count * unit
         two = 2 * unit
 
+        other_z = 4
+
         def of_down(k):
             return (k == 0) | ((k % 2 == 1) & (k >= 3) & (k < OUT))
+
+        def is_z_first(k):
+            return (k == 0) | ((sec == 1) & (k == other_z))
 
         def is_down(k):
             return (sec == 0) & of_down(k) & (k > 0)
@@ -455,14 +486,20 @@
 
         def y_copy(k, i):
             rows_of = pl.ds(pl.multiple_of(jnp.where(z < count // 2, 1 - i, i) * two, two), two)
-            slot = k - 1
+            first = jnp.where(k < 4, k - 1, jnp.where(k < QKV, k // 2, k - 4))
+            second = k - 1 - jnp.where(k > 4, 1, 0)
+            slot = jnp.where(sec == 0, first, second)
             return rows_of, y_buf.at[slot, i], remote(
                 pool.at[slot_of(k, 1 - hi), rows_of], y_buf.at[slot, i],
                 y_ss.at[slot, i], y_rs.at[slot, i], y_dev,
             )
 
-        def turn_copy():
-            return remote(turn_src, turn_buf, turn_ss, turn_rs, y_dev)
+        def turn_copy(k):
+            i = jnp.where(k == 0, 0, 1)
+            return remote(turn_src.at[i], turn_buf.at[i], turn_ss.at[i], turn_rs.at[i], y_dev)
+
+        def z_first_jobs(k):
+            return ((k, hi), (CHUNKS + jnp.where(k == 0, 0, 1), 1 - hi))
 
         def piece(k, half, target):
             return pool.at[slot_of(k, half), pl.ds(pl.multiple_of(target * unit, unit), unit)]
@@ -574,12 +611,12 @@
                     slot = slot_of(k, half)
                     pool[slot] = (product(k, half * 2 + lo) + pool[slot].astype(F32)).astype(BF)
 
-                @pl.when(k == 0)
+                @pl.when(is_z_first(k))
                 def _():
-                    for job, half in ((0, hi), (CHUNKS, 1 - hi)):
-                        hop(1, job, 0, half)
-
-                @pl.when(k > 0)
+                    for job, half in z_first_jobs(k):
+                        hop(1, job, k, half)
+
+                @pl.when(jnp.logical_not(is_z_first(k)))
                 def _():
                     for i in range(2):
                         y_copy(k, i)[2].start()
@@ -600,6 +637,30 @@
                     for target in ((0, 1), (2,))[i]:
                         down_copy(k, k, hi, target).start()
 
+        def finished(k):
+            arrive(k, k, hi)
+            part_copy(k).start()
+
+        def sent(job, k, half):
+            for target in range(count):
+                if target > 0:
+                    @pl.when(target > z)
+                    def _(target=target):
+                        up_copy(job, k, half, target).wait_send()
+
+                if target < count - 1:
+                    @pl.when(target < z)
+                    def _(target=target):
+                        down_copy(job, k, half, target).wait_send()
+
+        def drain(k):
+            sent(k, k, hi)
+
+            @pl.when(jnp.logical_not(is_z_first(k) | is_down(k)))
+            def _():
+                for i in range(2):
+                    y_copy(k, i)[2].wait_send()
+
         def part_copy(k):
             return pltpu.make_async_copy(out.at[k], out_hbm.at[k], part_sem)
 
@@ -634,39 +695,42 @@
                 def _():
                     action(k)
 
-            def both_halves(number):
-                for job, half in ((0, hi), (CHUNKS, 1 - hi)):
-                    hop(number, job, 0, half)
+            def both_halves(number, k):
+                for job, half in z_first_jobs(k):
+                    hop(number, job, k, half)
+
+            def turn(k):
+                stays, goes = z_first_jobs(k)
+                arrive(goes[0], k, goes[1])
+                turn_src[jnp.where(k == 0, 0, 1)] = out[k].astype(BF)
+                turn_copy(k).start()
+                arrive(stays[0], k, stays[1])
 
             at(FROM_Y, from_y)
             at(THIRD, lambda k: hop(3, k, k, hi))
             at(SECOND, lambda k: hop(2, k, k, hi))
 
-            @pl.when(t == 6)
-            def _():
-                both_halves(2)
-
-            @pl.when(t == 10)
-            def _():
-                both_halves(3)
+            at(Z_THIRD, lambda k: both_halves(3, k))
+            at(Z_SECOND, lambda k: both_halves(2, k))
+
+            at(ARRIVE, finished)
+
+            @pl.when((t >= 14) & (t < 14 + LAST))
+            def _():
+                drain(t - 14)
 
             @pl.when(t == CHUNKS + 1)
             def _():
-                send_input_grad(MICRO - 1)
-
-            @pl.when(t == CHUNKS + 1)
-            def _():
-                arrive(CHUNKS, 0, 1 - hi)
-                turn_src[...] = out[0].astype(BF)
-                turn_copy().start()
-                arrive(0, 0, hi)
-
-            @pl.when(t == 5)
+                send_late_grads()
+
+            at(TURN, turn)
+
+            @pl.when(t == EARLY)
             def _():
                 b_src[0] = bg[...]
                 bias_core().start()
 
-            @pl.when(t == 6)
+            @pl.when(t == EARLY + 1)
             def _():
                 bias_core().wait_recv()
                 b_src[1] = b_src[0] + b_core[...]
@@ -722,8 +786,13 @@
 
     lax.fori_loop(0, 8, one_step, 0)
 
+    @pl.when(sec == 1)
+    def _():
+        for m in range(MICRO):
+            turn_left_sides(m)
+
     if not with_sums:
-        send_input_grad(MICRO - 1)
+        send_late_grads()
 
     if with_sums:
         def rest(t, carry):
@@ -732,15 +801,14 @@
 
         lax.fori_loop(jnp.where(sec == 0, EARLY, 0), STEPS, rest, 0)
 
-        def last_sum(k, carry):
-            arrive(k, k, hi)
-            part_copy(k).start()
-            return carry
-
-        lax.fori_loop(1, CHUNKS, last_sum, 0)
-        turn_copy().wait_recv()
-        out[0] += turn_buf[...].astype(F32)
-        part_copy(0).start()
+        for k in range(LAST, CHUNKS):
+            finished(k)
+        for i, k in enumerate((0, other_z)):
+            @pl.when((sec == 1) | (i == 0))
+            def _(i=i, k=k):
+                turn_copy(k).wait_recv()
+                out[k] += turn_buf[i].astype(F32)
+                part_copy(k).start()
 
         total = b_src[2]
         for by in range(1, count):
@@ -752,32 +820,14 @@
         for by in range(1, count):
             bias_z(by).wait_send()
 
-        def sent(job, k, half):
-            for target in range(count):
-                if target > 0:
-                    @pl.when(target > z)
-                    def _(target=target):
-                        up_copy(job, k, half, target).wait_send()
-
-                if target < count - 1:
-                    @pl.when(target < z)
-                    def _(target=target):
-                        down_copy(job, k, half, target).wait_send()
-
-        def drain(k, carry):
-            sent(k, k, hi)
-
-            @pl.when((k > 0) & jnp.logical_not(is_down(k)))
-            def _():
-                for i in range(2):
-                    y_copy(k, i)[2].wait_send()
-
-            return carry
-
-        lax.fori_loop(0, CHUNKS, drain, 0)
+        for k in range(LAST, CHUNKS):
+            drain(k)
         pltpu.make_async_copy(out, out_hbm, part_sem).wait()
-        sent(CHUNKS, 0, 1 - hi)
-        turn_copy().wait_send()
+        for i, k in enumerate((0, other_z)):
+            @pl.when((sec == 1) | (i == 0))
+            def _(i=i, k=k):
+                sent(CHUNKS + i, k, 1 - hi)
+                turn_copy(k).wait_send()
         for k in (CHUNKS - 2, CHUNKS - 1):
             for half in range(2):
                 core_copy(k, half, half).wait_send()
@@ -838,10 +888,9 @@
         pltpu.VMEM((MICRO, 2, keys, width), BF),
         pltpu.VMEM((MICRO, 8, keys), F32),
         pltpu.VMEM((total, width), BF),
-        pltpu.VMEM((rows, width), BF),
         pltpu.VMEM((total, width), BF),
         pltpu.VMEM((total, width), BF),
-        pltpu.VMEM((total, LANES), F32),
+        pltpu.VMEM((total, width), BF),
         pltpu.VMEM((total, LANES), F32),
         pltpu.VMEM((rows, width), F32),
         pltpu.VMEM((rows, width), F32),
@@ -861,16 +910,17 @@
             pltpu.VMEM((ff // width, 2 * block, total), BF),
             pltpu.VMEM((total, width), BF),
             pltpu.VMEM((2, 2, block, width), BF),
-            pltpu.VMEM((CHUNKS - 1, 2, 2 * unit, width), BF),
-            pltpu.VMEM((CHUNKS + 1, LANDINGS, unit, width), BF),
-            pltpu.VMEM((unit, width), BF),
-            pltpu.VMEM((unit, width), BF),
+            pltpu.VMEM((Y_SLOTS, 2, 2 * unit, width), BF),
+            pltpu.VMEM((CHUNKS + Z_FIRST, LANDINGS, unit, width), BF),
+            pltpu.VMEM((Z_FIRST, unit, width), BF),
+            pltpu.VMEM((Z_FIRST, unit, width), BF),
             pltpu.VMEM((3, 12, 1, width), F32),
             pltpu.VMEM((12, 1, width), F32),
             pltpu.VMEM((12, 1, width), F32),
             pltpu.VMEM((count - 1, 12, 1, width), F32),
-            dma((2, 2)), dma((4, 2)), dma((CHUNKS - 1, 2)), dma((CHUNKS - 1, 2)),
-            dma((CHUNKS + 1, count - 1)), dma((CHUNKS + 1, LANDINGS)), dma, dma,
+            dma((2, 2)), dma((4, 2)), dma((Y_SLOTS, 2)), dma((Y_SLOTS, 2)),
+            dma((CHUNKS + Z_FIRST, count - 1)), dma((CHUNKS + Z_FIRST, LANDINGS)),
+            dma((Z_FIRST,)), dma((Z_FIRST,)),
             dma((2,)), dma((2,)), dma((count - 1,)), dma((count - 1,)), dma,
             dma((MICRO,)), dma((MICRO,)), dma((MICRO,)), dma((MICRO,)),
         ]
@@ -924,14 +974,14 @@
     sums_in = copy(0, sums_hbm, sums)
     grad_in = copy(1, sgrad, low)
     out_in = copy(2, sout, kept)
-    parts_in = copy(3, grads, parts)
+    parts_in = [copy(6 + CHUNKS + k, grads.at[k], parts.at[k]) for k in range(CHUNKS)]
     grad_in.wait()
     wide_grad[...] = low[...].astype(F32)
     copies = [copy(4, wide_grad, sgrad_ref.at[0])]
     out_in.wait()
     copies.append(copy(5, kept, sout_ref.at[0]))
-    parts_in.wait()
     for k in range(CHUNKS):
+        parts_in[k].wait()
         if k in (0, 3, 5, 7):
             dst = down_ref.at[0, pl.ds(k // 2 * unit, unit), :]
         elif k < OUT:
@@ -993,7 +1043,7 @@
             pltpu.VMEM(sgrad.shape, F32),
             pltpu.VMEM(grads.shape, F32),
             pltpu.VMEM(sums.shape, F32),
-            pltpu.SemaphoreType.DMA((6 + CHUNKS,)),
+            pltpu.SemaphoreType.DMA((6 + 2 * CHUNKS,)),
         ],
         compiler_params=pltpu.CompilerParams(vmem_limit_bytes=VMEM_LIMIT),
     )(sout, sgrad, grads, sums)

time: 169 us -> 165 us (0.976)
  Pallas kernels: 168 us -> 164 us
    pallas_call x1, Pallas kernels: 164 us -> 160 us  [run_train(): pl.pallas_call(functools.partial(train_kernel, with_sums), name='train',...]
where the time goes in v7:
time: 165 us
  Pallas kernels  164 us (99%)
    pallas_call x1, Pallas kernels, run_train(): pl.pallas_call(functools.partial(train_kernel, with_sums), name='train',...  160 us
    pallas_call x1, Pallas kernels, run_finish(): pl.pallas_call(finish_kernel, name='finish', out_shape=(shape((1,) + sout...  4.07 us

profile of v7, /device:TPU:0, one launch (start us, length us, event | category | flops | bytes accessed | tf_op | source)
XLA Modules:
  0.0 164.7 jit_solution(13491179118154462819)
XLA Ops:
  0.6 159.8 %train.1 = (bf16[4,128,768]{2,1,0:T(8,128)(2,1)}, bf16[4,128,768]{2,1,0:T(8,128)(2,1)}, f32[12,48,768]{2,1,0:T(8,128)}, f32[12,1,768]{2,1,0:T(1,128)}) custom-call(s32[4]{0:T(128)} %refs_0_.1, bf16[4,128,768]{2,1,0:T(8,128)(2,1)} %refs_1_.1, bf16[4,128,768]{2,1,0:T(8,128)(2,1)} %refs_2_.1, bf16[1,768,2304]{2,1,0:T(8,128)(2,1)} %refs_3_.1, ...), custom_call_target="tpu_custom_call" | custom-call | tf_op jit(solution)/shard_map/train/pallas_call | solution.py:927
  160.5 4.1 %finish.1 = (bf16[1,4,128,768]{3,2,1,0:T(8,128)(2,1)}, f32[1,4,128,768]{3,2,1,0:T(8,128)}, f32[1,48,2304]{2,1,0:T(8,128)}, f32[1,96]{1,0:T(1,128)}, f32[1,48,768...) custom-call(bf16[4,128,768]{2,1,0:T(8,128)(2,1)} %get-tuple-element., ...), custom_call_target="tpu_custom_call" | custom-call | tf_op jit(solution)/shard_map/finish/pallas_call | solution.py:1021

commit v8 on v7

--- a/solution.py
+++ b/solution.py
@@ -161,8 +161,14 @@
 
     bg[...] = jnp.zeros_like(bg)
 
-    def hop_copy(src, m):
-        return remote(src.at[mrows(m)], ab.at[1, mrows(m)], hop_send.at[m], hop_recv.at[m], x_dev)
+    def part_rows(m, base, size):
+        return pl.ds(pl.multiple_of(m * rows + base, size), size)
+
+    def hop_copy(m, part):
+        place = part_rows(m, part * span, span)
+        return remote(
+            yb.at[place], ab.at[1, place], hop_send.at[m, part], hop_recv.at[m, part], x_dev
+        )
 
     def kv_copy(m, part):
         return remote(
@@ -200,7 +206,8 @@
 
         @pl.when(which == 1)
         def _():
-            hop_copy(yb, m).wait_recv()
+            for part in range(2):
+                hop_copy(m, part).wait_recv()
 
     def positions(shape, dim):
         row = lax.broadcasted_iota(jnp.int32, shape, dim)
@@ -308,26 +315,39 @@
         rs[r] = jnp.broadcast_to(scale, (rows, LANES))
         n_s[r] = n1.astype(BF)
         acc[...] = n1 + vec(obias_ref, 1)
-        for j in range(nff):
-            cols = pl.ds(j * width, width)
-            u = dot_nn(n_s[r], wup(j)) + bup_ref[0:1, cols].astype(F32)
-            phi = 0.5 + 0.5 * lax.erf(u * INV_SQRT_2)
-            f = (u * phi).astype(BF)
-            f_t = f.T
-            for owner in range(quarter):
-                for part in range(nff):
-                    at = (owner * nff + part) * unit
-                    lt[part, pl.ds((j * quarter + owner) * unit, unit), r] = f_t[at:at + unit]
-            rt[R_U + j, r] = (phi + u * (jnp.exp(-0.5 * u * u) * INV_SQRT_2PI)).astype(BF)
-            acc[...] += dot_nn(f, wdown[cols, :])
-        hat, scale, result = norm(acc[...], vec(gain_ref, 1), vec(shift_ref, 1))
-        xh2[r] = hat.astype(BF)
-        rs[r] = jnp.where(left_lanes(), rs[r], scale)
-        yb[r] = result.astype(BF)
+
+        def feed_forward(base, size):
+            place = part_rows(m, base, size)
+            for j in range(nff):
+                cols = pl.ds(j * width, width)
+                u = dot_nn(n_s[place], wup(j)) + bup_ref[0:1, cols].astype(F32)
+                phi = 0.5 + 0.5 * lax.erf(u * INV_SQRT_2)
+                f = (u * phi).astype(BF)
+                f_t = f.T
+                for owner in range(quarter):
+                    for part in range(nff):
+                        at = (owner * nff + part) * unit
+                        lt[part, pl.ds((j * quarter + owner) * unit, unit), place] = (
+                            f_t[at:at + unit]
+                        )
+                rt[R_U + j, place] = (
+                    phi + u * (jnp.exp(-0.5 * u * u) * INV_SQRT_2PI)
+                ).astype(BF)
+                acc[base:base + size] += dot_nn(f, wdown[cols, :])
+            hat, scale, result = norm(acc[base:base + size], vec(gain_ref, 1), vec(shift_ref, 1))
+            xh2[place] = hat.astype(BF)
+            rs[place] = jnp.where(left_lanes(), rs[place], scale)
+            yb[place] = result.astype(BF)
 
         @pl.when(sec == 0)
         def _():
-            hop_copy(yb, m).start()
+            for part in range(2):
+                feed_forward(part * span, span)
+                hop_copy(m, part).start()
+
+        @pl.when(sec == 1)
+        def _():
+            feed_forward(0, rows)
 
         for copy in out_copies(0, yb, sout_hbm, m):
             copy.start()
@@ -416,29 +436,32 @@
 
     def input_grad(m):
         r = mrows(m)
-        dx = dr1[...]
         part = width // 2
         for group in range(2):
             dkv_copy(m, group).wait_recv()
             both = (dkv_own[group] + dkv_recv[m, group].astype(F32)).astype(BF)
             for which in range(2):
-                at = (1 + which) * width + group * part
-                piece = both[:, which * part:(which + 1) * part]
-                rt[R_P + 1 + which, r, group * part:(group + 1) * part] = piece
-                dx = dx + dot_nt(piece, wqkv[:, at:at + part])
+                rt[R_P + 1 + which, r, group * part:(group + 1) * part] = (
+                    both[:, which * part:(which + 1) * part]
+                )
         local_out, remote_out = out_copies(0, yb, sout_hbm, m)
         local_out.wait()
         remote_out.wait_send()
 
         @pl.when(sec == 0)
         def _():
-            hop_copy(yb, m).wait_send()
-
+            for piece_of in range(2):
+                hop_copy(m, piece_of).wait_send()
+
+        dx = dr1[...]
+        for which in range(1, 3):
+            dx = dx + dot_nt(rt[R_P + which, r], wqkv[:, which * width:(which + 1) * width])
         yb[r] = dx.astype(BF)
 
         @pl.when(sec == 1)
         def _():
-            hop_copy(yb, m).start()
+            for piece_of in range(2):
+                hop_copy(m, piece_of).start()
 
         @pl.when((m == 0) & (sec == 1))
         def _():
@@ -507,14 +530,14 @@
         def up_copy(job, k, half, target):
             i = target - 1
             return remote(
-                piece(k, half, target), land.at[job, i], z_ss.at[job, i], z_rs.at[job, i],
+                piece(k, half, target), land.at[job, i], z_ss.at[job], z_rs.at[job, i],
                 z_dev(jnp.minimum(z + 1, count - 1)),
             )
 
         def down_copy(job, k, half, target):
             i = (target + count - 1) % LANDINGS
             return remote(
-                piece(k, half, target), land.at[job, i], z_ss.at[job, target], z_rs.at[job, i],
+                piece(k, half, target), land.at[job, i], z_ss.at[job], z_rs.at[job, i],
                 z_dev(jnp.maximum(z - 1, 0)),
             )
 
@@ -641,20 +664,12 @@
             arrive(k, k, hi)
             part_copy(k).start()
 
-        def sent(job, k, half):
-            for target in range(count):
-                if target > 0:
-                    @pl.when(target > z)
-                    def _(target=target):
-                        up_copy(job, k, half, target).wait_send()
-
-                if target < count - 1:
-                    @pl.when(target < z)
-                    def _(target=target):
-                        down_copy(job, k, half, target).wait_send()
+        def sent(job):
+            others = land.at[job, pl.ds(0, count - 1)]
+            pltpu.make_async_copy(others, others, z_ss.at[job]).wait()
 
         def drain(k):
-            sent(k, k, hi)
+            sent(k)
 
             @pl.when(jnp.logical_not(is_z_first(k) | is_down(k)))
             def _():
@@ -826,7 +841,7 @@
         for i, k in enumerate((0, other_z)):
             @pl.when((sec == 1) | (i == 0))
             def _(i=i, k=k):
-                sent(CHUNKS + i, k, 1 - hi)
+                sent(CHUNKS + i)
                 turn_copy(k).wait_send()
         for k in (CHUNKS - 2, CHUNKS - 1):
             for half in range(2):
@@ -849,7 +864,8 @@
 
         @pl.when(sec == 1)
         def _():
-            hop_copy(yb, m).wait_send()
+            for part in range(2):
+                hop_copy(m, part).wait_send()
 
 
 def run_train(args, with_sums):
@@ -899,7 +915,7 @@
         pltpu.VMEM((2, rows, width), BF),
         pltpu.VMEM((MICRO, 2, rows, width), BF),
         pltpu.VMEM((total, width), BF),
-        dma((4,)), dma((MICRO,)), dma((MICRO,)), dma((MICRO,)), dma((MICRO,)), dma((MICRO,)),
+        dma((4,)), dma((MICRO,)), dma((MICRO,)), dma((MICRO,)), dma((MICRO, 2)), dma((MICRO, 2)),
         dma((MICRO, 2)), dma((MICRO, 2)), dma((MICRO, 2)), dma((MICRO, 2)),
         dma((2, MICRO)), dma((2, MICRO)), dma((2, MICRO)),
     ]
@@ -919,7 +935,7 @@
             pltpu.VMEM((12, 1, width), F32),
             pltpu.VMEM((count - 1, 12, 1, width), F32),
             dma((2, 2)), dma((4, 2)), dma((Y_SLOTS, 2)), dma((Y_SLOTS, 2)),
-            dma((CHUNKS + Z_FIRST, count - 1)), dma((CHUNKS + Z_FIRST, LANDINGS)),
+            dma((CHUNKS + Z_FIRST,)), dma((CHUNKS + Z_FIRST, LANDINGS)),
             dma((Z_FIRST,)), dma((Z_FIRST,)),
             dma((2,)), dma((2,)), dma((count - 1,)), dma((count - 1,)), dma,
             dma((MICRO,)), dma((MICRO,)), dma((MICRO,)), dma((MICRO,)),

time: 165 us -> 165 us (level)
  no operation moved by 1% of the time
where the time goes in v8:
time: 165 us; the launch traced here: 164 us
  Pallas kernels  163 us (99%)
    pallas_call x1, Pallas kernels, run_train(): pl.pallas_call(functools.partial(train_kernel, with_sums), name='train',...  159 us
    pallas_call x1, Pallas kernels, run_finish(): pl.pallas_call(finish_kernel, name='finish', out_shape=(shape((1,) + sout...  4.07 us

profile of v8, /device:TPU:0, one launch (start us, length us, event | category | flops | bytes accessed | tf_op | source)
XLA Modules:
  0.0 164.3 jit_solution(15693343453831888079)
XLA Ops:
  0.6 159.4 %train.1 = (bf16[4,128,768]{2,1,0:T(8,128)(2,1)}, bf16[4,128,768]{2,1,0:T(8,128)(2,1)}, f32[12,48,768]{2,1,0:T(8,128)}, f32[12,1,768]{2,1,0:T(1,128)}) custom-call(s32[4]{0:T(128)} %refs_0_.1, bf16[4,128,768]{2,1,0:T(8,128)(2,1)} %refs_1_.1, bf16[4,128,768]{2,1,0:T(8,128)(2,1)} %refs_2_.1, bf16[1,768,2304]{2,1,0:T(8,128)(2,1)} %refs_3_.1, ...), custom_call_target="tpu_custom_call" | custom-call | tf_op jit(solution)/shard_map/train/pallas_call | solution.py:943
  160.1 4.1 %finish.1 = (bf16[1,4,128,768]{3,2,1,0:T(8,128)(2,1)}, f32[1,4,128,768]{3,2,1,0:T(8,128)}, f32[1,48,2304]{2,1,0:T(8,128)}, f32[1,96]{1,0:T(1,128)}, f32[1,48,768...) custom-call(bf16[4,128,768]{2,1,0:T(8,128)(2,1)} %get-tuple-element., ...), custom_call_target="tpu_custom_call" | custom-call | tf_op jit(solution)/shard_map/finish/pallas_call | solution.py:1037
